TPU v7x, 128 devices: a whole 4x4x4 slice. The times are simulated.
128 devices in a mesh: strip: 4 (over y), depth: 32 (over x, z, core).
Axes of the slice: x: 4, y: 4, z: 4, core: 2. Of those that a mesh axis runs over, the one named last changes fastest.
Arguments:
- volume: bfloat16 [256, 128, 2048], P('depth', 'strip'), may hold values from -6 to 6
- occupancy: int32 [32, 4, 16], P('depth', 'strip'), may hold values from 0 to 1
- slab_order: int32 [32], replicated, may hold values from 0 to 31, as said below
- w_in: bfloat16 [4, 64], replicated, may hold values from -3 to 3
- b_in: float32 [64], replicated, may hold values from -3 to 3
- w_out: bfloat16 [64, 4], replicated, may hold values from -1.5 to 1.5
- b_out: float32 [4], replicated, may hold values from -3 to 3
- conv_weight: float32 [3, 3, 3, 3], replicated, may hold values from -1.25 to 1.25
- conv_bias: float32 [3], replicated, may hold values from -3 to 3
Outputs:
- denoised: float32 [3, 4, 1, 32, 2048], P(None, 'strip', None, 'depth')
Inputs may be any that keep to these rules, and one draw needn't show every extreme that they name: slab_order is a permutation; for every bit b, bit b of slab_order[d] is bit b of d XOR a value that depends only on d's bits above b (so slabs that agree on their bits above b hold consecutive positions).
All inputs are finite; a program needn't handle non-finite values.
Results may differ from a plain program's by a relative error of at most 0.0003.
Values may be sent and summed in bfloat16 or wider, within the bound.
No kernel may reach another device: no remote copies, remote signals or barrier semaphores. Data moves between devices by JAX's collectives and lax.ppermute only.
A program may use at most 64 MiB of HBM per device.

v0:
```python
import jax
import jax.numpy as jnp
from jax import lax
from jax.sharding import PartitionSpec as P

BRICK_ROWS = 32
BRICK_COLS = 128


def with_halo(cells, sides, width, closed):
    for axis, dim in sides:
        count = lax.axis_size(axis)
        ends = count if closed else count - 1
        head = lax.slice_in_dim(cells, 0, width, axis=dim)
        tail = lax.slice_in_dim(cells, cells.shape[dim] - width, cells.shape[dim], axis=dim)
        cells = jnp.concatenate(
            [
                lax.ppermute(tail, axis, [(i, (i + 1) % count) for i in range(ends)]),
                cells,
                lax.ppermute(head, axis, [((i + 1) % count, i) for i in range(ends)]),
            ],
            axis=dim,
        )
    return cells


def partner(block, axis, stride):
    count = lax.axis_size(axis)
    route = []
    for low in range(count):
        high = low | 1 << stride
        if high != low and high < count:
            route += [(low, high), (high, low)]
    return lax.ppermute(block, axis, route)


def expand_bricks(bricks):
    brick_rows_n, brick_cols_n = bricks.shape
    spread = jnp.broadcast_to(
        bricks.astype(jnp.float32)[:, None, :, None],
        (brick_rows_n, BRICK_ROWS, brick_cols_n, BRICK_COLS),
    )
    return spread.reshape(brick_rows_n * BRICK_ROWS, brick_cols_n * BRICK_COLS)


def march_slab(features, coverage, w_in, b_in, w_out, b_out, optical):
    rows_all = features.shape[2]
    cols_all = features.shape[3]

    def layer_step(state_pair, layer_feats):
        colour_sum, remaining = state_pair
        flattened = layer_feats.reshape(4, rows_all * cols_all)
        hidden = jax.nn.silu(
            jnp.dot(w_in.T, flattened, preferred_element_type=jnp.float32) + b_in[:, None]
        ).astype(jnp.bfloat16)
        output = jnp.dot(w_out.T, hidden, preferred_element_type=jnp.float32) + b_out[:, None]
        output = output.reshape(4, rows_all, cols_all)
        colour = jax.nn.sigmoid(output[:3])
        density = jax.nn.softplus(output[3]) * coverage
        alpha_val = 1.0 - jnp.exp(-optical * density)
        colour_sum = colour_sum + (remaining * alpha_val)[None] * colour
        remaining = remaining * (1.0 - alpha_val)
        return ((colour_sum, remaining), None)

    start = (
        jnp.zeros((3, rows_all, cols_all), jnp.float32),
        jnp.ones((rows_all, cols_all), jnp.float32),
    )
    (colour_sum, remaining), unused = lax.scan(layer_step, start, features)
    return (colour_sum, remaining)


def over_pair(front_part, back_part):
    colour = front_part[:3] + front_part[3:4] * back_part[:3]
    remaining = front_part[3:4] * back_part[3:4]
    return jnp.concatenate([colour, remaining], 0)


def shards(volume, occupancy, slab_order, w_in, b_in, w_out, b_out, conv_weight, conv_bias):
    depth_count = lax.axis_size("depth")
    depth_index = lax.axis_index("depth")
    strip_count = lax.axis_size("strip")
    strip_index = lax.axis_index("strip")
    layers, rows_here, columns = volume.shape
    optical = 2.0 / (layers * depth_count)
    rimmed = with_halo(volume, (("strip", 1),), 1, False).astype(jnp.float32)
    scalar_field = rimmed[:, 1:-1]
    grad_rows = 0.5 * (rimmed[:, 2:] - rimmed[:, :-2])
    padded_cols = jnp.pad(scalar_field, ((0, 0), (0, 0), (1, 1)))
    grad_cols = 0.5 * (padded_cols[:, :, 2:] - padded_cols[:, :, :-2])
    padded_depth = jnp.concatenate([scalar_field[:1], scalar_field, scalar_field[-1:]], 0)
    grad_depth = 0.5 * (padded_depth[2:] - padded_depth[:-2])
    features = jnp.stack([scalar_field, grad_cols, grad_rows, grad_depth], 1).astype(jnp.bfloat16)
    coverage = expand_bricks(occupancy[0])
    colour_sum, remaining = march_slab(features, coverage, w_in, b_in, w_out, b_out, optical)
    partial_value = jnp.concatenate([colour_sum, remaining[None]], 0)
    own_order = slab_order[depth_index]
    rounds = depth_count.bit_length() - 1
    row_share = rows_here // depth_count
    composed = partial_value
    for bit_index in range(rounds):
        pieces = composed.shape[1]
        paired = composed.reshape(4, pieces // 2, 2, columns)
        mine_bit = jnp.bitwise_and(jnp.right_shift(depth_index, bit_index), 1)
        keep_part = jnp.where(mine_bit == 0, paired[:, :, 0], paired[:, :, 1])
        give_part = jnp.where(mine_bit == 0, paired[:, :, 1], paired[:, :, 0])
        received = partner(give_part, "depth", bit_index)
        in_front = jnp.bitwise_and(jnp.right_shift(own_order, bit_index), 1) == 0
        front_part = jnp.where(in_front, keep_part, received)
        back_part = jnp.where(in_front, received, keep_part)
        composed = over_pair(front_part, back_part)
    picture = composed[:3][:, :, None, :]
    extended = with_halo(picture, (("strip", 1), ("depth", 2)), 1, True)
    edge_weight = jnp.concatenate(
        [
            (strip_index > 0).astype(jnp.float32)[None],
            jnp.ones((row_share,), jnp.float32),
            (strip_index < strip_count - 1).astype(jnp.float32)[None],
        ],
        0,
    )
    extended = extended * edge_weight[None, :, None, None]
    row_centre = extended[:, 1 : row_share + 1, 1]
    row_above = jnp.where(
        depth_index == 0, extended[:, 0:row_share, 0], extended[:, 1 : row_share + 1, 0]
    )
    row_below = jnp.where(
        depth_index == depth_count - 1,
        extended[:, 2 : row_share + 2, 2],
        extended[:, 1 : row_share + 1, 2],
    )
    row_sets = [row_above, row_centre, row_below]
    filtered = jnp.broadcast_to(conv_bias[:, None, None], (3, row_share, columns))
    for row_off in range(3):
        padded = jnp.pad(row_sets[row_off], ((0, 0), (0, 0), (1, 1)))
        for col_off in range(3):
            window = padded[:, :, col_off : col_off + columns]
            filtered = filtered + jnp.sum(
                conv_weight[:, :, row_off, col_off][:, :, None, None] * window[None], axis=1
            )
    return filtered.reshape(3, 1, row_share, 1, columns)


def solution(mesh):
    placed = (
        P("depth", "strip", None),
        P("depth", "strip", None),
        P(),
        P(),
        P(),
        P(),
        P(),
        P(),
        P(),
    )
    return jax.shard_map(
        shards,
        mesh=mesh,
        in_specs=placed,
        out_specs=P(None, "strip", None, "depth", None),
        check_vma=False,
    )
```

profile of v0, /device:TPU:16, one launch (start us, length us, event | category | flops | bytes accessed | tf_op | source)
XLA Modules:
  0.0 156.3 jit_solution(9777938371478616563)
XLA Ops:
  0.0 1.1 fusion.39
  1.1 3.2 %collective-permute-start = (bf16[8,1,2048]{2,1,0:T(2,128)(2,1)S(1)}, bf16[8,1,2048]{2,1,0:T(2,128)(2,1)S(1)}, u32[]{:S(2)}, u32[]{:S(2)}) collective-permute-start(bf16[8,1,2048]{2,1,0:T(2,128)(2,1)S(1)} %get-tuple-element.129), channel_id=1, source_target_pairs={{0,32},{32,64},{64,96},{1,33},{33,65},{65,97},{2,34},{34,66},{66,9... | collective-permute-start | bytes 98312 | tf_op jit(solution)/shard_map/ppermute | solution.py:18
  4.3 2.7 %collective-permute-start.1 = (bf16[8,1,2048]{2,1,0:T(2,128)(2,1)S(1)}, bf16[8,1,2048]{2,1,0:T(2,128)(2,1)S(1)}, u32[]{:S(2)}, u32[]{:S(2)}) collective-permute-start(bf16[8,1,2048]{2,1,0:T(2,128)(2,1)S(1)} %get-tuple-element.130), channel_id=1, source_target_pairs={{32,0},{64,32},{96,64},{33,1},{65,33},{97,65},{34,2},{66,34},{98,6... | collective-permute-start | bytes 98312 | tf_op jit(solution)/shard_map/ppermute | solution.py:20
  7.7 2.8 %collective-permute-done.1 = bf16[8,1,2048]{2,1,0:T(2,128)(2,1)S(1)} collective-permute-done((bf16[8,1,2048]{2,1,0:T(2,128)(2,1)S(1)}, bf16[8,1,2048]{2,1,0:T(2,128)(2,1)S(1)}, u32[]{:S(2)}, u32[]{:S(2)}) %collective-permute-start.1) | collective-permute-done | bytes 32800 | tf_op jit(solution)/shard_map/ppermute | solution.py:20
  10.5 1.7 %maximum_convert_fusion = f32[8,34,2048]{2,1,0:T(8,128)S(1)} fusion(bf16[8,1,2048]{2,1,0:T(2,128)(2,1)S(1)} %collective-permute-done.1, bf16[8,32,2048]{2,1,0:T(8,128)(2,1)} %param.11, bf16[8,1,2048]{2,1,0:T(2,128)(2,1)S(1)} %collective-permute-done), kind=kLoop, calls=%fused_computation.36 | loop fusion | flops 3342336 | bytes 3342336 | tf_op jit(solution)/shard_map/convert_element_type | solution.py:86
  13.9 1.4 fusion.23
  15.3 2.4 %pad_maximum_fusion = bf16[8,4,32,2048]{3,2,1,0:T(8,128)(2,1)} fusion(bf16[8,1,32,2048]{3,2,1,0:T(8,128)(2,1)S(1)} %get-tuple-element.126, bf16[8,1,32,2048]{3,2,1,0:T(8,128)(2,1)S(1)} %get-tuple-element.121, bf16[8,1,32,2048]{3,2,1,0:T(8,128)(2,1)S(1)} %get-tuple-element.125, bf16[8,1,32,2048]{3,2,1,0:T(8,128)(2,1)S(1)} %convert_bitcast_fusion), kind=kLoop, calls=%fused_computation.22 | loop fusion | flops 6291456 | bytes 8388608 | tf_op jit(solution)/shard_map/stack | solution.py:93
  17.7 91.5 %while.13 = (s32[]{:T(128)}, f32[3,32,2048]{2,1,0:T(8,128)S(1)}, f32[32,2048]{1,0:T(8,128)S(1)}, bf16[8,4,32,2048]{3,2,1,0:T(8,128)(2,1)}, bf16[4,64]{1,0:T(4,12...) while((s32[]{:T(128)}, f32[3,32,2048]{2,1,0:T(8,128)S(1)}, ...), condition=%wide.region_1.2_spmd.clone, body=%wide.region_0.1_spmd.clone.sunk | while | flops 94568448 | bytes 9971084 | solution.py:69
  17.7 1.1 dynamic-slice_bitcast_fusion.2
  19.2 7.6 %fusion.56 = f32[4,65536]{1,0:T(4,128)S(1)} fusion(bf16[64,4]{0,1:T(4,128)(2,1)S(1)} %get-tuple-element.250, bf16[4,65536]{1,0:T(4,128)(2,1)S(1)} %bitcast.230, bf16[4,64]{1,0:T(4,128)(2,1)S(1)} %get-tuple-element.248, f32[64]{0:T(128)S(1)} %get-tuple-element.249, f32[4]{0:T(128)S(1)} %get-tuple-element.251), kind=kOutput, calls=%fused_computation.4.clone.1 | convolution fusion | flops 92536832 | bytes 1574160 | tf_op jit(solution)/shard_map/while/body/eval_jaxpr/dot_general | solution.py:56
  29.2 1.1 dynamic-slice_bitcast_fusion.2
  30.7 7.6 %fusion.56 = f32[4,65536]{1,0:T(4,128)S(1)} fusion(bf16[64,4]{0,1:T(4,128)(2,1)S(1)} %get-tuple-element.250, bf16[4,65536]{1,0:T(4,128)(2,1)S(1)} %bitcast.230, bf16[4,64]{1,0:T(4,128)(2,1)S(1)} %get-tuple-element.248, f32[64]{0:T(128)S(1)} %get-tuple-element.249, f32[4]{0:T(128)S(1)} %get-tuple-element.251), kind=kOutput, calls=%fused_computation.4.clone.1 | convolution fusion | flops 92536832 | bytes 1574160 | tf_op jit(solution)/shard_map/while/body/eval_jaxpr/dot_general | solution.py:56
  40.6 1.1 dynamic-slice_bitcast_fusion.2
  42.1 7.6 %fusion.56 = f32[4,65536]{1,0:T(4,128)S(1)} fusion(bf16[64,4]{0,1:T(4,128)(2,1)S(1)} %get-tuple-element.250, bf16[4,65536]{1,0:T(4,128)(2,1)S(1)} %bitcast.230, bf16[4,64]{1,0:T(4,128)(2,1)S(1)} %get-tuple-element.248, f32[64]{0:T(128)S(1)} %get-tuple-element.249, f32[4]{0:T(128)S(1)} %get-tuple-element.251), kind=kOutput, calls=%fused_computation.4.clone.1 | convolution fusion | flops 92536832 | bytes 1574160 | tf_op jit(solution)/shard_map/while/body/eval_jaxpr/dot_general | solution.py:56
  52.0 1.1 dynamic-slice_bitcast_fusion.2
  53.5 7.6 %fusion.56 = f32[4,65536]{1,0:T(4,128)S(1)} fusion(bf16[64,4]{0,1:T(4,128)(2,1)S(1)} %get-tuple-element.250, bf16[4,65536]{1,0:T(4,128)(2,1)S(1)} %bitcast.230, bf16[4,64]{1,0:T(4,128)(2,1)S(1)} %get-tuple-element.248, f32[64]{0:T(128)S(1)} %get-tuple-element.249, f32[4]{0:T(128)S(1)} %get-tuple-element.251), kind=kOutput, calls=%fused_computation.4.clone.1 | convolution fusion | flops 92536832 | bytes 1574160 | tf_op jit(solution)/shard_map/while/body/eval_jaxpr/dot_general | solution.py:56
  65.0 7.6 %fusion.56 = f32[4,65536]{1,0:T(4,128)S(1)} fusion(bf16[64,4]{0,1:T(4,128)(2,1)S(1)} %get-tuple-element.250, bf16[4,65536]{1,0:T(4,128)(2,1)S(1)} %bitcast.230, bf16[4,64]{1,0:T(4,128)(2,1)S(1)} %get-tuple-element.248, f32[64]{0:T(128)S(1)} %get-tuple-element.249, f32[4]{0:T(128)S(1)} %get-tuple-element.251), kind=kOutput, calls=%fused_computation.4.clone.1 | convolution fusion | flops 92536832 | bytes 1574160 | tf_op jit(solution)/shard_map/while/body/eval_jaxpr/dot_general | solution.py:56
  76.4 7.6 %fusion.56 = f32[4,65536]{1,0:T(4,128)S(1)} fusion(bf16[64,4]{0,1:T(4,128)(2,1)S(1)} %get-tuple-element.250, bf16[4,65536]{1,0:T(4,128)(2,1)S(1)} %bitcast.230, bf16[4,64]{1,0:T(4,128)(2,1)S(1)} %get-tuple-element.248, f32[64]{0:T(128)S(1)} %get-tuple-element.249, f32[4]{0:T(128)S(1)} %get-tuple-element.251), kind=kOutput, calls=%fused_computation.4.clone.1 | convolution fusion | flops 92536832 | bytes 1574160 | tf_op jit(solution)/shard_map/while/body/eval_jaxpr/dot_general | solution.py:56
  87.8 7.6 %fusion.56 = f32[4,65536]{1,0:T(4,128)S(1)} fusion(bf16[64,4]{0,1:T(4,128)(2,1)S(1)} %get-tuple-element.250, bf16[4,65536]{1,0:T(4,128)(2,1)S(1)} %bitcast.230, bf16[4,64]{1,0:T(4,128)(2,1)S(1)} %get-tuple-element.248, f32[64]{0:T(128)S(1)} %get-tuple-element.249, f32[4]{0:T(128)S(1)} %get-tuple-element.251), kind=kOutput, calls=%fused_computation.4.clone.1 | convolution fusion | flops 92536832 | bytes 1574160 | tf_op jit(solution)/shard_map/while/body/eval_jaxpr/dot_general | solution.py:56
  99.3 7.6 %fusion.56 = f32[4,65536]{1,0:T(4,128)S(1)} fusion(bf16[64,4]{0,1:T(4,128)(2,1)S(1)} %get-tuple-element.250, bf16[4,65536]{1,0:T(4,128)(2,1)S(1)} %bitcast.230, bf16[4,64]{1,0:T(4,128)(2,1)S(1)} %get-tuple-element.248, f32[64]{0:T(128)S(1)} %get-tuple-element.249, f32[4]{0:T(128)S(1)} %get-tuple-element.251), kind=kOutput, calls=%fused_computation.4.clone.1 | convolution fusion | flops 92536832 | bytes 1574160 | tf_op jit(solution)/shard_map/while/body/eval_jaxpr/dot_general | solution.py:56
  114.6 2.0 %collective-permute-start.3 = (f32[4,8,2048]{2,0,1:T(4,128)S(1)}, f32[4,8,2048]{2,0,1:T(4,128)S(1)}, u32[]{:S(2)}, u32[]{:S(2)}) collective-permute-start(f32[4,8,2048]{2,0,1:T(4,128)S(1)} %select_bitcast_fusion.1), channel_id=1, source_target_pairs={{0,2},{2,0},{1,3},{3,1},{4,6},{6,4},{5,7},{7,5},{8,10},{10,8},{9,1... | collective-permute-start | bytes 786440 | tf_op jit(solution)/shard_map/ppermute | solution.py:34
  117.3 5.9 %collective-permute-done.3 = f32[4,8,2048]{2,0,1:T(4,128)S(1)} collective-permute-done((f32[4,8,2048]{2,0,1:T(4,128)S(1)}, f32[4,8,2048]{2,0,1:T(4,128)S(1)}, u32[]{:S(2)}, u32[]{:S(2)}) %collective-permute-start.3) | collective-permute-done | bytes 262176 | tf_op jit(solution)/shard_map/ppermute | solution.py:34
  123.9 3.8 %collective-permute-start.4 = (f32[4,4,2048]{2,0,1:T(4,128)S(1)}, f32[4,4,2048]{2,0,1:T(4,128)S(1)}, u32[]{:S(2)}, u32[]{:S(2)}) collective-permute-start(f32[4,4,2048]{2,0,1:T(4,128)S(1)} %select_bitcast_fusion.2), channel_id=1, source_target_pairs={{0,4},{4,0},{1,5},{5,1},{2,6},{6,2},{3,7},{7,3},{8,12},{12,8},{9,1... | collective-permute-start | bytes 393224 | tf_op jit(solution)/shard_map/ppermute | solution.py:34
  128.3 2.3 %collective-permute-done.4 = f32[4,4,2048]{2,0,1:T(4,128)S(1)} collective-permute-done((f32[4,4,2048]{2,0,1:T(4,128)S(1)}, f32[4,4,2048]{2,0,1:T(4,128)S(1)}, u32[]{:S(2)}, u32[]{:S(2)}) %collective-permute-start.4) | collective-permute-done | bytes 131104 | tf_op jit(solution)/shard_map/ppermute | solution.py:34
  130.9 1.6 %collective-permute-start.5 = (f32[4,2,2048]{2,0,1:T(4,128)S(1)}, f32[4,2,2048]{2,0,1:T(4,128)S(1)}, u32[]{:S(2)}, u32[]{:S(2)}) collective-permute-start(f32[4,2,2048]{2,0,1:T(4,128)S(1)} %select_bitcast_fusion.3), channel_id=1, source_target_pairs={{0,8},{8,0},{1,9},{9,1},{2,10},{10,2},{3,11},{11,3},{4,12},{12,4},... | collective-permute-start | bytes 196616 | tf_op jit(solution)/shard_map/ppermute | solution.py:34
  133.2 2.1 %collective-permute-done.5 = f32[4,2,2048]{2,0,1:T(4,128)S(1)} collective-permute-done((f32[4,2,2048]{2,0,1:T(4,128)S(1)}, f32[4,2,2048]{2,0,1:T(4,128)S(1)}, u32[]{:S(2)}, u32[]{:S(2)}) %collective-permute-start.5) | collective-permute-done | bytes 65568 | tf_op jit(solution)/shard_map/ppermute | solution.py:34
  135.5 3.1 %collective-permute-start.6 = (f32[4,1,2048]{2,0,1:T(4,128)S(1)}, f32[4,1,2048]{2,0,1:T(4,128)S(1)}, u32[]{:S(2)}, u32[]{:S(2)}) collective-permute-start(f32[4,1,2048]{2,0,1:T(4,128)S(1)} %select_bitcast_fusion.4), channel_id=1, source_target_pairs={{0,16},{16,0},{1,17},{17,1},{2,18},{18,2},{3,19},{19,3},{4,20},{20... | collective-permute-start | bytes 98312 | tf_op jit(solution)/shard_map/ppermute | solution.py:34
  139.2 1.7 %collective-permute-done.6 = f32[4,1,2048]{2,0,1:T(4,128)S(1)} collective-permute-done((f32[4,1,2048]{2,0,1:T(4,128)S(1)}, f32[4,1,2048]{2,0,1:T(4,128)S(1)}, u32[]{:S(2)}, u32[]{:S(2)}) %collective-permute-start.6) | collective-permute-done | bytes 32800 | tf_op jit(solution)/shard_map/ppermute | solution.py:34
  141.1 2.0 %collective-permute-start.8 = (f32[3,1,1,2048]{3,0,2,1:T(4,128)S(1)}, f32[3,1,1,2048]{3,0,2,1:T(4,128)S(1)}, u32[]{:S(2)}, u32[]{:S(2)}) collective-permute-start(f32[3,1,1,2048]{3,0,2,1:T(4,128)S(1)} %fusion.34), channel_id=1, source_target_pairs={{32,0},{64,32},{96,64},{0,96},{33,1},{65,33},{97,65},{1,97},{34,2}... | collective-permute-start | bytes 73736 | tf_op jit(solution)/shard_map/ppermute | solution.py:20
  143.4 1.6 %collective-permute-done.7 = f32[3,1,1,2048]{3,0,2,1:T(4,128)S(1)} collective-permute-done((f32[3,1,1,2048]{3,0,2,1:T(4,128)S(1)}, f32[3,1,1,2048]{3,0,2,1:T(4,128)S(1)}, u32[]{:S(2)}, u32[]{:S(2)}) %collective-permute-start.7) | collective-permute-done | bytes 24608 | tf_op jit(solution)/shard_map/ppermute | solution.py:18
  145.8 1.8 %collective-permute-done.10 = f32[3,3,1,2048]{3,0,2,1:T(4,128)S(1)} collective-permute-done((f32[3,3,1,2048]{3,0,2,1:T(4,128)S(1)}, f32[3,3,1,2048]{3,0,2,1:T(4,128)S(1)}, u32[]{:S(2)}, u32[]{:S(2)}) %collective-permute-start.10) | collective-permute-done | bytes 73760 | tf_op jit(solution)/shard_map/ppermute | solution.py:20
  147.6 6.1 %collective-permute-done.9 = f32[3,3,1,2048]{3,0,2,1:T(4,128)S(1)} collective-permute-done((f32[3,3,1,2048]{3,0,2,1:T(4,128)S(1)}, f32[3,3,1,2048]{3,0,2,1:T(4,128)S(1)}, u32[]{:S(2)}, u32[]{:S(2)}) %collective-permute-start.9) | collective-permute-done | bytes 73760 | tf_op jit(solution)/shard_map/ppermute | solution.py:18
  (131 shorter events, 37.5 us)
Async XLA Ops:
  1.1 6.6 %collective-permute-start = (bf16[8,1,2048]{2,1,0:T(2,128)(2,1)S(1)}, bf16[8,1,2048]{2,1,0:T(2,128)(2,1)S(1)}, u32[]{:S(2)}, u32[]{:S(2)}) collective-permute-start(bf16[8,1,2048]{2,1,0:T(2,128)(2,1)S(1)} %get-tuple-element.129), channel_id=1, source_target_pairs={{0,32},{32,64},{64,96},{1,33},{33,65},{65,97},{2,34},{34,66},{66,9... | collective-permute-start | bytes 98312 | tf_op jit(solution)/shard_map/ppermute | solution.py:18
  4.3 6.2 %collective-permute-start.1 = (bf16[8,1,2048]{2,1,0:T(2,128)(2,1)S(1)}, bf16[8,1,2048]{2,1,0:T(2,128)(2,1)S(1)}, u32[]{:S(2)}, u32[]{:S(2)}) collective-permute-start(bf16[8,1,2048]{2,1,0:T(2,128)(2,1)S(1)} %get-tuple-element.130), channel_id=1, source_target_pairs={{32,0},{64,32},{96,64},{33,1},{65,33},{97,65},{34,2},{66,34},{98,6... | collective-permute-start | bytes 98312 | tf_op jit(solution)/shard_map/ppermute | solution.py:20
  12.6 1.2 copy-start
  15.3 2.4 %copy-start.3 = (bf16[4,64]{1,0:T(4,128)(2,1)S(1)}, bf16[4,64]{1,0:T(4,128)(2,1)}, u32[]{:S(2)}) copy-start(bf16[4,64]{1,0:T(4,128)(2,1)} %param.14) | copy-start | bytes 1540
  15.3 2.4 %copy-start.4 = (bf16[64,4]{0,1:T(4,128)(2,1)S(1)}, bf16[64,4]{0,1:T(4,128)(2,1)}, u32[]{:S(2)}) copy-start(bf16[64,4]{0,1:T(4,128)(2,1)} %param.16) | copy-start | bytes 1540
  15.3 2.4 %copy-start.5 = (f32[64]{0:T(128)S(1)}, f32[64]{0:T(128)}, u32[]{:S(2)}) copy-start(f32[64]{0:T(128)} %param.15) | copy-start | bytes 772
  15.3 2.4 %copy-start.6 = (f32[4]{0:T(128)S(1)}, f32[4]{0:T(128)}, u32[]{:S(2)}) copy-start(f32[4]{0:T(128)} %param.17) | copy-start | bytes 52
  109.7 1.8 %copy-start.7 = (s32[32]{0:T(128)S(1)}, s32[32]{0:T(128)}, u32[]{:S(2)}) copy-start(s32[32]{0:T(128)} %param.13) | copy-start | bytes 388
  111.2 2.2 %collective-permute-start.2 = (f32[4,16,2048]{2,0,1:T(4,128)S(1)}, f32[4,16,2048]{2,0,1:T(4,128)S(1)}, u32[]{:S(2)}, u32[]{:S(2)}) collective-permute-start(f32[4,16,2048]{2,0,1:T(4,128)S(1)} %get-tuple-element.117), channel_id=1, source_target_pairs={{0,1},{1,0},{2,3},{3,2},{4,5},{5,4},{6,7},{7,6},{8,9},{9,8},{10,11... | collective-permute-start | bytes 1572872 | tf_op jit(solution)/shard_map/ppermute | solution.py:34
  114.6 8.6 %collective-permute-start.3 = (f32[4,8,2048]{2,0,1:T(4,128)S(1)}, f32[4,8,2048]{2,0,1:T(4,128)S(1)}, u32[]{:S(2)}, u32[]{:S(2)}) collective-permute-start(f32[4,8,2048]{2,0,1:T(4,128)S(1)} %select_bitcast_fusion.1), channel_id=1, source_target_pairs={{0,2},{2,0},{1,3},{3,1},{4,6},{6,4},{5,7},{7,5},{8,10},{10,8},{9,1... | collective-permute-start | bytes 786440 | tf_op jit(solution)/shard_map/ppermute | solution.py:34
  123.4 19.7 %copy-start.1 = (f32[3,3,3,3]{3,2,1,0:T(4,128)S(1)}, f32[3,3,3,3]{3,2,1,0:T(4,128)}, u32[]{:S(2)}) copy-start(f32[3,3,3,3]{3,2,1,0:T(4,128)} %param.18) | copy-start | bytes 976
  123.9 31.7 %copy-start.2 = (f32[3]{0:T(128)S(1)}, f32[3]{0:T(128)}, u32[]{:S(2)}) copy-start(f32[3]{0:T(128)} %param.19) | copy-start | bytes 40
  123.9 6.7 %collective-permute-start.4 = (f32[4,4,2048]{2,0,1:T(4,128)S(1)}, f32[4,4,2048]{2,0,1:T(4,128)S(1)}, u32[]{:S(2)}, u32[]{:S(2)}) collective-permute-start(f32[4,4,2048]{2,0,1:T(4,128)S(1)} %select_bitcast_fusion.2), channel_id=1, source_target_pairs={{0,4},{4,0},{1,5},{5,1},{2,6},{6,2},{3,7},{7,3},{8,12},{12,8},{9,1... | collective-permute-start | bytes 393224 | tf_op jit(solution)/shard_map/ppermute | solution.py:34
  130.9 4.3 %collective-permute-start.5 = (f32[4,2,2048]{2,0,1:T(4,128)S(1)}, f32[4,2,2048]{2,0,1:T(4,128)S(1)}, u32[]{:S(2)}, u32[]{:S(2)}) collective-permute-start(f32[4,2,2048]{2,0,1:T(4,128)S(1)} %select_bitcast_fusion.3), channel_id=1, source_target_pairs={{0,8},{8,0},{1,9},{9,1},{2,10},{10,2},{3,11},{11,3},{4,12},{12,4},... | collective-permute-start | bytes 196616 | tf_op jit(solution)/shard_map/ppermute | solution.py:34
  135.5 5.5 %collective-permute-start.6 = (f32[4,1,2048]{2,0,1:T(4,128)S(1)}, f32[4,1,2048]{2,0,1:T(4,128)S(1)}, u32[]{:S(2)}, u32[]{:S(2)}) collective-permute-start(f32[4,1,2048]{2,0,1:T(4,128)S(1)} %select_bitcast_fusion.4), channel_id=1, source_target_pairs={{0,16},{16,0},{1,17},{17,1},{2,18},{18,2},{3,19},{19,3},{4,20},{20... | collective-permute-start | bytes 98312 | tf_op jit(solution)/shard_map/ppermute | solution.py:34
  141.0 4.0 %collective-permute-start.7 = (f32[3,1,1,2048]{3,0,2,1:T(4,128)S(1)}, f32[3,1,1,2048]{3,0,2,1:T(4,128)S(1)}, u32[]{:S(2)}, u32[]{:S(2)}) collective-permute-start(f32[3,1,1,2048]{3,0,2,1:T(4,128)S(1)} %fusion.34), channel_id=1, source_target_pairs={{0,32},{32,64},{64,96},{96,0},{1,33},{33,65},{65,97},{97,1},{2,34}... | collective-permute-start | bytes 73736 | tf_op jit(solution)/shard_map/ppermute | solution.py:18
  141.1 4.0 %collective-permute-start.8 = (f32[3,1,1,2048]{3,0,2,1:T(4,128)S(1)}, f32[3,1,1,2048]{3,0,2,1:T(4,128)S(1)}, u32[]{:S(2)}, u32[]{:S(2)}) collective-permute-start(f32[3,1,1,2048]{3,0,2,1:T(4,128)S(1)} %fusion.34), channel_id=1, source_target_pairs={{32,0},{64,32},{96,64},{0,96},{33,1},{65,33},{97,65},{1,97},{34,2}... | collective-permute-start | bytes 73736 | tf_op jit(solution)/shard_map/ppermute | solution.py:20
  145.1 2.5 %collective-permute-start.10 = (f32[3,3,1,2048]{3,0,2,1:T(4,128)S(1)}, f32[3,3,1,2048]{3,0,2,1:T(4,128)S(1)}, u32[]{:S(2)}, u32[]{:S(2)}) collective-permute-start(f32[3,3,1,2048]{3,0,2,1:T(4,128)S(1)} %pad_maximum_fusion.7), channel_id=1, source_target_pairs={{1,0},{2,1},{3,2},{4,3},{5,4},{6,5},{7,6},{8,7},{9,8},{10,9},{11,1... | collective-permute-start | bytes 221192 | tf_op jit(solution)/shard_map/ppermute | solution.py:20
  145.4 8.3 %collective-permute-start.9 = (f32[3,3,1,2048]{3,0,2,1:T(4,128)S(1)}, f32[3,3,1,2048]{3,0,2,1:T(4,128)S(1)}, u32[]{:S(2)}, u32[]{:S(2)}) collective-permute-start(f32[3,3,1,2048]{3,0,2,1:T(4,128)S(1)} %pad_maximum_fusion.7), channel_id=1, source_target_pairs={{0,1},{1,2},{2,3},{3,4},{4,5},{5,6},{6,7},{7,8},{8,9},{9,10},{10,1... | collective-permute-start | bytes 221192 | tf_op jit(solution)/shard_map/ppermute | solution.py:18
where the time goes:
time: 159 us; the launch traced here: 156 us
  matrix products  61.1 us (38%)
  waiting for transfers between devices  25.1 us (16%)
  local copies, waits for them, and re-layouts  24 us (15%)
  other arithmetic  22.6 us (14%)
  starting transfers between devices  19.3 us (12%)
  between operations  3.77 us (2%)
    dot_general x8, matrix products, layer_step(): jnp.dot(w_out.T, hidden, preferred_element_type=jnp.float32)  61.1 us
    ppermute x5, waiting for transfers between devices, partner(): return lax.ppermute(block, axis, route)  12.7 us
    while x16, local copies, waits for them, and re-layouts  11.9 us
    ppermute x5, starting transfers between devices, partner(): return lax.ppermute(block, axis, route)  10.8 us
    ppermute x3, waiting for transfers between devices, with_halo(): lax.ppermute(tail, axis, [(i, (i + 1) % count) for i in range(ends)])  7.71 us
    slice x8, local copies, waits for them, and re-layouts, layer_step(): density = jax.nn.softplus(output[3]) * coverage  6.04 us
    add x8, other arithmetic, layer_step(): colour_sum = colour_sum + (remaining * alpha_val)[None] * colour  5.35 us
    ppermute x3, starting transfers between devices, with_halo(): lax.ppermute(head, axis, [((i + 1) % count, i) for i in range(ends)])  4.91 us
  transfers between devices with their start and end apart: 11, of which 10 were waited for; matrix products, arithmetic and copies ran while one was open for 1% of the time, Pallas kernels for 0%

commit v1 on v0

v1 whole, which is shorter than its diff:
```python
import functools

import jax
import jax.numpy as jnp
from jax import lax
from jax.experimental import pallas as pl
from jax.experimental.pallas import tpu as pltpu
from jax.sharding import PartitionSpec as P

HIDDEN = 64
KDIM = 48
F32 = jnp.float32
BF16 = jnp.bfloat16


def iota(shape, dim):
    return lax.broadcasted_iota(jnp.int32, shape, dim)


def prepare_weights(w_in, b_in, w_out, w1, w2):
    bias = 0.5 * b_in[...]
    hi = bias.astype(BF16).astype(F32)
    mid = (bias - hi).astype(BF16).astype(F32)
    low = bias - hi - mid
    table = jnp.concatenate(
        [0.5 * w_in[...].astype(F32), hi, mid, low, jnp.zeros((1, HIDDEN), F32)], 0
    ).astype(BF16)
    spread = (iota((HIDDEN * 8, HIDDEN), 0) // 8 == iota((HIDDEN * 8, HIDDEN), 1)).astype(BF16)
    nt = (((1,), (1,)), ((), ()))
    by_row = lax.dot_general(spread, table, nt, preferred_element_type=F32).astype(BF16)
    slot = iota((8, KDIM), 0)
    col = iota((8, KDIM), 1)
    place = jnp.where(col < 32, col // 8, col - 28) == slot
    wide = jnp.dot(by_row, place.astype(BF16), preferred_element_type=F32)
    r = iota((HIDDEN * 8, KDIM), 0)
    k = iota((HIDDEN * 8, KDIM), 1)
    w1[...] = jnp.where((k >= 32) | (r % 8 == k % 8), wide, 0.0).astype(BF16)
    pick = (iota((32, 4), 0) // 8 == iota((32, 4), 1)).astype(BF16)
    out_rows = lax.dot_general(
        pick, w_out[...], (((1,), (1,)), ((), ())), preferred_element_type=F32
    ).astype(BF16)
    full = lax.dot_general(out_rows, spread, nt, preferred_element_type=F32)
    o = iota((32, HIDDEN * 8), 0)
    q = iota((32, HIDDEN * 8), 1)
    scale = jnp.where(o < 24, 0.5, 1.0)
    w2[...] = jnp.where(o % 8 == q % 8, full * scale, 0.0).astype(BF16)


def feature_kernel(vol, top, bot, w_in, b_in, w_out, feats, w1, w2, lines, planes):
    layers, rows, columns = vol.shape
    half = columns // 2
    prepare_weights(w_in, b_in, w_out, w1, w2)

    blocks = half // 128

    def permute(z, carry):
        field = vol[z].astype(F32)
        for k in range(2 * blocks):
            lines[k * rows : (k + 1) * rows] = field[:, k * 128 : (k + 1) * 128]
        for j in range(8):
            for k in range(blocks):
                left = lines[pl.ds(k * rows + j, 4, stride=8)]
                right = lines[pl.ds((k + blocks) * rows + j, 4, stride=8)]
                planes[z, j, :, k * 128 : (k + 1) * 128] = jnp.concatenate([left, right], 0)
        return carry

    lax.fori_loop(0, layers, permute, 0)
    lane = iota((8, half), 1)
    sub = iota((8, half), 0)
    ones = jnp.ones((KDIM - 32, half), BF16)

    def gradients(z, carry):
        before = jnp.maximum(z - 1, 0)
        after = jnp.minimum(z + 1, layers - 1)
        first = jnp.broadcast_to(top[z].astype(F32), (8, columns))
        last = jnp.broadcast_to(bot[z].astype(F32), (8, columns))
        for j in range(8):
            s = planes[z, j]
            ahead = pltpu.roll(s, half - 1, 1)
            behind = pltpu.roll(s, 1, 1)
            ahead = jnp.where(
                lane == half - 1, jnp.where(sub < 4, pltpu.roll(ahead, 4, 0), 0.0), ahead
            )
            behind = jnp.where(lane == 0, jnp.where(sub >= 4, pltpu.roll(behind, 4, 0), 0.0), behind)
            if j > 0:
                above = planes[z, j - 1]
            else:
                above = pltpu.roll(planes[z, 7], 1, 0)
                above = jnp.where(sub == 0, first[:, :half], above)
                above = jnp.where(sub == 4, first[:, half:], above)
            if j < 7:
                below = planes[z, j + 1]
            else:
                below = pltpu.roll(planes[z, 0], 7, 0)
                below = jnp.where(sub == 3, last[:, :half], below)
                below = jnp.where(sub == 7, last[:, half:], below)
            deep = planes[after, j] - planes[before, j]
            block = jnp.concatenate(
                [s, 0.5 * (ahead - behind), 0.5 * (below - above), 0.5 * deep], 0
            )
            feats[j % 2, j // 2, z, 0:32] = block.astype(BF16)
            feats[j % 2, j // 2, z, 32:KDIM] = ones
        return carry

    lax.fori_loop(0, layers, gradients, 0)


def march(feats, w1, w2, b_out, coverage, parity, zpos):
    layers = feats.shape[2]
    half = feats.shape[4]

    def layer(z, state):
        x = feats[parity, zpos, z]
        u = jnp.dot(w1[...], x, preferred_element_type=F32)
        hidden = (u * jnp.tanh(u) + u).astype(BF16)
        e = jnp.dot(w2[...], hidden, preferred_element_type=F32)
        raw = e[24:32] + b_out[3]
        density = jnp.maximum(raw, 0.0) + jnp.log1p(jnp.exp(-jnp.abs(raw)))
        alpha = 1.0 - jnp.exp(coverage * density)
        remaining = state[3]
        share = remaining * alpha
        colours = [
            state[o] + share * (0.5 * jnp.tanh(e[8 * o : 8 * o + 8] + 0.5 * b_out[o]) + 0.5)
            for o in range(3)
        ]
        return (*colours, remaining * (1.0 - alpha))

    zero = jnp.zeros((8, half), F32)
    return lax.fori_loop(0, layers, layer, (zero, zero, zero, zero + 1.0), unroll=2)


def coverage_of(occ, optical, half):
    blocks = half // 128
    sub = iota((8, 128), 0)
    cols = []
    for k in range(blocks):
        left = -optical * occ[k].astype(F32)
        right = -optical * occ[k + blocks].astype(F32)
        cols.append(jnp.where(sub < 4, left, right))
    return jnp.concatenate(cols, 1)


def send_kernel(where, feats, w1, w2, b_out, occ, out, *, optical):
    half = feats.shape[4]
    coverage = coverage_of(occ, optical, half)
    parity = 1 - (where[0] & 1)

    def piece(zpos, carry):
        state = march(feats, w1, w2, b_out, coverage, parity, zpos)
        for o in range(4):
            out[zpos, o] = state[o]
        return carry

    lax.fori_loop(0, 4, piece, 0)


def over(parts, places):
    colours = [None] * 3
    total = None
    for i, part in enumerate(parts):
        light = None
        for j, other in enumerate(parts):
            if j != i:
                factor = jnp.where(places[j] < places[i], other[3], 1.0)
                light = factor if light is None else light * factor
        for o in range(3):
            term = light * part[o]
            colours[o] = term if colours[o] is None else colours[o] + term
        total = part[3] if total is None else total * part[3]
    return (*colours, total)


def keep_kernel(where, order, feats, w1, w2, b_out, occ, received, out, *, optical, step):
    half = feats.shape[4]
    coverage = coverage_of(occ, optical, half)
    d = where[0]
    zpos = ((d >> 1) & 3) ^ step
    state = march(feats, w1, w2, b_out, coverage, d & 1, zpos)
    other = tuple(received[zpos, o] for o in range(4))
    merged = over((state, other), (order[d] & 1, order[d ^ 1] & 1))
    for o in range(4):
        out[o] = merged[o]


def merge_z_kernel(where, order, part0, part1, part2, part3, out0, out1, out2, out3):
    d = where[0]
    parts = [tuple(p[o] for o in range(4)) for p in (part0, part1, part2, part3)]
    places = [(order[d ^ (k << 1)] >> 1) & 3 for k in range(4)]
    merged = over(parts, places)
    xpos = d >> 3
    for k, out in enumerate((out0, out1, out2, out3)):
        shift = (8 - (xpos ^ k)) % 8
        for o in range(4):
            turned = pltpu.roll(merged[o], shift, 0)
            out[o] = jnp.concatenate([turned[0:1], turned[4:5]], 0)


def merge_x_kernel(where, order, part0, part1, part2, part3, out):
    d = where[0]
    parts = [tuple(p[o] for o in range(4)) for p in (part0, part1, part2, part3)]
    places = [order[d ^ (k << 3)] >> 3 for k in range(4)]
    merged = over(parts, places)
    for o in range(3):
        out[o] = merged[o]


def filter_kernel(weight, bias, above, centre, below, out):
    half = centre.shape[2]
    lane = iota((2, half), 1)
    sub = iota((2, half), 0)
    sums = [jnp.full((2, half), bias[o], F32) for o in range(3)]
    for i in range(3):
        for a, rows in enumerate((above, centre, below)):
            row = rows[i]
            flipped = jnp.concatenate([row[1:2], row[0:1]], 0)
            left = jnp.where(
                lane == 0, jnp.where(sub == 1, pltpu.roll(flipped, 1, 1), 0.0), pltpu.roll(row, 1, 1)
            )
            right = jnp.where(
                lane == half - 1,
                jnp.where(sub == 0, pltpu.roll(flipped, half - 1, 1), 0.0),
                pltpu.roll(row, half - 1, 1),
            )
            for b, window in enumerate((left, row, right)):
                for o in range(3):
                    sums[o] = sums[o] + weight[((o * 3 + i) * 3 + a) * 3 + b] * window
    for o in range(3):
        out[o, :, :half] = sums[o][0:1]
        out[o, :, half:] = sums[o][1:2]


VMEM = pl.BlockSpec(memory_space=pltpu.VMEM)
SMEM = pl.BlockSpec(memory_space=pltpu.SMEM)


def call(kernel, name, outs, specs, *args, scratch=()):
    return pl.pallas_call(
        kernel,
        out_shape=outs,
        in_specs=specs,
        out_specs=jax.tree.map(lambda _: VMEM, outs),
        scratch_shapes=scratch,
        compiler_params=pltpu.CompilerParams(vmem_limit_bytes=40 * 2**20),
        name=name,
    )(*args)


def shape(dims, dtype=F32):
    return jax.ShapeDtypeStruct(dims, dtype)


def shards(volume, occupancy, slab_order, w_in, b_in, w_out, b_out, conv_weight, conv_bias):
    strips = lax.axis_size("strip")
    depths = lax.axis_size("depth")
    layers, rows, columns = volume.shape
    half = columns // 2
    optical = 2.0 / (layers * depths)
    d = lax.axis_index("depth")
    where = d.astype(jnp.int32).reshape(1)
    down = [(i, i + 1) for i in range(strips - 1)]
    up = [(i + 1, i) for i in range(strips - 1)]
    top = lax.ppermute(volume[:, rows - 1 :], "strip", down)
    bot = lax.ppermute(volume[:, :1], "strip", up)
    feats, w1, w2 = call(
        feature_kernel,
        "features",
        (
            shape((2, 4, layers, KDIM, half), BF16),
            shape((HIDDEN * 8, KDIM), BF16),
            shape((32, HIDDEN * 8), BF16),
        ),
        [VMEM] * 6,
        volume,
        top,
        bot,
        w_in,
        b_in.reshape(1, HIDDEN),
        w_out,
        scratch=[pltpu.VMEM((rows * columns // 128, 128), F32), pltpu.VMEM((layers, 8, 8, half), F32)],
    )
    occ = occupancy.reshape(-1)
    net = (feats, w1, w2, b_out, occ)
    net_specs = [VMEM, VMEM, VMEM, SMEM, SMEM]
    sent = call(
        functools.partial(send_kernel, optical=optical),
        "march_send",
        shape((4, 4, 8, half)),
        [SMEM] + net_specs,
        where,
        *net,
    )
    received = lax.ppermute(sent, "depth", [(i, i ^ 1) for i in range(depths)])
    parts = [None] * 4
    for step in (1, 2, 3, 0):
        piece = call(
            functools.partial(keep_kernel, optical=optical, step=step),
            f"march_keep{step}",
            shape((4, 8, half)),
            [SMEM, SMEM] + net_specs + [VMEM],
            where,
            slab_order,
            *net,
            received,
        )
        if step:
            piece = lax.ppermute(piece, "depth", [(i, i ^ (step << 1)) for i in range(depths)])
        parts[step] = piece
    quads = call(
        merge_z_kernel,
        "merge_z",
        tuple(shape((4, 2, half)) for _ in range(4)),
        [SMEM, SMEM] + [VMEM] * 4,
        where,
        slab_order,
        *parts,
    )
    quads = [
        lax.ppermute(quads[k], "depth", [(i, i ^ (k << 3)) for i in range(depths)]) if k else quads[0]
        for k in range(4)
    ]
    picture = call(
        merge_x_kernel,
        "merge_x",
        shape((3, 2, half)),
        [SMEM, SMEM] + [VMEM] * 4,
        where,
        slab_order,
        *quads,
    )
    count = strips * depths
    above = lax.ppermute(picture, ("strip", "depth"), [(i, i + 1) for i in range(count - 1)])
    below = lax.ppermute(picture, ("strip", "depth"), [(i + 1, i) for i in range(count - 1)])
    filtered = call(
        filter_kernel,
        "filter",
        shape((3, 1, columns)),
        [SMEM, SMEM] + [VMEM] * 3,
        conv_weight.reshape(-1),
        conv_bias,
        above,
        picture,
        below,
    )
    return filtered.reshape(3, 1, 1, 1, columns)


def solution(mesh):
    placed = (
        P("depth", "strip", None),
        P("depth", "strip", None),
        P(),
        P(),
        P(),
        P(),
        P(),
        P(),
        P(),
    )
    return jax.shard_map(
        shards,
        mesh=mesh,
        in_specs=placed,
        out_specs=P(None, "strip", None, "depth", None),
        check_vma=False,
    )
```

time: 159 us -> 86.5 us (0.54); the launches traced: 156 us -> 86.2 us
  matrix products: 61.1 us -> 0 us
  Pallas kernels: 0 us -> 43.3 us
  other arithmetic: 22.6 us -> 0 us
  local copies, waits for them, and re-layouts: 24 us -> 5.91 us
  waiting for transfers between devices: 25.1 us -> 16.6 us
  between operations: 3.77 us -> 0.2 us
    dot_general x8 -> x0, matrix products: 61.1 us -> none  [layer_step(): jnp.dot(w_out.T, hidden, preferred_element_type=jnp.float32)]
    pallas_call x0 -> x9, Pallas kernels: none -> 43.3 us  [call(): pl.pallas_call(kernel, out_shape=outs, in_specs=specs, out_specs=jax.tree...]
    while x16 -> x0, local copies, waits for them, and re-layouts: 11.9 us -> none
    ppermute x11, waiting for transfers between devices: 25.1 us -> 16.6 us  [the longest x1 7.3 us: shards(): lax.ppermute(picture, ('strip', 'depth'), [(i, i + 1) for i in range(coun...]
    slice x11 -> x1, local copies, waits for them, and re-layouts: 7.47 us -> 1.15 us  [shards(): bot = lax.ppermute(volume[:, :1], 'strip', up)]
    add x13 -> x0, other arithmetic: 5.83 us -> none  [the longest x8 5.35 us: layer_step(): colour_sum = colour_sum + (remaining * alpha_val)[None] * colour]
    div x8 -> x0, other arithmetic: 4.4 us -> none  [layer_step(): colour = jax.nn.sigmoid(output[:3])]
    another operation x3 -> x0, other arithmetic: 4.21 us -> none  [shards(): jnp.stack([scalar_field, grad_cols, grad_rows, grad_depth], 1)]
  transfers between devices with their start and end apart: 11 -> 11, of which waited for: 10 -> 5; matrix products, arithmetic and copies ran while one was open for 1% -> 1% of each run, Pallas kernels for 0% -> 17%
where the time goes in v1:
time: 86.5 us; the launch traced here: 86.2 us
  Pallas kernels  43.3 us (50%)
  starting transfers between devices  20.2 us (23%)
  waiting for transfers between devices  16.6 us (19%)
  local copies, waits for them, and re-layouts  5.91 us (7%)
    pallas_call x9, Pallas kernels, call(): pl.pallas_call(kernel, out_shape=outs, in_specs=specs, out_specs=jax.tree...  43.3 us
    ppermute x1, waiting for transfers between devices, shards(): lax.ppermute(picture, ('strip', 'depth'), [(i, i + 1) for i in range(coun...  7.3 us
    ppermute x3, starting transfers between devices, shards(): lax.ppermute(piece, 'depth', [(i, i ^ step << 1) for i in range(depths)])  5.16 us
    ppermute x3, starting transfers between devices, shards(): lax.ppermute(quads[k], 'depth', [(i, i ^ k << 3) for i in range(depths)])  4.78 us
    unnamed x17, local copies, waits for them, and re-layouts  4.67 us
    ppermute x3, waiting for transfers between devices, shards(): lax.ppermute(quads[k], 'depth', [(i, i ^ k << 3) for i in range(depths)])  4.65 us
    ppermute x1, starting transfers between devices, shards(): top = lax.ppermute(volume[:, rows - 1:], 'strip', down)  3.19 us
    ppermute x1, waiting for transfers between devices, shards(): bot = lax.ppermute(volume[:, :1], 'strip', up)  2.7 us
  transfers between devices with their start and end apart: 11, of which 5 were waited for; matrix products, arithmetic and copies ran while one was open for 1% of the time, Pallas kernels for 17%

profile of v1, /device:TPU:16, one launch (start us, length us, event | category | flops | bytes accessed | tf_op | source)
XLA Modules:
  0.0 86.2 jit_solution(10546813847758842380)
XLA Ops:
  0.0 1.1 %fusion = (bf16[8,1,2048]{2,1,0:T(2,128)(2,1)S(1)}, bf16[8,1,2048]{2,1,0:T(2,128)(2,1)S(1)}) fusion(bf16[8,32,2048]{2,1,0:T(8,128)(2,1)} %vol.1), kind=kLoop, calls=%fused_computation | loop fusion | bytes 131072 | tf_op jit(solution)/shard_map/slice | solution.py:263
  1.2 3.2 %collective-permute-start = (bf16[8,1,2048]{2,1,0:T(2,128)(2,1)S(1)}, bf16[8,1,2048]{2,1,0:T(2,128)(2,1)S(1)}, u32[]{:S(2)}, u32[]{:S(2)}) collective-permute-start(bf16[8,1,2048]{2,1,0:T(2,128)(2,1)S(1)} %get-tuple-element.20), channel_id=1, source_target_pairs={{0,32},{32,64},{64,96},{1,33},{33,65},{65,97},{2,34},{34,66},{66,9... | collective-permute-start | bytes 98312 | tf_op jit(solution)/shard_map/ppermute | solution.py:262
  4.4 2.7 %collective-permute-start.1 = (bf16[8,1,2048]{2,1,0:T(2,128)(2,1)S(1)}, bf16[8,1,2048]{2,1,0:T(2,128)(2,1)S(1)}, u32[]{:S(2)}, u32[]{:S(2)}) collective-permute-start(bf16[8,1,2048]{2,1,0:T(2,128)(2,1)S(1)} %get-tuple-element.19), channel_id=1, source_target_pairs={{32,0},{64,32},{96,64},{33,1},{65,33},{97,65},{34,2},{66,34},{98,6... | collective-permute-start | bytes 98312 | tf_op jit(solution)/shard_map/ppermute | solution.py:263
  7.0 0.8 copy.10.w_out
  7.8 2.7 %collective-permute-done.1.bot = bf16[8,1,2048]{2,1,0:T(2,128)(2,1)S(1)} collective-permute-done((bf16[8,1,2048]{2,1,0:T(2,128)(2,1)S(1)}, bf16[8,1,2048]{2,1,0:T(2,128)(2,1)S(1)}, u32[]{:S(2)}, u32[]{:S(2)}) %collective-permute-start.1) | collective-permute-done | bytes 32800 | tf_op jit(solution)/shard_map/ppermute | solution.py:263
  10.5 1.2 %copy-done = bf16[8,32,2048]{2,1,0:T(8,128)(2,1)S(1)} copy-done((bf16[8,32,2048]{2,1,0:T(8,128)(2,1)S(1)}, bf16[8,32,2048]{2,1,0:T(8,128)(2,1)}, u32[]{:S(2)}) %copy-start) | copy-done | bytes 1048600
  11.7 0.7 copy-done.4
  12.4 0.7 copy-done.5
  13.1 3.2 %features.1 = (bf16[2,4,8,48,1024]{4,3,2,1,0:T(8,128)(2,1)S(1)}, bf16[512,48]{1,0:T(8,128)(2,1)S(1)}, bf16[32,512]{1,0:T(8,128)(2,1)S(1)}) custom-call(bf16[8,32,2048]{2,1,0:T(8,128)(2,1)S(1)} %copy-done, bf16[8,1,2048]{2,1,0:T(2,128)(2,1)S(1)} %collective-permute-done.top, bf16[8,1,2048]{2,1,0:T(2,128)(2,1)S(1)} %collective-permute-done.1.bot, ...), custom_call_target="tpu_custom_call" | custom-call | tf_op jit(solution)/shard_map/features/pallas_call | solution.py:237
  16.3 0.6 copy-done.2
  17.0 0.7 copy-done.3
  17.6 17.8 %march_send.1 = f32[4,4,8,1024]{3,2,1,0:T(8,128)S(1)} custom-call(s32[1]{0:T(128)} %bitcast.where, bf16[2,4,8,48,1024]{4,3,2,1,0:T(8,128)(2,1)S(1)} %get-tuple-element.12.feats, bf16[512,48]{1,0:T(8,128)(2,1)S(1)} %get-tuple-element.13.w1, bf16[32,512]{1,0:T(8,128)(2,1)S(1)} %get-tuple-element.14.w2, f32[4]{0:T(128)S(1)} %copy-done.2, s32[16]{0:T(128)S(1)} %bitcast.6), custom_call_target="tpu_custom_call" | custom-call | tf_op jit(solution)/shard_map/march_send/pallas_call | solution.py:237
  35.5 1.9 %collective-permute-done.2.received = f32[4,4,8,1024]{3,2,1,0:T(8,128)S(1)} collective-permute-done((f32[4,4,8,1024]{3,2,1,0:T(8,128)S(1)}, f32[4,4,8,1024]{3,2,1,0:T(8,128)S(1)}, u32[]{:S(2)}, u32[]{:S(2)}) %collective-permute-start.2) | collective-permute-done | bytes 524320 | tf_op jit(solution)/shard_map/ppermute | solution.py:292
  37.4 4.9 %march_keep3.1 = f32[4,8,1024]{2,1,0:T(8,128)S(1)} custom-call(s32[1]{0:T(128)} %bitcast.where, s32[32]{0:T(128)S(1)} %copy-done.1, bf16[2,4,8,48,1024]{4,3,2,1,0:T(8,128)(2,1)S(1)} %get-tuple-element.12.feats, bf16[512,48]{1,0:T(8,128)(2,1)S(1)} %get-tuple-element.13.w1, bf16[32,512]{1,0:T(8,128)(2,1)S(1)} %get-tuple-element.14.w2, f32[4]{0:T(128)S(1)} %copy-done.2, ...), custom_call_target="tpu_custom_call" | custom-call | tf_op jit(solution)/shard_map/march_keep3/pallas_call | solution.py:237
  42.3 4.1 %collective-permute-start.5 = (f32[4,8,1024]{2,1,0:T(8,128)S(1)}, f32[4,8,1024]{2,1,0:T(8,128)S(1)}, u32[]{:S(2)}, u32[]{:S(2)}) collective-permute-start(f32[4,8,1024]{2,1,0:T(8,128)S(1)} %march_keep3.1), channel_id=1, source_target_pairs={{0,6},{1,7},{2,4},{3,5},{4,2},{5,3},{6,0},{7,1},{8,14},{9,15},{10,... | collective-permute-start | bytes 393224 | tf_op jit(solution)/shard_map/ppermute | solution.py:306
  46.5 4.9 %march_keep2.1 = f32[4,8,1024]{2,1,0:T(8,128)S(1)} custom-call(s32[1]{0:T(128)} %bitcast.where, s32[32]{0:T(128)S(1)} %copy-done.1, bf16[2,4,8,48,1024]{4,3,2,1,0:T(8,128)(2,1)S(1)} %get-tuple-element.12.feats, bf16[512,48]{1,0:T(8,128)(2,1)S(1)} %get-tuple-element.13.w1, bf16[32,512]{1,0:T(8,128)(2,1)S(1)} %get-tuple-element.14.w2, f32[4]{0:T(128)S(1)} %copy-done.2, ...), custom_call_target="tpu_custom_call" | custom-call | tf_op jit(solution)/shard_map/march_keep2/pallas_call | solution.py:237
  51.4 0.1 collective-permute-start.4
  51.5 4.9 %march_keep1.1 = f32[4,8,1024]{2,1,0:T(8,128)S(1)} custom-call(s32[1]{0:T(128)} %bitcast.where, s32[32]{0:T(128)S(1)} %copy-done.1, bf16[2,4,8,48,1024]{4,3,2,1,0:T(8,128)(2,1)S(1)} %get-tuple-element.12.feats, bf16[512,48]{1,0:T(8,128)(2,1)S(1)} %get-tuple-element.13.w1, bf16[32,512]{1,0:T(8,128)(2,1)S(1)} %get-tuple-element.14.w2, f32[4]{0:T(128)S(1)} %copy-done.2, ...), custom_call_target="tpu_custom_call" | custom-call | tf_op jit(solution)/shard_map/march_keep1/pallas_call | solution.py:237
  56.4 0.9 %collective-permute-start.3 = (f32[4,8,1024]{2,1,0:T(8,128)S(1)}, f32[4,8,1024]{2,1,0:T(8,128)S(1)}, u32[]{:S(2)}, u32[]{:S(2)}) collective-permute-start(f32[4,8,1024]{2,1,0:T(8,128)S(1)} %march_keep1.1), channel_id=1, source_target_pairs={{0,2},{1,3},{2,0},{3,1},{4,6},{5,7},{6,4},{7,5},{8,10},{9,11},{10,... | collective-permute-start | bytes 393224 | tf_op jit(solution)/shard_map/ppermute | solution.py:306
  57.3 4.9 %march_keep0.1.part0 = f32[4,8,1024]{2,1,0:T(8,128)S(1)} custom-call(s32[1]{0:T(128)} %bitcast.where, s32[32]{0:T(128)S(1)} %copy-done.1, bf16[2,4,8,48,1024]{4,3,2,1,0:T(8,128)(2,1)S(1)} %get-tuple-element.12.feats, bf16[512,48]{1,0:T(8,128)(2,1)S(1)} %get-tuple-element.13.w1, bf16[32,512]{1,0:T(8,128)(2,1)S(1)} %get-tuple-element.14.w2, f32[4]{0:T(128)S(1)} %copy-done.2, ...), custom_call_target="tpu_custom_call" | custom-call | tf_op jit(solution)/shard_map/march_keep0/pallas_call | solution.py:237
  62.3 0.7 merge_z.1
  62.9 1.6 %collective-permute-start.6 = (f32[4,2,1024]{2,1,0:T(2,128)S(1)}, f32[4,2,1024]{2,1,0:T(2,128)S(1)}, u32[]{:S(2)}, u32[]{:S(2)}) collective-permute-start(f32[4,2,1024]{2,1,0:T(2,128)S(1)} %get-tuple-element.16), channel_id=1, source_target_pairs={{0,8},{1,9},{2,10},{3,11},{4,12},{5,13},{6,14},{7,15},{8,0},{9,1},... | collective-permute-start | bytes 98312 | tf_op jit(solution)/shard_map/ppermute | solution.py:318
  64.5 2.7 %collective-permute-start.7 = (f32[4,2,1024]{2,1,0:T(2,128)S(1)}, f32[4,2,1024]{2,1,0:T(2,128)S(1)}, u32[]{:S(2)}, u32[]{:S(2)}) collective-permute-start(f32[4,2,1024]{2,1,0:T(2,128)S(1)} %get-tuple-element.17), channel_id=1, source_target_pairs={{0,16},{1,17},{2,18},{3,19},{4,20},{5,21},{6,22},{7,23},{8,24},{9,... | collective-permute-start | bytes 98312 | tf_op jit(solution)/shard_map/ppermute | solution.py:318
  67.2 0.5 collective-permute-start.8
  67.7 2.2 %collective-permute-done.7.part2 = f32[4,2,1024]{2,1,0:T(2,128)S(1)} collective-permute-done((f32[4,2,1024]{2,1,0:T(2,128)S(1)}, f32[4,2,1024]{2,1,0:T(2,128)S(1)}, u32[]{:S(2)}, u32[]{:S(2)}) %collective-permute-start.7) | collective-permute-done | bytes 32800 | tf_op jit(solution)/shard_map/ppermute | solution.py:318
  69.9 2.4 %collective-permute-done.8.part3 = f32[4,2,1024]{2,1,0:T(2,128)S(1)} collective-permute-done((f32[4,2,1024]{2,1,0:T(2,128)S(1)}, f32[4,2,1024]{2,1,0:T(2,128)S(1)}, u32[]{:S(2)}, u32[]{:S(2)}) %collective-permute-start.8) | collective-permute-done | bytes 32800 | tf_op jit(solution)/shard_map/ppermute | solution.py:318
  72.4 0.6 merge_x.1.centre
  72.9 2.4 %collective-permute-start.10 = (f32[3,2,1024]{2,1,0:T(2,128)S(1)}, f32[3,2,1024]{2,1,0:T(2,128)S(1)}, u32[]{:S(2)}, u32[]{:S(2)}) collective-permute-start(f32[3,2,1024]{2,1,0:T(2,128)S(1)} %merge_x.1.centre), channel_id=1, source_target_pairs={{1,0},{2,1},{3,2},{4,3},{5,4},{6,5},{7,6},{8,7},{9,8},{10,9},{11,1... | collective-permute-start | bytes 73736 | tf_op jit(solution)/shard_map/ppermute | solution.py:332
  75.4 1.9 %collective-permute-start.9 = (f32[3,2,1024]{2,1,0:T(2,128)S(1)}, f32[3,2,1024]{2,1,0:T(2,128)S(1)}, u32[]{:S(2)}, u32[]{:S(2)}) collective-permute-start(f32[3,2,1024]{2,1,0:T(2,128)S(1)} %merge_x.1.centre), channel_id=1, source_target_pairs={{0,1},{1,2},{2,3},{3,4},{4,5},{5,6},{6,7},{7,8},{8,9},{9,10},{10,1... | collective-permute-start | bytes 73736 | tf_op jit(solution)/shard_map/ppermute | solution.py:331
  77.3 0.1 reshape.15.weight
  77.4 7.3 %collective-permute-done.9.above = f32[3,2,1024]{2,1,0:T(2,128)S(1)} collective-permute-done((f32[3,2,1024]{2,1,0:T(2,128)S(1)}, f32[3,2,1024]{2,1,0:T(2,128)S(1)}, u32[]{:S(2)}, u32[]{:S(2)}) %collective-permute-start.9) | collective-permute-done | bytes 24608 | tf_op jit(solution)/shard_map/ppermute | solution.py:331
  84.7 1.5 %filter.1 = f32[3,1,2048]{2,1,0:T(1,128)} custom-call(f32[81]{0:T(128)S(1)} %reshape.15.weight, f32[3]{0:T(128)S(1)} %copy-done.6, f32[3,2,1024]{2,1,0:T(2,128)S(1)} %collective-permute-done.9.above, f32[3,2,1024]{2,1,0:T(2,128)S(1)} %merge_x.1.centre, f32[3,2,1024]{2,1,0:T(2,128)S(1)} %collective-permute-done.10.below), custom_call_target="tpu_custom_call" | custom-call | tf_op jit(solution)/shard_map/filter/pallas_call | solution.py:237
  (18 shorter events, 0.1 us)
Async XLA Ops:
  0.0 37.4 %copy-start.1 = (s32[32]{0:T(128)S(1)}, s32[32]{0:T(128)}, u32[]{:S(2)}) copy-start(s32[32]{0:T(128)} %order.11) | copy-start | bytes 388
  1.2 6.7 %collective-permute-start = (bf16[8,1,2048]{2,1,0:T(2,128)(2,1)S(1)}, bf16[8,1,2048]{2,1,0:T(2,128)(2,1)S(1)}, u32[]{:S(2)}, u32[]{:S(2)}) collective-permute-start(bf16[8,1,2048]{2,1,0:T(2,128)(2,1)S(1)} %get-tuple-element.20), channel_id=1, source_target_pairs={{0,32},{32,64},{64,96},{1,33},{33,65},{65,97},{2,34},{34,66},{66,9... | collective-permute-start | bytes 98312 | tf_op jit(solution)/shard_map/ppermute | solution.py:262
  4.4 6.2 %collective-permute-start.1 = (bf16[8,1,2048]{2,1,0:T(2,128)(2,1)S(1)}, bf16[8,1,2048]{2,1,0:T(2,128)(2,1)S(1)}, u32[]{:S(2)}, u32[]{:S(2)}) collective-permute-start(bf16[8,1,2048]{2,1,0:T(2,128)(2,1)S(1)} %get-tuple-element.19), channel_id=1, source_target_pairs={{32,0},{64,32},{96,64},{33,1},{65,33},{97,65},{34,2},{66,34},{98,6... | collective-permute-start | bytes 98312 | tf_op jit(solution)/shard_map/ppermute | solution.py:263
  10.5 1.2 %copy-start = (bf16[8,32,2048]{2,1,0:T(8,128)(2,1)S(1)}, bf16[8,32,2048]{2,1,0:T(8,128)(2,1)}, u32[]{:S(2)}) copy-start(bf16[8,32,2048]{2,1,0:T(8,128)(2,1)} %vol.1) | copy-start | bytes 3145732
  11.7 0.7 copy-start.4
  12.4 0.7 copy-start.5
  16.3 0.7 copy-start.2
  17.0 0.7 copy-start.3
  35.5 2.0 %collective-permute-start.2 = (f32[4,4,8,1024]{3,2,1,0:T(8,128)S(1)}, f32[4,4,8,1024]{3,2,1,0:T(8,128)S(1)}, u32[]{:S(2)}, u32[]{:S(2)}) collective-permute-start(f32[4,4,8,1024]{3,2,1,0:T(8,128)S(1)} %march_send.1), channel_id=1, source_target_pairs={{0,1},{1,0},{2,3},{3,2},{4,5},{5,4},{6,7},{7,6},{8,9},{9,8},{10,11... | collective-permute-start | bytes 1572872 | tf_op jit(solution)/shard_map/ppermute | solution.py:292
  42.3 19.9 %collective-permute-start.5 = (f32[4,8,1024]{2,1,0:T(8,128)S(1)}, f32[4,8,1024]{2,1,0:T(8,128)S(1)}, u32[]{:S(2)}, u32[]{:S(2)}) collective-permute-start(f32[4,8,1024]{2,1,0:T(8,128)S(1)} %march_keep3.1), channel_id=1, source_target_pairs={{0,6},{1,7},{2,4},{3,5},{4,2},{5,3},{6,0},{7,1},{8,14},{9,15},{10,... | collective-permute-start | bytes 393224 | tf_op jit(solution)/shard_map/ppermute | solution.py:306
  51.4 25.9 %copy-start.7 = (f32[3,3,3,3]{3,2,1,0:T(4,128)S(1)}, f32[3,3,3,3]{3,2,1,0:T(4,128)}, u32[]{:S(2)}) copy-start(f32[3,3,3,3]{3,2,1,0:T(4,128)} %param.16) | copy-start | bytes 976
  51.4 33.3 %copy-start.6 = (f32[3]{0:T(128)S(1)}, f32[3]{0:T(128)}, u32[]{:S(2)}) copy-start(f32[3]{0:T(128)} %bias.1) | copy-start | bytes 40
  51.4 10.8 %collective-permute-start.4 = (f32[4,8,1024]{2,1,0:T(8,128)S(1)}, f32[4,8,1024]{2,1,0:T(8,128)S(1)}, u32[]{:S(2)}, u32[]{:S(2)}) collective-permute-start(f32[4,8,1024]{2,1,0:T(8,128)S(1)} %march_keep2.1), channel_id=1, source_target_pairs={{0,4},{1,5},{2,6},{3,7},{4,0},{5,1},{6,2},{7,3},{8,12},{9,13},{10,... | collective-permute-start | bytes 393224 | tf_op jit(solution)/shard_map/ppermute | solution.py:306
  56.4 5.9 %collective-permute-start.3 = (f32[4,8,1024]{2,1,0:T(8,128)S(1)}, f32[4,8,1024]{2,1,0:T(8,128)S(1)}, u32[]{:S(2)}, u32[]{:S(2)}) collective-permute-start(f32[4,8,1024]{2,1,0:T(8,128)S(1)} %march_keep1.1), channel_id=1, source_target_pairs={{0,2},{1,3},{2,0},{3,1},{4,6},{5,7},{6,4},{7,5},{8,10},{9,11},{10,... | collective-permute-start | bytes 393224 | tf_op jit(solution)/shard_map/ppermute | solution.py:306
  62.9 4.8 %collective-permute-start.6 = (f32[4,2,1024]{2,1,0:T(2,128)S(1)}, f32[4,2,1024]{2,1,0:T(2,128)S(1)}, u32[]{:S(2)}, u32[]{:S(2)}) collective-permute-start(f32[4,2,1024]{2,1,0:T(2,128)S(1)} %get-tuple-element.16), channel_id=1, source_target_pairs={{0,8},{1,9},{2,10},{3,11},{4,12},{5,13},{6,14},{7,15},{8,0},{9,1},... | collective-permute-start | bytes 98312 | tf_op jit(solution)/shard_map/ppermute | solution.py:318
  64.5 5.4 %collective-permute-start.7 = (f32[4,2,1024]{2,1,0:T(2,128)S(1)}, f32[4,2,1024]{2,1,0:T(2,128)S(1)}, u32[]{:S(2)}, u32[]{:S(2)}) collective-permute-start(f32[4,2,1024]{2,1,0:T(2,128)S(1)} %get-tuple-element.17), channel_id=1, source_target_pairs={{0,16},{1,17},{2,18},{3,19},{4,20},{5,21},{6,22},{7,23},{8,24},{9,... | collective-permute-start | bytes 98312 | tf_op jit(solution)/shard_map/ppermute | solution.py:318
  67.2 5.1 %collective-permute-start.8 = (f32[4,2,1024]{2,1,0:T(2,128)S(1)}, f32[4,2,1024]{2,1,0:T(2,128)S(1)}, u32[]{:S(2)}, u32[]{:S(2)}) collective-permute-start(f32[4,2,1024]{2,1,0:T(2,128)S(1)} %get-tuple-element.18), channel_id=1, source_target_pairs={{0,24},{1,25},{2,26},{3,27},{4,28},{5,29},{6,30},{7,31},{8,16},{9,... | collective-permute-start | bytes 98312 | tf_op jit(solution)/shard_map/ppermute | solution.py:318
  72.9 4.5 %collective-permute-start.10 = (f32[3,2,1024]{2,1,0:T(2,128)S(1)}, f32[3,2,1024]{2,1,0:T(2,128)S(1)}, u32[]{:S(2)}, u32[]{:S(2)}) collective-permute-start(f32[3,2,1024]{2,1,0:T(2,128)S(1)} %merge_x.1.centre), channel_id=1, source_target_pairs={{1,0},{2,1},{3,2},{4,3},{5,4},{6,5},{7,6},{8,7},{9,8},{10,9},{11,1... | collective-permute-start | bytes 73736 | tf_op jit(solution)/shard_map/ppermute | solution.py:332
  75.4 9.4 %collective-permute-start.9 = (f32[3,2,1024]{2,1,0:T(2,128)S(1)}, f32[3,2,1024]{2,1,0:T(2,128)S(1)}, u32[]{:S(2)}, u32[]{:S(2)}) collective-permute-start(f32[3,2,1024]{2,1,0:T(2,128)S(1)} %merge_x.1.centre), channel_id=1, source_target_pairs={{0,1},{1,2},{2,3},{3,4},{4,5},{5,6},{6,7},{7,8},{8,9},{9,10},{10,1... | collective-permute-start | bytes 73736 | tf_op jit(solution)/shard_map/ppermute | solution.py:331

commit v2 on v1

--- a/solution.py
+++ b/solution.py
@@ -17,13 +17,13 @@
     return lax.broadcasted_iota(jnp.int32, shape, dim)
 
 
-def prepare_weights(w_in, b_in, w_out, w1, w2):
-    bias = 0.5 * b_in[...]
+def prepare_weights(facts, w1, w2):
+    bias = 0.5 * facts[4:5]
     hi = bias.astype(BF16).astype(F32)
     mid = (bias - hi).astype(BF16).astype(F32)
     low = bias - hi - mid
     table = jnp.concatenate(
-        [0.5 * w_in[...].astype(F32), hi, mid, low, jnp.zeros((1, HIDDEN), F32)], 0
+        [0.5 * facts[0:4], hi, mid, low, jnp.zeros((1, HIDDEN), F32)], 0
     ).astype(BF16)
     spread = (iota((HIDDEN * 8, HIDDEN), 0) // 8 == iota((HIDDEN * 8, HIDDEN), 1)).astype(BF16)
     nt = (((1,), (1,)), ((), ()))
@@ -37,7 +37,7 @@
     w1[...] = jnp.where((k >= 32) | (r % 8 == k % 8), wide, 0.0).astype(BF16)
     pick = (iota((32, 4), 0) // 8 == iota((32, 4), 1)).astype(BF16)
     out_rows = lax.dot_general(
-        pick, w_out[...], (((1,), (1,)), ((), ())), preferred_element_type=F32
+        pick, facts[5:9].astype(BF16), (((1,), (0,)), ((), ())), preferred_element_type=F32
     ).astype(BF16)
     full = lax.dot_general(out_rows, spread, nt, preferred_element_type=F32)
     o = iota((32, HIDDEN * 8), 0)
@@ -46,11 +46,16 @@
     w2[...] = jnp.where(o % 8 == q % 8, full * scale, 0.0).astype(BF16)
 
 
-def feature_kernel(vol, top, bot, w_in, b_in, w_out, feats, w1, w2, lines, planes):
+def feature_kernel(
+    vol, facts, feats, w1, w2, coverage, shift, lines, planes, *, optical
+):
     layers, rows, columns = vol.shape
     half = columns // 2
-    prepare_weights(w_in, b_in, w_out, w1, w2)
-
+    prepare_weights(facts, w1, w2)
+    coverage[...] = coverage_of(facts[10:11], optical, half)
+    for o in range(4):
+        scale = 0.5 if o < 3 else 1.0
+        shift[8 * o : 8 * o + 8] = jnp.broadcast_to(scale * facts[9:10, o : o + 1], (8, 128))
     blocks = half // 128
 
     def permute(z, carry):
@@ -72,8 +77,6 @@
     def gradients(z, carry):
         before = jnp.maximum(z - 1, 0)
         after = jnp.minimum(z + 1, layers - 1)
-        first = jnp.broadcast_to(top[z].astype(F32), (8, columns))
-        last = jnp.broadcast_to(bot[z].astype(F32), (8, columns))
         for j in range(8):
             s = planes[z, j]
             ahead = pltpu.roll(s, half - 1, 1)
@@ -86,14 +89,10 @@
                 above = planes[z, j - 1]
             else:
                 above = pltpu.roll(planes[z, 7], 1, 0)
-                above = jnp.where(sub == 0, first[:, :half], above)
-                above = jnp.where(sub == 4, first[:, half:], above)
             if j < 7:
                 below = planes[z, j + 1]
             else:
                 below = pltpu.roll(planes[z, 0], 7, 0)
-                below = jnp.where(sub == 3, last[:, :half], below)
-                below = jnp.where(sub == 7, last[:, half:], below)
             deep = planes[after, j] - planes[before, j]
             block = jnp.concatenate(
                 [s, 0.5 * (ahead - behind), 0.5 * (below - above), 0.5 * deep], 0
@@ -105,23 +104,56 @@
     lax.fori_loop(0, layers, gradients, 0)
 
 
-def march(feats, w1, w2, b_out, coverage, parity, zpos):
+def edge_kernel(feats, top, bot, after, edges):
     layers = feats.shape[2]
     half = feats.shape[4]
+    sub = iota((8, half), 0)
+
+    def fix(z, carry):
+        for parity, zpos, rim, low in ((0, 0, top, 0), (1, 3, bot, 3)):
+            inner = feats[1 - parity, zpos, z, 0:16].astype(F32)[0:8]
+            both = feats[parity, zpos, z, 16:32].astype(F32)
+            line = rim[z].astype(F32)
+            outer = jnp.where(sub < 4, line[:, :half], line[:, half:])
+            slope = 0.5 * (inner - outer) if parity == 0 else 0.5 * (outer - inner)
+            fixed = jnp.where(sub % 4 == low, slope, both[0:8])
+            edges[parity, z, 0:16] = feats[parity, zpos, z, 0:16]
+            edges[parity, z, 16:32] = jnp.concatenate([fixed, both[8:16]], 0).astype(BF16)
+            edges[parity, z, 32:KDIM] = feats[parity, zpos, z, 32:KDIM]
+        return carry
+
+    lax.fori_loop(0, layers, fix, 0)
+
+
+def load_plane(feats, edges, parity, zpos, x):
+    at_edge = zpos == 3 * parity
+
+    @pl.when(at_edge)
+    def _():
+        x[...] = edges[parity]
+
+    @pl.when(jnp.logical_not(at_edge))
+    def _():
+        x[...] = feats[parity, zpos]
+
+
+def march(plane, w1, w2, coverage, shift):
+    layers, _, half = plane.shape
+    cover = coverage[...]
+    lift = jnp.concatenate([shift[...]] * (half // 128), 1)
 
     def layer(z, state):
-        x = feats[parity, zpos, z]
+        x = plane[z]
         u = jnp.dot(w1[...], x, preferred_element_type=F32)
         hidden = (u * jnp.tanh(u) + u).astype(BF16)
-        e = jnp.dot(w2[...], hidden, preferred_element_type=F32)
-        raw = e[24:32] + b_out[3]
+        e = jnp.dot(w2[...], hidden, preferred_element_type=F32) + lift
+        raw = e[24:32]
         density = jnp.maximum(raw, 0.0) + jnp.log1p(jnp.exp(-jnp.abs(raw)))
-        alpha = 1.0 - jnp.exp(coverage * density)
+        alpha = 1.0 - jnp.exp(cover * density)
         remaining = state[3]
         share = remaining * alpha
         colours = [
-            state[o] + share * (0.5 * jnp.tanh(e[8 * o : 8 * o + 8] + 0.5 * b_out[o]) + 0.5)
-            for o in range(3)
+            state[o] + share * (0.5 * jnp.tanh(e[8 * o : 8 * o + 8]) + 0.5) for o in range(3)
         ]
         return (*colours, remaining * (1.0 - alpha))
 
@@ -132,26 +164,38 @@
 def coverage_of(occ, optical, half):
     blocks = half // 128
     sub = iota((8, 128), 0)
+    scaled = -optical * occ
     cols = []
     for k in range(blocks):
-        left = -optical * occ[k].astype(F32)
-        right = -optical * occ[k + blocks].astype(F32)
+        left = jnp.broadcast_to(scaled[:, k : k + 1], (8, 128))
+        right = jnp.broadcast_to(scaled[:, k + blocks : k + blocks + 1], (8, 128))
         cols.append(jnp.where(sub < 4, left, right))
     return jnp.concatenate(cols, 1)
 
 
-def send_kernel(where, feats, w1, w2, b_out, occ, out, *, optical):
-    half = feats.shape[4]
-    coverage = coverage_of(occ, optical, half)
+def send_inner_kernel(where, feats, w1, w2, coverage, shift, out):
     parity = 1 - (where[0] & 1)
 
-    def piece(zpos, carry):
-        state = march(feats, w1, w2, b_out, coverage, parity, zpos)
+    def piece(i, carry):
+        state = march(feats.at[parity, 1 + i], w1, w2, coverage, shift)
         for o in range(4):
-            out[zpos, o] = state[o]
+            out[i, o] = state[o]
         return carry
 
-    lax.fori_loop(0, 4, piece, 0)
+    lax.fori_loop(0, 2, piece, 0)
+
+
+def send_outer_kernel(where, feats, edges, w1, w2, coverage, shift, out, x):
+    parity = 1 - (where[0] & 1)
+
+    def piece(i, carry):
+        load_plane(feats, edges, parity, 3 * i, x)
+        state = march(x, w1, w2, coverage, shift)
+        for o in range(4):
+            out[i, o] = state[o]
+        return carry
+
+    lax.fori_loop(0, 2, piece, 0)
 
 
 def over(parts, places):
@@ -170,13 +214,16 @@
     return (*colours, total)
 
 
-def keep_kernel(where, order, feats, w1, w2, b_out, occ, received, out, *, optical, step):
-    half = feats.shape[4]
-    coverage = coverage_of(occ, optical, half)
+def keep_kernel(
+    where, order, feats, edges, w1, w2, coverage, shift, inner, outer, out, x, *, step
+):
     d = where[0]
     zpos = ((d >> 1) & 3) ^ step
-    state = march(feats, w1, w2, b_out, coverage, d & 1, zpos)
-    other = tuple(received[zpos, o] for o in range(4))
+    load_plane(feats, edges, d & 1, zpos, x)
+    state = march(x, w1, w2, coverage, shift)
+    slot = zpos >> 1
+    middle = (zpos == 1) | (zpos == 2)
+    other = tuple(jnp.where(middle, inner[slot, o], outer[slot, o]) for o in range(4))
     merged = over((state, other), (order[d] & 1, order[d ^ 1] & 1))
     for o in range(4):
         out[o] = merged[o]
@@ -204,14 +251,16 @@
         out[o] = merged[o]
 
 
-def filter_kernel(weight, bias, above, centre, below, out):
+def filter_kernel(where, weight, bias, beside, centre, apart, out):
     half = centre.shape[2]
+    even = (where[0] & 1) == 0
     lane = iota((2, half), 1)
     sub = iota((2, half), 0)
     sums = [jnp.full((2, half), bias[o], F32) for o in range(3)]
     for i in range(3):
-        for a, rows in enumerate((above, centre, below)):
-            row = rows[i]
+        above = jnp.where(even, apart[i], beside[i])
+        below = jnp.where(even, beside[i], apart[i])
+        for a, row in enumerate((above, centre[i], below)):
             flipped = jnp.concatenate([row[1:2], row[0:1]], 0)
             left = jnp.where(
                 lane == 0, jnp.where(sub == 1, pltpu.roll(flipped, 1, 1), 0.0), pltpu.roll(row, 1, 1)
@@ -240,7 +289,7 @@
         in_specs=specs,
         out_specs=jax.tree.map(lambda _: VMEM, outs),
         scratch_shapes=scratch,
-        compiler_params=pltpu.CompilerParams(vmem_limit_bytes=40 * 2**20),
+        compiler_params=pltpu.CompilerParams(vmem_limit_bytes=24 * 2**20),
         name=name,
     )(*args)
 
@@ -257,50 +306,80 @@
     optical = 2.0 / (layers * depths)
     d = lax.axis_index("depth")
     where = d.astype(jnp.int32).reshape(1)
-    down = [(i, i + 1) for i in range(strips - 1)]
-    up = [(i + 1, i) for i in range(strips - 1)]
-    top = lax.ppermute(volume[:, rows - 1 :], "strip", down)
-    bot = lax.ppermute(volume[:, :1], "strip", up)
-    feats, w1, w2 = call(
-        feature_kernel,
+    wide = lambda v: jnp.pad(v.astype(F32).reshape(1, -1), ((0, 0), (0, HIDDEN - v.size)))
+    facts = jnp.concatenate(
+        [w_in.astype(F32), wide(b_in), w_out.T.astype(F32), wide(b_out), wide(occupancy)], 0
+    )
+    feats, w1, w2, coverage, shift = call(
+        functools.partial(feature_kernel, optical=optical),
         "features",
         (
             shape((2, 4, layers, KDIM, half), BF16),
             shape((HIDDEN * 8, KDIM), BF16),
             shape((32, HIDDEN * 8), BF16),
+            shape((8, half)),
+            shape((32, 128)),
         ),
-        [VMEM] * 6,
+        [VMEM] * 2,
         volume,
+        facts,
+        scratch=[
+            pltpu.VMEM((rows * columns // 128, 128), F32),
+            pltpu.VMEM((layers, 8, 8, half), F32),
+        ],
+    )
+    top = lax.ppermute(volume[:, rows - 1 :], "strip", [(i, i + 1) for i in range(strips - 1)])
+    bot = lax.ppermute(volume[:, :1], "strip", [(i + 1, i) for i in range(strips - 1)])
+    net = (w1, w2, coverage, shift)
+    cores = [(i, i ^ 1) for i in range(depths)]
+    sent = call(
+        send_inner_kernel,
+        "march_send_inner",
+        shape((2, 4, 8, half)),
+        [SMEM] + [VMEM] * 5,
+        where,
+        feats,
+        *net,
+    )
+    inner = lax.ppermute(sent, "depth", cores)
+    edges = call(
+        edge_kernel,
+        "edges",
+        shape((2, layers, KDIM, half), BF16),
+        [VMEM] * 3 + [pl.BlockSpec(memory_space=pl.ANY)],
+        feats,
         top,
         bot,
-        w_in,
-        b_in.reshape(1, HIDDEN),
-        w_out,
-        scratch=[pltpu.VMEM((rows * columns // 128, 128), F32), pltpu.VMEM((layers, 8, 8, half), F32)],
-    )
-    occ = occupancy.reshape(-1)
-    net = (feats, w1, w2, b_out, occ)
-    net_specs = [VMEM, VMEM, VMEM, SMEM, SMEM]
+        sent,
+    )
+    plane = pltpu.VMEM((layers, KDIM, half), BF16)
     sent = call(
-        functools.partial(send_kernel, optical=optical),
-        "march_send",
-        shape((4, 4, 8, half)),
-        [SMEM] + net_specs,
+        send_outer_kernel,
+        "march_send_outer",
+        shape((2, 4, 8, half)),
+        [SMEM] + [VMEM] * 6,
         where,
+        feats,
+        edges,
         *net,
-    )
-    received = lax.ppermute(sent, "depth", [(i, i ^ 1) for i in range(depths)])
+        scratch=[plane],
+    )
+    outer = lax.ppermute(sent, "depth", cores)
     parts = [None] * 4
     for step in (1, 2, 3, 0):
         piece = call(
-            functools.partial(keep_kernel, optical=optical, step=step),
+            functools.partial(keep_kernel, step=step),
             f"march_keep{step}",
             shape((4, 8, half)),
-            [SMEM, SMEM] + net_specs + [VMEM],
+            [SMEM, SMEM] + [VMEM] * 8,
             where,
             slab_order,
+            feats,
+            edges,
             *net,
-            received,
+            inner,
+            outer,
+            scratch=[plane],
         )
         if step:
             piece = lax.ppermute(piece, "depth", [(i, i ^ (step << 1)) for i in range(depths)])
@@ -327,19 +406,20 @@
         slab_order,
         *quads,
     )
-    count = strips * depths
-    above = lax.ppermute(picture, ("strip", "depth"), [(i, i + 1) for i in range(count - 1)])
-    below = lax.ppermute(picture, ("strip", "depth"), [(i + 1, i) for i in range(count - 1)])
+    pairs = [(i, i + 1) for i in range(1, strips * depths - 1, 2)]
+    apart = lax.ppermute(picture, ("strip", "depth"), pairs + [(j, i) for i, j in pairs])
+    beside = lax.ppermute(picture, "depth", cores)
     filtered = call(
         filter_kernel,
         "filter",
         shape((3, 1, columns)),
-        [SMEM, SMEM] + [VMEM] * 3,
+        [SMEM] * 3 + [VMEM] * 3,
+        where,
         conv_weight.reshape(-1),
         conv_bias,
-        above,
+        beside,
         picture,
-        below,
+        apart,
     )
     return filtered.reshape(3, 1, 1, 1, columns)
 

time: 86.5 us -> 82.3 us (0.951)
  waiting for transfers between devices: 16.6 us -> 14.5 us
  local copies, waits for them, and re-layouts: 5.91 us -> 3.91 us
  other arithmetic: 0 us -> 1.34 us
  starting transfers between devices: 20.2 us -> 19 us
    ppermute x5 -> x6, waiting for transfers between devices: 11.9 us -> 8.4 us  [the longest x1 7.23 us: shards(): lax.ppermute(picture, ('strip', 'depth'), pairs + [(j, i) for i, j in pai...]
    unnamed x17 -> x8, local copies, waits for them, and re-layouts: 4.67 us -> 1.24 us
    ppermute x5 -> x6, starting transfers between devices: 10.3 us -> 8.5 us  [the longest x1 3.48 us: shards(): lax.ppermute(volume[:, rows - 1:], 'strip', [(i, i + 1) for i in range(st...]
    ppermute x3, waiting for transfers between devices: 0.01 us -> 1.44 us  [shards(): lax.ppermute(piece, 'depth', [(i, i ^ step << 1) for i in range(depths)])]
    pallas_call x9 -> x11, Pallas kernels: 43.3 us -> 43.1 us  [call(): pl.pallas_call(kernel, out_shape=outs, in_specs=specs, out_specs=jax.tree...]
  transfers between devices with their start and end apart: 11 -> 12, of which waited for: 5 -> 5; matrix products, arithmetic and copies ran while one was open for 1% -> 4% of each run, Pallas kernels for 17% -> 43%
where the time goes in v2:
time: 82.3 us; the launch traced here: 82 us
  Pallas kernels  43.1 us (52%)
  starting transfers between devices  19 us (23%)
  waiting for transfers between devices  14.5 us (18%)
  local copies, waits for them, and re-layouts  3.91 us (5%)
  other arithmetic  1.34 us (2%)
    pallas_call x11, Pallas kernels, call(): pl.pallas_call(kernel, out_shape=outs, in_specs=specs, out_specs=jax.tree...  43.1 us
    ppermute x1, waiting for transfers between devices, shards(): lax.ppermute(picture, ('strip', 'depth'), pairs + [(j, i) for i, j in pai...  7.23 us
    ppermute x3, starting transfers between devices, shards(): lax.ppermute(piece, 'depth', [(i, i ^ step << 1) for i in range(depths)])  5.76 us
    ppermute x3, starting transfers between devices, shards(): lax.ppermute(quads[k], 'depth', [(i, i ^ k << 3) for i in range(depths)])  4.78 us
    ppermute x3, waiting for transfers between devices, shards(): lax.ppermute(quads[k], 'depth', [(i, i ^ k << 3) for i in range(depths)])  4.63 us
    ppermute x1, starting transfers between devices, shards(): lax.ppermute(volume[:, rows - 1:], 'strip', [(i, i + 1) for i in range(st...  3.48 us
    ppermute x1, starting transfers between devices, shards(): lax.ppermute(volume[:, :1], 'strip', [(i + 1, i) for i in range(strips -...  2.36 us
    ppermute x1, starting transfers between devices, shards(): lax.ppermute(picture, ('strip', 'depth'), pairs + [(j, i) for i, j in pai...  1.92 us
  transfers between devices with their start and end apart: 12, of which 5 were waited for; matrix products, arithmetic and copies ran while one was open for 4% of the time, Pallas kernels for 43%

profile of v2, /device:TPU:16, one launch (start us, length us, event | category | flops | bytes accessed | tf_op | source)
XLA Modules:
  0.0 82.0 jit_solution(956794274198749498)
XLA Ops:
  0.0 1.1 %fusion = (bf16[8,1,2048]{2,1,0:T(2,128)(2,1)S(1)}, bf16[8,1,2048]{2,1,0:T(2,128)(2,1)S(1)}) fusion(bf16[8,32,2048]{2,1,0:T(8,128)(2,1)} %vol.1), kind=kLoop, calls=%fused_computation.2 | loop fusion | bytes 131072 | tf_op jit(solution)/shard_map/slice | solution.py:332
  1.1 2.4 %collective-permute-start.1 = (bf16[8,1,2048]{2,1,0:T(2,128)(2,1)S(1)}, bf16[8,1,2048]{2,1,0:T(2,128)(2,1)S(1)}, u32[]{:S(2)}, u32[]{:S(2)}) collective-permute-start(bf16[8,1,2048]{2,1,0:T(2,128)(2,1)S(1)} %get-tuple-element.23), channel_id=1, source_target_pairs={{32,0},{64,32},{96,64},{33,1},{65,33},{97,65},{34,2},{66,34},{98,6... | collective-permute-start | bytes 98312 | tf_op jit(solution)/shard_map/ppermute | solution.py:332
  3.5 3.5 %collective-permute-start = (bf16[8,1,2048]{2,1,0:T(2,128)(2,1)S(1)}, bf16[8,1,2048]{2,1,0:T(2,128)(2,1)S(1)}, u32[]{:S(2)}, u32[]{:S(2)}) collective-permute-start(bf16[8,1,2048]{2,1,0:T(2,128)(2,1)S(1)} %get-tuple-element.24), channel_id=1, source_target_pairs={{0,32},{32,64},{64,96},{1,33},{33,65},{65,97},{2,34},{34,66},{66,9... | collective-permute-start | bytes 98312 | tf_op jit(solution)/shard_map/ppermute | solution.py:331
  7.0 0.7 convert_bitcast_fusion
  7.7 0.7 convert_bitcast_fusion.1
  8.3 0.7 pad.8
  9.0 0.8 concatenate.3.facts
  9.8 1.2 %copy-done = bf16[8,32,2048]{2,1,0:T(8,128)(2,1)S(1)} copy-done((bf16[8,32,2048]{2,1,0:T(8,128)(2,1)S(1)}, bf16[8,32,2048]{2,1,0:T(8,128)(2,1)}, u32[]{:S(2)}) %copy-start) | copy-done | bytes 1048600
  11.0 3.0 %features.1 = (bf16[2,4,8,48,1024]{4,3,2,1,0:T(8,128)(2,1)S(1)}, bf16[512,48]{1,0:T(8,128)(2,1)S(1)}, bf16[32,512]{1,0:T(8,128)(2,1)S(1)}, f32[8,1024]{1,0:T(8,128)S(1)}, f32[32,128]{1,0:T(8,128)S(1)}) custom-call(bf16[8,32,2048]{2,1,0:T(8,128)(2,1)S(1)} %copy-done, f32[11,64]{1,0:T(8,128)S(1)} %concatenate.3.facts), custom_call_target="tpu_custom_call" | custom-call | tf_op jit(solution)/shard_map/features/pallas_call | solution.py:286
  14.0 8.6 %march_send_inner.1.after = f32[2,4,8,1024]{3,2,1,0:T(8,128)S(1)} custom-call(s32[1]{0:T(128)} %bitcast.where, bf16[2,4,8,48,1024]{4,3,2,1,0:T(8,128)(2,1)S(1)} %get-tuple-element.14.feats, bf16[512,48]{1,0:T(8,128)(2,1)S(1)} %get-tuple-element.15.w1, bf16[32,512]{1,0:T(8,128)(2,1)S(1)} %get-tuple-element.16.w2, f32[8,1024]{1,0:T(8,128)S(1)} %get-tuple-element.17.coverage, ...), custom_call_target="tpu_custom_call" | custom-call | tf_op jit(solution)/shard_map/march_send_inner/pallas_call | solution.py:286
  22.8 0.3 edges.1
  23.0 8.7 %march_send_outer.1 = f32[2,4,8,1024]{3,2,1,0:T(8,128)S(1)} custom-call(s32[1]{0:T(128)} %bitcast.where, bf16[2,4,8,48,1024]{4,3,2,1,0:T(8,128)(2,1)S(1)} %get-tuple-element.14.feats, bf16[2,8,48,1024]{3,2,1,0:T(8,128)(2,1)S(1)} %edges.1, bf16[512,48]{1,0:T(8,128)(2,1)S(1)} %get-tuple-element.15.w1, bf16[32,512]{1,0:T(8,128)(2,1)S(1)} %get-tuple-element.16.w2, ...), custom_call_target="tpu_custom_call" | custom-call | tf_op jit(solution)/shard_map/march_send_outer/pallas_call | solution.py:286
  31.8 0.6 collective-permute-start.3
  32.4 1.2 %collective-permute-done.3.outer = f32[2,4,8,1024]{3,2,1,0:T(8,128)S(1)} collective-permute-done((f32[2,4,8,1024]{3,2,1,0:T(8,128)S(1)}, f32[2,4,8,1024]{3,2,1,0:T(8,128)S(1)}, u32[]{:S(2)}, u32[]{:S(2)}) %collective-permute-start.3) | collective-permute-done | bytes 262176 | tf_op jit(solution)/shard_map/ppermute | solution.py:367
  33.5 4.9 %march_keep1.1 = f32[4,8,1024]{2,1,0:T(8,128)S(1)} custom-call(s32[1]{0:T(128)} %bitcast.where, s32[32]{0:T(128)S(1)} %copy-done.1, bf16[2,4,8,48,1024]{4,3,2,1,0:T(8,128)(2,1)S(1)} %get-tuple-element.14.feats, bf16[2,8,48,1024]{3,2,1,0:T(8,128)(2,1)S(1)} %edges.1, bf16[512,48]{1,0:T(8,128)(2,1)S(1)} %get-tuple-element.15.w1, ...), custom_call_target="tpu_custom_call" | custom-call | tf_op jit(solution)/shard_map/march_keep1/pallas_call | solution.py:286
  38.5 2.0 %collective-permute-start.4 = (f32[4,8,1024]{2,1,0:T(8,128)S(1)}, f32[4,8,1024]{2,1,0:T(8,128)S(1)}, u32[]{:S(2)}, u32[]{:S(2)}) collective-permute-start(f32[4,8,1024]{2,1,0:T(8,128)S(1)} %march_keep1.1), channel_id=1, source_target_pairs={{0,2},{1,3},{2,0},{3,1},{4,6},{5,7},{6,4},{7,5},{8,10},{9,11},{10,... | collective-permute-start | bytes 393224 | tf_op jit(solution)/shard_map/ppermute | solution.py:385
  40.5 4.9 %march_keep2.1 = f32[4,8,1024]{2,1,0:T(8,128)S(1)} custom-call(s32[1]{0:T(128)} %bitcast.where, s32[32]{0:T(128)S(1)} %copy-done.1, bf16[2,4,8,48,1024]{4,3,2,1,0:T(8,128)(2,1)S(1)} %get-tuple-element.14.feats, bf16[2,8,48,1024]{3,2,1,0:T(8,128)(2,1)S(1)} %edges.1, bf16[512,48]{1,0:T(8,128)(2,1)S(1)} %get-tuple-element.15.w1, ...), custom_call_target="tpu_custom_call" | custom-call | tf_op jit(solution)/shard_map/march_keep2/pallas_call | solution.py:286
  45.4 3.7 %collective-permute-start.5 = (f32[4,8,1024]{2,1,0:T(8,128)S(1)}, f32[4,8,1024]{2,1,0:T(8,128)S(1)}, u32[]{:S(2)}, u32[]{:S(2)}) collective-permute-start(f32[4,8,1024]{2,1,0:T(8,128)S(1)} %march_keep2.1), channel_id=1, source_target_pairs={{0,4},{1,5},{2,6},{3,7},{4,0},{5,1},{6,2},{7,3},{8,12},{9,13},{10,... | collective-permute-start | bytes 393224 | tf_op jit(solution)/shard_map/ppermute | solution.py:385
  49.1 4.9 %march_keep3.1 = f32[4,8,1024]{2,1,0:T(8,128)S(1)} custom-call(s32[1]{0:T(128)} %bitcast.where, s32[32]{0:T(128)S(1)} %copy-done.1, bf16[2,4,8,48,1024]{4,3,2,1,0:T(8,128)(2,1)S(1)} %get-tuple-element.14.feats, bf16[2,8,48,1024]{3,2,1,0:T(8,128)(2,1)S(1)} %edges.1, bf16[512,48]{1,0:T(8,128)(2,1)S(1)} %get-tuple-element.15.w1, ...), custom_call_target="tpu_custom_call" | custom-call | tf_op jit(solution)/shard_map/march_keep3/pallas_call | solution.py:286
  54.1 4.9 %march_keep0.1.part0 = f32[4,8,1024]{2,1,0:T(8,128)S(1)} custom-call(s32[1]{0:T(128)} %bitcast.where, s32[32]{0:T(128)S(1)} %copy-done.1, bf16[2,4,8,48,1024]{4,3,2,1,0:T(8,128)(2,1)S(1)} %get-tuple-element.14.feats, bf16[2,8,48,1024]{3,2,1,0:T(8,128)(2,1)S(1)} %edges.1, bf16[512,48]{1,0:T(8,128)(2,1)S(1)} %get-tuple-element.15.w1, ...), custom_call_target="tpu_custom_call" | custom-call | tf_op jit(solution)/shard_map/march_keep0/pallas_call | solution.py:286
  59.1 1.4 %collective-permute-done.6.part3 = f32[4,8,1024]{2,1,0:T(8,128)S(1)} collective-permute-done((f32[4,8,1024]{2,1,0:T(8,128)S(1)}, f32[4,8,1024]{2,1,0:T(8,128)S(1)}, u32[]{:S(2)}, u32[]{:S(2)}) %collective-permute-start.6) | collective-permute-done | bytes 131104 | tf_op jit(solution)/shard_map/ppermute | solution.py:385
  60.5 0.7 merge_z.1
  61.2 1.6 %collective-permute-start.7 = (f32[4,2,1024]{2,1,0:T(2,128)S(1)}, f32[4,2,1024]{2,1,0:T(2,128)S(1)}, u32[]{:S(2)}, u32[]{:S(2)}) collective-permute-start(f32[4,2,1024]{2,1,0:T(2,128)S(1)} %get-tuple-element.20), channel_id=1, source_target_pairs={{0,8},{1,9},{2,10},{3,11},{4,12},{5,13},{6,14},{7,15},{8,0},{9,1},... | collective-permute-start | bytes 98312 | tf_op jit(solution)/shard_map/ppermute | solution.py:397
  62.8 2.7 %collective-permute-start.8 = (f32[4,2,1024]{2,1,0:T(2,128)S(1)}, f32[4,2,1024]{2,1,0:T(2,128)S(1)}, u32[]{:S(2)}, u32[]{:S(2)}) collective-permute-start(f32[4,2,1024]{2,1,0:T(2,128)S(1)} %get-tuple-element.21), channel_id=1, source_target_pairs={{0,16},{1,17},{2,18},{3,19},{4,20},{5,21},{6,22},{7,23},{8,24},{9,... | collective-permute-start | bytes 98312 | tf_op jit(solution)/shard_map/ppermute | solution.py:397
  65.5 0.5 collective-permute-start.9
  66.0 2.3 %collective-permute-done.8.part2 = f32[4,2,1024]{2,1,0:T(2,128)S(1)} collective-permute-done((f32[4,2,1024]{2,1,0:T(2,128)S(1)}, f32[4,2,1024]{2,1,0:T(2,128)S(1)}, u32[]{:S(2)}, u32[]{:S(2)}) %collective-permute-start.8) | collective-permute-done | bytes 32800 | tf_op jit(solution)/shard_map/ppermute | solution.py:397
  68.3 2.3 %collective-permute-done.9.part3 = f32[4,2,1024]{2,1,0:T(2,128)S(1)} collective-permute-done((f32[4,2,1024]{2,1,0:T(2,128)S(1)}, f32[4,2,1024]{2,1,0:T(2,128)S(1)}, u32[]{:S(2)}, u32[]{:S(2)}) %collective-permute-start.9) | collective-permute-done | bytes 32800 | tf_op jit(solution)/shard_map/ppermute | solution.py:397
  70.6 0.6 merge_x.1.centre
  71.2 1.9 %collective-permute-start.11 = (f32[3,2,1024]{2,1,0:T(2,128)S(1)}, f32[3,2,1024]{2,1,0:T(2,128)S(1)}, u32[]{:S(2)}, u32[]{:S(2)}) collective-permute-start(f32[3,2,1024]{2,1,0:T(2,128)S(1)} %merge_x.1.centre), channel_id=1, source_target_pairs={{1,2},{3,4},{5,6},{7,8},{9,10},{11,12},{13,14},{15,16},{17,18},{19... | collective-permute-start | bytes 73736 | tf_op jit(solution)/shard_map/ppermute | solution.py:410
  73.2 0.1 reshape.19.weight
  73.3 7.2 %collective-permute-done.11.apart = f32[3,2,1024]{2,1,0:T(2,128)S(1)} collective-permute-done((f32[3,2,1024]{2,1,0:T(2,128)S(1)}, f32[3,2,1024]{2,1,0:T(2,128)S(1)}, u32[]{:S(2)}, u32[]{:S(2)}) %collective-permute-start.11) | collective-permute-done | bytes 24608 | tf_op jit(solution)/shard_map/ppermute | solution.py:410
  80.6 1.5 %filter.1 = f32[3,1,2048]{2,1,0:T(1,128)} custom-call(s32[1]{0:T(128)} %bitcast.where, f32[81]{0:T(128)S(1)} %reshape.19.weight, f32[3]{0:T(128)S(1)} %copy-done.2, f32[3,2,1024]{2,1,0:T(2,128)S(1)} %collective-permute-done.10.beside, f32[3,2,1024]{2,1,0:T(2,128)S(1)} %merge_x.1.centre, f32[3,2,1024]{2,1,0:T(2,128)S(1)} %collective-permute-done.11.apart), custom_call_target="tpu_custom_call" | custom-call | tf_op jit(solution)/shard_map/filter/pallas_call | solution.py:286
  (18 shorter events, 0.3 us)
Async XLA Ops:
  1.1 21.6 %collective-permute-start.1 = (bf16[8,1,2048]{2,1,0:T(2,128)(2,1)S(1)}, bf16[8,1,2048]{2,1,0:T(2,128)(2,1)S(1)}, u32[]{:S(2)}, u32[]{:S(2)}) collective-permute-start(bf16[8,1,2048]{2,1,0:T(2,128)(2,1)S(1)} %get-tuple-element.23), channel_id=1, source_target_pairs={{32,0},{64,32},{96,64},{33,1},{65,33},{97,65},{34,2},{66,34},{98,6... | collective-permute-start | bytes 98312 | tf_op jit(solution)/shard_map/ppermute | solution.py:332
  3.5 19.3 %collective-permute-start = (bf16[8,1,2048]{2,1,0:T(2,128)(2,1)S(1)}, bf16[8,1,2048]{2,1,0:T(2,128)(2,1)S(1)}, u32[]{:S(2)}, u32[]{:S(2)}) collective-permute-start(bf16[8,1,2048]{2,1,0:T(2,128)(2,1)S(1)} %get-tuple-element.24), channel_id=1, source_target_pairs={{0,32},{32,64},{64,96},{1,33},{33,65},{65,97},{2,34},{34,66},{66,9... | collective-permute-start | bytes 98312 | tf_op jit(solution)/shard_map/ppermute | solution.py:331
  9.8 1.2 %copy-start = (bf16[8,32,2048]{2,1,0:T(8,128)(2,1)S(1)}, bf16[8,32,2048]{2,1,0:T(8,128)(2,1)}, u32[]{:S(2)}) copy-start(bf16[8,32,2048]{2,1,0:T(8,128)(2,1)} %vol.1) | copy-start | bytes 3145732
  22.6 10.9 %copy-start.1 = (s32[32]{0:T(128)S(1)}, s32[32]{0:T(128)}, u32[]{:S(2)}) copy-start(s32[32]{0:T(128)} %order.11) | copy-start | bytes 388
  22.7 9.7 %collective-permute-start.2 = (f32[2,4,8,1024]{3,2,1,0:T(8,128)S(1)}, f32[2,4,8,1024]{3,2,1,0:T(8,128)S(1)}, u32[]{:S(2)}, u32[]{:S(2)}) collective-permute-start(f32[2,4,8,1024]{3,2,1,0:T(8,128)S(1)} %march_send_inner.1.after), channel_id=1, source_target_pairs={{0,1},{1,0},{2,3},{3,2},{4,5},{5,4},{6,7},{7,6},{8,9},{9,8},{10,11... | collective-permute-start | bytes 786440 | tf_op jit(solution)/shard_map/ppermute | solution.py:344
  31.8 1.7 %collective-permute-start.3 = (f32[2,4,8,1024]{3,2,1,0:T(8,128)S(1)}, f32[2,4,8,1024]{3,2,1,0:T(8,128)S(1)}, u32[]{:S(2)}, u32[]{:S(2)}) collective-permute-start(f32[2,4,8,1024]{3,2,1,0:T(8,128)S(1)} %march_send_outer.1), channel_id=1, source_target_pairs={{0,1},{1,0},{2,3},{3,2},{4,5},{5,4},{6,7},{7,6},{8,9},{9,8},{10,11... | collective-permute-start | bytes 786440 | tf_op jit(solution)/shard_map/ppermute | solution.py:367
  38.5 20.6 %collective-permute-start.4 = (f32[4,8,1024]{2,1,0:T(8,128)S(1)}, f32[4,8,1024]{2,1,0:T(8,128)S(1)}, u32[]{:S(2)}, u32[]{:S(2)}) collective-permute-start(f32[4,8,1024]{2,1,0:T(8,128)S(1)} %march_keep1.1), channel_id=1, source_target_pairs={{0,2},{1,3},{2,0},{3,1},{4,6},{5,7},{6,4},{7,5},{8,10},{9,11},{10,... | collective-permute-start | bytes 393224 | tf_op jit(solution)/shard_map/ppermute | solution.py:385
  45.4 13.7 %collective-permute-start.5 = (f32[4,8,1024]{2,1,0:T(8,128)S(1)}, f32[4,8,1024]{2,1,0:T(8,128)S(1)}, u32[]{:S(2)}, u32[]{:S(2)}) collective-permute-start(f32[4,8,1024]{2,1,0:T(8,128)S(1)} %march_keep2.1), channel_id=1, source_target_pairs={{0,4},{1,5},{2,6},{3,7},{4,0},{5,1},{6,2},{7,3},{8,12},{9,13},{10,... | collective-permute-start | bytes 393224 | tf_op jit(solution)/shard_map/ppermute | solution.py:385
  54.0 19.2 %copy-start.3 = (f32[3,3,3,3]{3,2,1,0:T(4,128)S(1)}, f32[3,3,3,3]{3,2,1,0:T(4,128)}, u32[]{:S(2)}) copy-start(f32[3,3,3,3]{3,2,1,0:T(4,128)} %param.16) | copy-start | bytes 976
  54.0 26.5 %copy-start.2 = (f32[3]{0:T(128)S(1)}, f32[3]{0:T(128)}, u32[]{:S(2)}) copy-start(f32[3]{0:T(128)} %bias.1) | copy-start | bytes 40
  54.0 6.5 %collective-permute-start.6 = (f32[4,8,1024]{2,1,0:T(8,128)S(1)}, f32[4,8,1024]{2,1,0:T(8,128)S(1)}, u32[]{:S(2)}, u32[]{:S(2)}) collective-permute-start(f32[4,8,1024]{2,1,0:T(8,128)S(1)} %march_keep3.1), channel_id=1, source_target_pairs={{0,6},{1,7},{2,4},{3,5},{4,2},{5,3},{6,0},{7,1},{8,14},{9,15},{10,... | collective-permute-start | bytes 393224 | tf_op jit(solution)/shard_map/ppermute | solution.py:385
  61.2 4.8 %collective-permute-start.7 = (f32[4,2,1024]{2,1,0:T(2,128)S(1)}, f32[4,2,1024]{2,1,0:T(2,128)S(1)}, u32[]{:S(2)}, u32[]{:S(2)}) collective-permute-start(f32[4,2,1024]{2,1,0:T(2,128)S(1)} %get-tuple-element.20), channel_id=1, source_target_pairs={{0,8},{1,9},{2,10},{3,11},{4,12},{5,13},{6,14},{7,15},{8,0},{9,1},... | collective-permute-start | bytes 98312 | tf_op jit(solution)/shard_map/ppermute | solution.py:397
  62.8 5.5 %collective-permute-start.8 = (f32[4,2,1024]{2,1,0:T(2,128)S(1)}, f32[4,2,1024]{2,1,0:T(2,128)S(1)}, u32[]{:S(2)}, u32[]{:S(2)}) collective-permute-start(f32[4,2,1024]{2,1,0:T(2,128)S(1)} %get-tuple-element.21), channel_id=1, source_target_pairs={{0,16},{1,17},{2,18},{3,19},{4,20},{5,21},{6,22},{7,23},{8,24},{9,... | collective-permute-start | bytes 98312 | tf_op jit(solution)/shard_map/ppermute | solution.py:397
  65.5 5.1 %collective-permute-start.9 = (f32[4,2,1024]{2,1,0:T(2,128)S(1)}, f32[4,2,1024]{2,1,0:T(2,128)S(1)}, u32[]{:S(2)}, u32[]{:S(2)}) collective-permute-start(f32[4,2,1024]{2,1,0:T(2,128)S(1)} %get-tuple-element.22), channel_id=1, source_target_pairs={{0,24},{1,25},{2,26},{3,27},{4,28},{5,29},{6,30},{7,31},{8,16},{9,... | collective-permute-start | bytes 98312 | tf_op jit(solution)/shard_map/ppermute | solution.py:397
  71.2 9.4 %collective-permute-start.11 = (f32[3,2,1024]{2,1,0:T(2,128)S(1)}, f32[3,2,1024]{2,1,0:T(2,128)S(1)}, u32[]{:S(2)}, u32[]{:S(2)}) collective-permute-start(f32[3,2,1024]{2,1,0:T(2,128)S(1)} %merge_x.1.centre), channel_id=1, source_target_pairs={{1,2},{3,4},{5,6},{7,8},{9,10},{11,12},{13,14},{15,16},{17,18},{19... | collective-permute-start | bytes 73736 | tf_op jit(solution)/shard_map/ppermute | solution.py:410
  73.1 7.4 %collective-permute-start.10 = (f32[3,2,1024]{2,1,0:T(2,128)S(1)}, f32[3,2,1024]{2,1,0:T(2,128)S(1)}, u32[]{:S(2)}, u32[]{:S(2)}) collective-permute-start(f32[3,2,1024]{2,1,0:T(2,128)S(1)} %merge_x.1.centre), channel_id=1, source_target_pairs={{0,1},{1,0},{2,3},{3,2},{4,5},{5,4},{6,7},{7,6},{8,9},{9,8},{10,11... | collective-permute-start | bytes 73736 | tf_op jit(solution)/shard_map/ppermute | solution.py:411

commit v3 on v2

--- a/solution.py
+++ b/solution.py
@@ -9,6 +9,8 @@
 
 HIDDEN = 64
 KDIM = 48
+CHUNK = 256
+LAG = 2
 F32 = jnp.float32
 BF16 = jnp.bfloat16
 
@@ -137,28 +139,36 @@
         x[...] = feats[parity, zpos]
 
 
-def march(plane, w1, w2, coverage, shift):
+def march(plane, w1, w2, coverage, shift, out):
     layers, _, half = plane.shape
-    cover = coverage[...]
-    lift = jnp.concatenate([shift[...]] * (half // 128), 1)
-
-    def layer(z, state):
-        x = plane[z]
-        u = jnp.dot(w1[...], x, preferred_element_type=F32)
-        hidden = (u * jnp.tanh(u) + u).astype(BF16)
-        e = jnp.dot(w2[...], hidden, preferred_element_type=F32) + lift
+    lift = jnp.concatenate([shift[...]] * (CHUNK // 128), 1)
+    steps = [(c, z) for c in range(0, half, CHUNK) for z in range(layers)]
+    waiting = []
+    states = {}
+    for n in range(len(steps) + LAG):
+        if n < len(steps):
+            c, z = steps[n]
+            u = jnp.dot(w1[...], plane[z, :, c : c + CHUNK], preferred_element_type=F32)
+            waiting.append((u * jnp.tanh(u) + u).astype(BF16))
+        if n < LAG:
+            continue
+        c, z = steps[n - LAG]
+        e = jnp.dot(w2[...], waiting[n - LAG], preferred_element_type=F32) + lift
+        waiting[n - LAG] = None
         raw = e[24:32]
         density = jnp.maximum(raw, 0.0) + jnp.log1p(jnp.exp(-jnp.abs(raw)))
-        alpha = 1.0 - jnp.exp(cover * density)
-        remaining = state[3]
-        share = remaining * alpha
-        colours = [
-            state[o] + share * (0.5 * jnp.tanh(e[8 * o : 8 * o + 8]) + 0.5) for o in range(3)
-        ]
-        return (*colours, remaining * (1.0 - alpha))
-
-    zero = jnp.zeros((8, half), F32)
-    return lax.fori_loop(0, layers, layer, (zero, zero, zero, zero + 1.0), unroll=2)
+        alpha = 1.0 - jnp.exp(coverage[:, c : c + CHUNK] * density)
+        colours = [0.5 * jnp.tanh(e[8 * o : 8 * o + 8]) + 0.5 for o in range(3)]
+        if z == 0:
+            state = [alpha * colour for colour in colours] + [1.0 - alpha]
+        else:
+            share = states[c][3] * alpha
+            state = [states[c][o] + share * colours[o] for o in range(3)]
+            state.append(states[c][3] * (1.0 - alpha))
+        states[c] = state
+        if z == layers - 1:
+            for o in range(4):
+                out[o, :, c : c + CHUNK] = states[c][o]
 
 
 def coverage_of(occ, optical, half):
@@ -177,9 +187,7 @@
     parity = 1 - (where[0] & 1)
 
     def piece(i, carry):
-        state = march(feats.at[parity, 1 + i], w1, w2, coverage, shift)
-        for o in range(4):
-            out[i, o] = state[o]
+        march(feats.at[parity, 1 + i], w1, w2, coverage, shift, out.at[i])
         return carry
 
     lax.fori_loop(0, 2, piece, 0)
@@ -190,9 +198,7 @@
 
     def piece(i, carry):
         load_plane(feats, edges, parity, 3 * i, x)
-        state = march(x, w1, w2, coverage, shift)
-        for o in range(4):
-            out[i, o] = state[o]
+        march(x, w1, w2, coverage, shift, out.at[i])
         return carry
 
     lax.fori_loop(0, 2, piece, 0)
@@ -220,7 +226,8 @@
     d = where[0]
     zpos = ((d >> 1) & 3) ^ step
     load_plane(feats, edges, d & 1, zpos, x)
-    state = march(x, w1, w2, coverage, shift)
+    march(x, w1, w2, coverage, shift, out)
+    state = tuple(out[o] for o in range(4))
     slot = zpos >> 1
     middle = (zpos == 1) | (zpos == 2)
     other = tuple(jnp.where(middle, inner[slot, o], outer[slot, o]) for o in range(4))
@@ -298,6 +305,17 @@
     return jax.ShapeDtypeStruct(dims, dtype)
 
 
+def table_of(*arrays):
+    flat = [v.astype(F32).reshape(-1, v.shape[-1]) for v in arrays]
+    rows = sum(v.shape[0] for v in flat)
+    total, at = 0.0, 0
+    for v in flat:
+        n, width = v.shape
+        total = total + jnp.pad(v, ((at, rows - at - n), (0, HIDDEN - width)))
+        at += n
+    return total
+
+
 def shards(volume, occupancy, slab_order, w_in, b_in, w_out, b_out, conv_weight, conv_bias):
     strips = lax.axis_size("strip")
     depths = lax.axis_size("depth")
@@ -306,10 +324,9 @@
     optical = 2.0 / (layers * depths)
     d = lax.axis_index("depth")
     where = d.astype(jnp.int32).reshape(1)
-    wide = lambda v: jnp.pad(v.astype(F32).reshape(1, -1), ((0, 0), (0, HIDDEN - v.size)))
-    facts = jnp.concatenate(
-        [w_in.astype(F32), wide(b_in), w_out.T.astype(F32), wide(b_out), wide(occupancy)], 0
-    )
+    facts = table_of(w_in, b_in, w_out.T, b_out, occupancy)
+    top = lax.ppermute(volume[:, rows - 1 :], "strip", [(i, i + 1) for i in range(strips - 1)])
+    bot = lax.ppermute(volume[:, :1], "strip", [(i + 1, i) for i in range(strips - 1)])
     feats, w1, w2, coverage, shift = call(
         functools.partial(feature_kernel, optical=optical),
         "features",
@@ -328,8 +345,6 @@
             pltpu.VMEM((layers, 8, 8, half), F32),
         ],
     )
-    top = lax.ppermute(volume[:, rows - 1 :], "strip", [(i, i + 1) for i in range(strips - 1)])
-    bot = lax.ppermute(volume[:, :1], "strip", [(i + 1, i) for i in range(strips - 1)])
     net = (w1, w2, coverage, shift)
     cores = [(i, i ^ 1) for i in range(depths)]
     sent = call(

time: 82.3 us -> 74.5 us (0.905)
  Pallas kernels: 43.1 us -> 35.7 us
  local copies, waits for them, and re-layouts: 3.91 us -> 2.47 us
  waiting for transfers between devices: 14.5 us -> 15.4 us
    pallas_call x11, Pallas kernels: 43.1 us -> 35.7 us  [call(): pl.pallas_call(kernel, out_shape=outs, in_specs=specs, out_specs=jax.tree...]
    ppermute x3, waiting for transfers between devices: 1.44 us -> 2.39 us  [shards(): lax.ppermute(piece, 'depth', [(i, i ^ step << 1) for i in range(depths)])]
  transfers between devices with their start and end apart: 12 -> 12, of which waited for: 5 -> 5; matrix products, arithmetic and copies ran while one was open for 4% -> 2% of each run, Pallas kernels for 43% -> 39%
where the time goes in v3:
time: 74.5 us; the launch traced here: 74.2 us
  Pallas kernels  35.7 us (48%)
  starting transfers between devices  19 us (26%)
  waiting for transfers between devices  15.4 us (21%)
  local copies, waits for them, and re-layouts  2.47 us (3%)
  other arithmetic  1.4 us (2%)
    pallas_call x11, Pallas kernels, call(): pl.pallas_call(kernel, out_shape=outs, in_specs=specs, out_specs=jax.tree...  35.7 us
    ppermute x1, waiting for transfers between devices, shards(): lax.ppermute(picture, ('strip', 'depth'), pairs + [(j, i) for i, j in pai...  7.23 us
    ppermute x3, starting transfers between devices, shards(): lax.ppermute(piece, 'depth', [(i, i ^ step << 1) for i in range(depths)])  5.75 us
    ppermute x3, starting transfers between devices, shards(): lax.ppermute(quads[k], 'depth', [(i, i ^ k << 3) for i in range(depths)])  4.78 us
    ppermute x3, waiting for transfers between devices, shards(): lax.ppermute(quads[k], 'depth', [(i, i ^ k << 3) for i in range(depths)])  4.66 us
    ppermute x1, starting transfers between devices, shards(): lax.ppermute(volume[:, rows - 1:], 'strip', [(i, i + 1) for i in range(st...  3.48 us
    ppermute x3, waiting for transfers between devices, shards(): lax.ppermute(piece, 'depth', [(i, i ^ step << 1) for i in range(depths)])  2.39 us
    ppermute x1, starting transfers between devices, shards(): lax.ppermute(volume[:, :1], 'strip', [(i + 1, i) for i in range(strips -...  2.36 us
  transfers between devices with their start and end apart: 12, of which 5 were waited for; matrix products, arithmetic and copies ran while one was open for 2% of the time, Pallas kernels for 39%

profile of v3, /device:TPU:16, one launch (start us, length us, event | category | flops | bytes accessed | tf_op | source)
XLA Modules:
  0.0 74.2 jit_solution(2113101223144735028)
XLA Ops:
  0.0 1.1 %fusion = (bf16[8,1,2048]{2,1,0:T(2,128)(2,1)S(1)}, bf16[8,1,2048]{2,1,0:T(2,128)(2,1)S(1)}) fusion(bf16[8,32,2048]{2,1,0:T(8,128)(2,1)} %vol.1), kind=kLoop, calls=%fused_computation.2 | loop fusion | bytes 131072 | tf_op jit(solution)/shard_map/slice | solution.py:329
  1.1 2.4 %collective-permute-start.1 = (bf16[8,1,2048]{2,1,0:T(2,128)(2,1)S(1)}, bf16[8,1,2048]{2,1,0:T(2,128)(2,1)S(1)}, u32[]{:S(2)}, u32[]{:S(2)}) collective-permute-start(bf16[8,1,2048]{2,1,0:T(2,128)(2,1)S(1)} %get-tuple-element.23), channel_id=1, source_target_pairs={{32,0},{64,32},{96,64},{33,1},{65,33},{97,65},{34,2},{66,34},{98,6... | collective-permute-start | bytes 98312 | tf_op jit(solution)/shard_map/ppermute | solution.py:329
  3.5 3.5 %collective-permute-start = (bf16[8,1,2048]{2,1,0:T(2,128)(2,1)S(1)}, bf16[8,1,2048]{2,1,0:T(2,128)(2,1)S(1)}, u32[]{:S(2)}, u32[]{:S(2)}) collective-permute-start(bf16[8,1,2048]{2,1,0:T(2,128)(2,1)S(1)} %get-tuple-element.24), channel_id=1, source_target_pairs={{0,32},{32,64},{64,96},{1,33},{33,65},{65,97},{2,34},{34,66},{66,9... | collective-permute-start | bytes 98312 | tf_op jit(solution)/shard_map/ppermute | solution.py:328
  7.0 0.7 convert_bitcast_fusion
  7.7 0.7 pad_add_fusion.facts
  8.4 1.2 %copy-done = bf16[8,32,2048]{2,1,0:T(8,128)(2,1)S(1)} copy-done((bf16[8,32,2048]{2,1,0:T(8,128)(2,1)S(1)}, bf16[8,32,2048]{2,1,0:T(8,128)(2,1)}, u32[]{:S(2)}) %copy-start) | copy-done | bytes 1048600
  9.6 3.0 %features.1 = (bf16[2,4,8,48,1024]{4,3,2,1,0:T(8,128)(2,1)S(1)}, bf16[512,48]{1,0:T(8,128)(2,1)S(1)}, bf16[32,512]{1,0:T(8,128)(2,1)S(1)}, f32[8,1024]{1,0:T(8,128)S(1)}, f32[32,128]{1,0:T(8,128)S(1)}) custom-call(bf16[8,32,2048]{2,1,0:T(8,128)(2,1)S(1)} %copy-done, f32[11,64]{1,0:T(8,128)S(1)} %pad_add_fusion.facts), custom_call_target="tpu_custom_call" | custom-call | tf_op jit(solution)/shard_map/features/pallas_call | solution.py:293
  12.6 6.7 %march_send_inner.1.after = f32[2,4,8,1024]{3,2,1,0:T(8,128)S(1)} custom-call(s32[1]{0:T(128)} %bitcast.where, bf16[2,4,8,48,1024]{4,3,2,1,0:T(8,128)(2,1)S(1)} %get-tuple-element.14.feats, bf16[512,48]{1,0:T(8,128)(2,1)S(1)} %get-tuple-element.15.w1, bf16[32,512]{1,0:T(8,128)(2,1)S(1)} %get-tuple-element.16.w2, f32[8,1024]{1,0:T(8,128)S(1)} %get-tuple-element.17.coverage, ...), custom_call_target="tpu_custom_call" | custom-call | tf_op jit(solution)/shard_map/march_send_inner/pallas_call | solution.py:293
  19.4 0.1 collective-permute-start.2
  19.5 0.3 edges.1
  19.8 6.9 %march_send_outer.1 = f32[2,4,8,1024]{3,2,1,0:T(8,128)S(1)} custom-call(s32[1]{0:T(128)} %bitcast.where, bf16[2,4,8,48,1024]{4,3,2,1,0:T(8,128)(2,1)S(1)} %get-tuple-element.14.feats, bf16[2,8,48,1024]{3,2,1,0:T(8,128)(2,1)S(1)} %edges.1, bf16[512,48]{1,0:T(8,128)(2,1)S(1)} %get-tuple-element.15.w1, bf16[32,512]{1,0:T(8,128)(2,1)S(1)} %get-tuple-element.16.w2, ...), custom_call_target="tpu_custom_call" | custom-call | tf_op jit(solution)/shard_map/march_send_outer/pallas_call | solution.py:293
  26.6 0.6 collective-permute-start.3
  27.2 1.2 %collective-permute-done.3.outer = f32[2,4,8,1024]{3,2,1,0:T(8,128)S(1)} collective-permute-done((f32[2,4,8,1024]{3,2,1,0:T(8,128)S(1)}, f32[2,4,8,1024]{3,2,1,0:T(8,128)S(1)}, u32[]{:S(2)}, u32[]{:S(2)}) %collective-permute-start.3) | collective-permute-done | bytes 262176 | tf_op jit(solution)/shard_map/ppermute | solution.py:382
  28.4 4.0 %march_keep1.1 = f32[4,8,1024]{2,1,0:T(8,128)S(1)} custom-call(s32[1]{0:T(128)} %bitcast.where, s32[32]{0:T(128)S(1)} %copy-done.1, bf16[2,4,8,48,1024]{4,3,2,1,0:T(8,128)(2,1)S(1)} %get-tuple-element.14.feats, bf16[2,8,48,1024]{3,2,1,0:T(8,128)(2,1)S(1)} %edges.1, bf16[512,48]{1,0:T(8,128)(2,1)S(1)} %get-tuple-element.15.w1, ...), custom_call_target="tpu_custom_call" | custom-call | tf_op jit(solution)/shard_map/march_keep1/pallas_call | solution.py:293
  32.4 2.0 %collective-permute-start.4 = (f32[4,8,1024]{2,1,0:T(8,128)S(1)}, f32[4,8,1024]{2,1,0:T(8,128)S(1)}, u32[]{:S(2)}, u32[]{:S(2)}) collective-permute-start(f32[4,8,1024]{2,1,0:T(8,128)S(1)} %march_keep1.1), channel_id=1, source_target_pairs={{0,2},{1,3},{2,0},{3,1},{4,6},{5,7},{6,4},{7,5},{8,10},{9,11},{10,... | collective-permute-start | bytes 393224 | tf_op jit(solution)/shard_map/ppermute | solution.py:400
  34.4 4.2 %march_keep2.1 = f32[4,8,1024]{2,1,0:T(8,128)S(1)} custom-call(s32[1]{0:T(128)} %bitcast.where, s32[32]{0:T(128)S(1)} %copy-done.1, bf16[2,4,8,48,1024]{4,3,2,1,0:T(8,128)(2,1)S(1)} %get-tuple-element.14.feats, bf16[2,8,48,1024]{3,2,1,0:T(8,128)(2,1)S(1)} %edges.1, bf16[512,48]{1,0:T(8,128)(2,1)S(1)} %get-tuple-element.15.w1, ...), custom_call_target="tpu_custom_call" | custom-call | tf_op jit(solution)/shard_map/march_keep2/pallas_call | solution.py:293
  38.5 3.7 %collective-permute-start.5 = (f32[4,8,1024]{2,1,0:T(8,128)S(1)}, f32[4,8,1024]{2,1,0:T(8,128)S(1)}, u32[]{:S(2)}, u32[]{:S(2)}) collective-permute-start(f32[4,8,1024]{2,1,0:T(8,128)S(1)} %march_keep2.1), channel_id=1, source_target_pairs={{0,4},{1,5},{2,6},{3,7},{4,0},{5,1},{6,2},{7,3},{8,12},{9,13},{10,... | collective-permute-start | bytes 393224 | tf_op jit(solution)/shard_map/ppermute | solution.py:400
  42.2 4.0 %march_keep3.1 = f32[4,8,1024]{2,1,0:T(8,128)S(1)} custom-call(s32[1]{0:T(128)} %bitcast.where, s32[32]{0:T(128)S(1)} %copy-done.1, bf16[2,4,8,48,1024]{4,3,2,1,0:T(8,128)(2,1)S(1)} %get-tuple-element.14.feats, bf16[2,8,48,1024]{3,2,1,0:T(8,128)(2,1)S(1)} %edges.1, bf16[512,48]{1,0:T(8,128)(2,1)S(1)} %get-tuple-element.15.w1, ...), custom_call_target="tpu_custom_call" | custom-call | tf_op jit(solution)/shard_map/march_keep3/pallas_call | solution.py:293
  46.2 0.1 collective-permute-start.6
  46.3 4.0 %march_keep0.1.part0 = f32[4,8,1024]{2,1,0:T(8,128)S(1)} custom-call(s32[1]{0:T(128)} %bitcast.where, s32[32]{0:T(128)S(1)} %copy-done.1, bf16[2,4,8,48,1024]{4,3,2,1,0:T(8,128)(2,1)S(1)} %get-tuple-element.14.feats, bf16[2,8,48,1024]{3,2,1,0:T(8,128)(2,1)S(1)} %edges.1, bf16[512,48]{1,0:T(8,128)(2,1)S(1)} %get-tuple-element.15.w1, ...), custom_call_target="tpu_custom_call" | custom-call | tf_op jit(solution)/shard_map/march_keep0/pallas_call | solution.py:293
  50.3 2.4 %collective-permute-done.6.part3 = f32[4,8,1024]{2,1,0:T(8,128)S(1)} collective-permute-done((f32[4,8,1024]{2,1,0:T(8,128)S(1)}, f32[4,8,1024]{2,1,0:T(8,128)S(1)}, u32[]{:S(2)}, u32[]{:S(2)}) %collective-permute-start.6) | collective-permute-done | bytes 131104 | tf_op jit(solution)/shard_map/ppermute | solution.py:400
  52.7 0.7 merge_z.1
  53.4 1.6 %collective-permute-start.7 = (f32[4,2,1024]{2,1,0:T(2,128)S(1)}, f32[4,2,1024]{2,1,0:T(2,128)S(1)}, u32[]{:S(2)}, u32[]{:S(2)}) collective-permute-start(f32[4,2,1024]{2,1,0:T(2,128)S(1)} %get-tuple-element.20), channel_id=1, source_target_pairs={{0,8},{1,9},{2,10},{3,11},{4,12},{5,13},{6,14},{7,15},{8,0},{9,1},... | collective-permute-start | bytes 98312 | tf_op jit(solution)/shard_map/ppermute | solution.py:412
  55.0 2.7 %collective-permute-start.8 = (f32[4,2,1024]{2,1,0:T(2,128)S(1)}, f32[4,2,1024]{2,1,0:T(2,128)S(1)}, u32[]{:S(2)}, u32[]{:S(2)}) collective-permute-start(f32[4,2,1024]{2,1,0:T(2,128)S(1)} %get-tuple-element.21), channel_id=1, source_target_pairs={{0,16},{1,17},{2,18},{3,19},{4,20},{5,21},{6,22},{7,23},{8,24},{9,... | collective-permute-start | bytes 98312 | tf_op jit(solution)/shard_map/ppermute | solution.py:412
  57.7 0.5 collective-permute-start.9
  58.2 2.3 %collective-permute-done.8.part2 = f32[4,2,1024]{2,1,0:T(2,128)S(1)} collective-permute-done((f32[4,2,1024]{2,1,0:T(2,128)S(1)}, f32[4,2,1024]{2,1,0:T(2,128)S(1)}, u32[]{:S(2)}, u32[]{:S(2)}) %collective-permute-start.8) | collective-permute-done | bytes 32800 | tf_op jit(solution)/shard_map/ppermute | solution.py:412
  60.5 2.3 %collective-permute-done.9.part3 = f32[4,2,1024]{2,1,0:T(2,128)S(1)} collective-permute-done((f32[4,2,1024]{2,1,0:T(2,128)S(1)}, f32[4,2,1024]{2,1,0:T(2,128)S(1)}, u32[]{:S(2)}, u32[]{:S(2)}) %collective-permute-start.9) | collective-permute-done | bytes 32800 | tf_op jit(solution)/shard_map/ppermute | solution.py:412
  62.8 0.6 merge_x.1.centre
  63.4 1.9 %collective-permute-start.11 = (f32[3,2,1024]{2,1,0:T(2,128)S(1)}, f32[3,2,1024]{2,1,0:T(2,128)S(1)}, u32[]{:S(2)}, u32[]{:S(2)}) collective-permute-start(f32[3,2,1024]{2,1,0:T(2,128)S(1)} %merge_x.1.centre), channel_id=1, source_target_pairs={{1,2},{3,4},{5,6},{7,8},{9,10},{11,12},{13,14},{15,16},{17,18},{19... | collective-permute-start | bytes 73736 | tf_op jit(solution)/shard_map/ppermute | solution.py:425
  65.4 0.1 reshape.19.weight
  65.5 7.2 %collective-permute-done.11.apart = f32[3,2,1024]{2,1,0:T(2,128)S(1)} collective-permute-done((f32[3,2,1024]{2,1,0:T(2,128)S(1)}, f32[3,2,1024]{2,1,0:T(2,128)S(1)}, u32[]{:S(2)}, u32[]{:S(2)}) %collective-permute-start.11) | collective-permute-done | bytes 24608 | tf_op jit(solution)/shard_map/ppermute | solution.py:425
  72.8 1.5 %filter.1 = f32[3,1,2048]{2,1,0:T(1,128)} custom-call(s32[1]{0:T(128)} %bitcast.where, f32[81]{0:T(128)S(1)} %reshape.19.weight, f32[3]{0:T(128)S(1)} %copy-done.2, f32[3,2,1024]{2,1,0:T(2,128)S(1)} %collective-permute-done.10.beside, f32[3,2,1024]{2,1,0:T(2,128)S(1)} %merge_x.1.centre, f32[3,2,1024]{2,1,0:T(2,128)S(1)} %collective-permute-done.11.apart), custom_call_target="tpu_custom_call" | custom-call | tf_op jit(solution)/shard_map/filter/pallas_call | solution.py:293
  (15 shorter events, 0.1 us)
Async XLA Ops:
  1.1 18.3 %collective-permute-start.1 = (bf16[8,1,2048]{2,1,0:T(2,128)(2,1)S(1)}, bf16[8,1,2048]{2,1,0:T(2,128)(2,1)S(1)}, u32[]{:S(2)}, u32[]{:S(2)}) collective-permute-start(bf16[8,1,2048]{2,1,0:T(2,128)(2,1)S(1)} %get-tuple-element.23), channel_id=1, source_target_pairs={{32,0},{64,32},{96,64},{33,1},{65,33},{97,65},{34,2},{66,34},{98,6... | collective-permute-start | bytes 98312 | tf_op jit(solution)/shard_map/ppermute | solution.py:329
  3.5 16.0 %collective-permute-start = (bf16[8,1,2048]{2,1,0:T(2,128)(2,1)S(1)}, bf16[8,1,2048]{2,1,0:T(2,128)(2,1)S(1)}, u32[]{:S(2)}, u32[]{:S(2)}) collective-permute-start(bf16[8,1,2048]{2,1,0:T(2,128)(2,1)S(1)} %get-tuple-element.24), channel_id=1, source_target_pairs={{0,32},{32,64},{64,96},{1,33},{33,65},{65,97},{2,34},{34,66},{66,9... | collective-permute-start | bytes 98312 | tf_op jit(solution)/shard_map/ppermute | solution.py:328
  8.4 1.2 %copy-start = (bf16[8,32,2048]{2,1,0:T(8,128)(2,1)S(1)}, bf16[8,32,2048]{2,1,0:T(8,128)(2,1)}, u32[]{:S(2)}) copy-start(bf16[8,32,2048]{2,1,0:T(8,128)(2,1)} %vol.1) | copy-start | bytes 3145732
  19.4 9.0 %copy-start.1 = (s32[32]{0:T(128)S(1)}, s32[32]{0:T(128)}, u32[]{:S(2)}) copy-start(s32[32]{0:T(128)} %order.11) | copy-start | bytes 388
  19.4 7.8 %collective-permute-start.2 = (f32[2,4,8,1024]{3,2,1,0:T(8,128)S(1)}, f32[2,4,8,1024]{3,2,1,0:T(8,128)S(1)}, u32[]{:S(2)}, u32[]{:S(2)}) collective-permute-start(f32[2,4,8,1024]{3,2,1,0:T(8,128)S(1)} %march_send_inner.1.after), channel_id=1, source_target_pairs={{0,1},{1,0},{2,3},{3,2},{4,5},{5,4},{6,7},{7,6},{8,9},{9,8},{10,11... | collective-permute-start | bytes 786440 | tf_op jit(solution)/shard_map/ppermute | solution.py:359
  26.6 1.7 %collective-permute-start.3 = (f32[2,4,8,1024]{3,2,1,0:T(8,128)S(1)}, f32[2,4,8,1024]{3,2,1,0:T(8,128)S(1)}, u32[]{:S(2)}, u32[]{:S(2)}) collective-permute-start(f32[2,4,8,1024]{3,2,1,0:T(8,128)S(1)} %march_send_outer.1), channel_id=1, source_target_pairs={{0,1},{1,0},{2,3},{3,2},{4,5},{5,4},{6,7},{7,6},{8,9},{9,8},{10,11... | collective-permute-start | bytes 786440 | tf_op jit(solution)/shard_map/ppermute | solution.py:382
  32.4 17.9 %collective-permute-start.4 = (f32[4,8,1024]{2,1,0:T(8,128)S(1)}, f32[4,8,1024]{2,1,0:T(8,128)S(1)}, u32[]{:S(2)}, u32[]{:S(2)}) collective-permute-start(f32[4,8,1024]{2,1,0:T(8,128)S(1)} %march_keep1.1), channel_id=1, source_target_pairs={{0,2},{1,3},{2,0},{3,1},{4,6},{5,7},{6,4},{7,5},{8,10},{9,11},{10,... | collective-permute-start | bytes 393224 | tf_op jit(solution)/shard_map/ppermute | solution.py:400
  38.5 11.8 %collective-permute-start.5 = (f32[4,8,1024]{2,1,0:T(8,128)S(1)}, f32[4,8,1024]{2,1,0:T(8,128)S(1)}, u32[]{:S(2)}, u32[]{:S(2)}) collective-permute-start(f32[4,8,1024]{2,1,0:T(8,128)S(1)} %march_keep2.1), channel_id=1, source_target_pairs={{0,4},{1,5},{2,6},{3,7},{4,0},{5,1},{6,2},{7,3},{8,12},{9,13},{10,... | collective-permute-start | bytes 393224 | tf_op jit(solution)/shard_map/ppermute | solution.py:400
  46.2 19.2 %copy-start.3 = (f32[3,3,3,3]{3,2,1,0:T(4,128)S(1)}, f32[3,3,3,3]{3,2,1,0:T(4,128)}, u32[]{:S(2)}) copy-start(f32[3,3,3,3]{3,2,1,0:T(4,128)} %param.16) | copy-start | bytes 976
  46.2 26.6 %copy-start.2 = (f32[3]{0:T(128)S(1)}, f32[3]{0:T(128)}, u32[]{:S(2)}) copy-start(f32[3]{0:T(128)} %bias.1) | copy-start | bytes 40
  46.2 6.5 %collective-permute-start.6 = (f32[4,8,1024]{2,1,0:T(8,128)S(1)}, f32[4,8,1024]{2,1,0:T(8,128)S(1)}, u32[]{:S(2)}, u32[]{:S(2)}) collective-permute-start(f32[4,8,1024]{2,1,0:T(8,128)S(1)} %march_keep3.1), channel_id=1, source_target_pairs={{0,6},{1,7},{2,4},{3,5},{4,2},{5,3},{6,0},{7,1},{8,14},{9,15},{10,... | collective-permute-start | bytes 393224 | tf_op jit(solution)/shard_map/ppermute | solution.py:400
  53.4 4.8 %collective-permute-start.7 = (f32[4,2,1024]{2,1,0:T(2,128)S(1)}, f32[4,2,1024]{2,1,0:T(2,128)S(1)}, u32[]{:S(2)}, u32[]{:S(2)}) collective-permute-start(f32[4,2,1024]{2,1,0:T(2,128)S(1)} %get-tuple-element.20), channel_id=1, source_target_pairs={{0,8},{1,9},{2,10},{3,11},{4,12},{5,13},{6,14},{7,15},{8,0},{9,1},... | collective-permute-start | bytes 98312 | tf_op jit(solution)/shard_map/ppermute | solution.py:412
  55.0 5.5 %collective-permute-start.8 = (f32[4,2,1024]{2,1,0:T(2,128)S(1)}, f32[4,2,1024]{2,1,0:T(2,128)S(1)}, u32[]{:S(2)}, u32[]{:S(2)}) collective-permute-start(f32[4,2,1024]{2,1,0:T(2,128)S(1)} %get-tuple-element.21), channel_id=1, source_target_pairs={{0,16},{1,17},{2,18},{3,19},{4,20},{5,21},{6,22},{7,23},{8,24},{9,... | collective-permute-start | bytes 98312 | tf_op jit(solution)/shard_map/ppermute | solution.py:412
  57.7 5.1 %collective-permute-start.9 = (f32[4,2,1024]{2,1,0:T(2,128)S(1)}, f32[4,2,1024]{2,1,0:T(2,128)S(1)}, u32[]{:S(2)}, u32[]{:S(2)}) collective-permute-start(f32[4,2,1024]{2,1,0:T(2,128)S(1)} %get-tuple-element.22), channel_id=1, source_target_pairs={{0,24},{1,25},{2,26},{3,27},{4,28},{5,29},{6,30},{7,31},{8,16},{9,... | collective-permute-start | bytes 98312 | tf_op jit(solution)/shard_map/ppermute | solution.py:412
  63.4 9.4 %collective-permute-start.11 = (f32[3,2,1024]{2,1,0:T(2,128)S(1)}, f32[3,2,1024]{2,1,0:T(2,128)S(1)}, u32[]{:S(2)}, u32[]{:S(2)}) collective-permute-start(f32[3,2,1024]{2,1,0:T(2,128)S(1)} %merge_x.1.centre), channel_id=1, source_target_pairs={{1,2},{3,4},{5,6},{7,8},{9,10},{11,12},{13,14},{15,16},{17,18},{19... | collective-permute-start | bytes 73736 | tf_op jit(solution)/shard_map/ppermute | solution.py:425
  65.3 7.4 %collective-permute-start.10 = (f32[3,2,1024]{2,1,0:T(2,128)S(1)}, f32[3,2,1024]{2,1,0:T(2,128)S(1)}, u32[]{:S(2)}, u32[]{:S(2)}) collective-permute-start(f32[3,2,1024]{2,1,0:T(2,128)S(1)} %merge_x.1.centre), channel_id=1, source_target_pairs={{0,1},{1,0},{2,3},{3,2},{4,5},{5,4},{6,7},{7,6},{8,9},{9,8},{10,11... | collective-permute-start | bytes 73736 | tf_op jit(solution)/shard_map/ppermute | solution.py:426

commit v4 on v3

--- a/solution.py
+++ b/solution.py
@@ -9,8 +9,11 @@
 
 HIDDEN = 64
 KDIM = 48
-CHUNK = 256
-LAG = 2
+CHUNK = 512
+LAG = 1
+SPLIT = 2
+FIRST = 2
+ORDER = (2, 1, 3, 0)
 F32 = jnp.float32
 BF16 = jnp.bfloat16
 
@@ -145,15 +148,22 @@
     steps = [(c, z) for c in range(0, half, CHUNK) for z in range(layers)]
     waiting = []
     states = {}
+    part = HIDDEN * 8 // SPLIT
     for n in range(len(steps) + LAG):
-        if n < len(steps):
-            c, z = steps[n]
-            u = jnp.dot(w1[...], plane[z, :, c : c + CHUNK], preferred_element_type=F32)
-            waiting.append((u * jnp.tanh(u) + u).astype(BF16))
+        e = lift
+        fresh = []
+        for p in range(SPLIT):
+            k = slice(p * part, (p + 1) * part)
+            if n < len(steps):
+                c, z = steps[n]
+                u = jnp.dot(w1[k], plane[z, :, c : c + CHUNK], preferred_element_type=F32)
+                fresh.append((u * jnp.tanh(u) + u).astype(BF16))
+            if n >= LAG:
+                e = e + jnp.dot(w2[:, k], waiting[n - LAG][p], preferred_element_type=F32)
+        waiting.append(fresh)
         if n < LAG:
             continue
         c, z = steps[n - LAG]
-        e = jnp.dot(w2[...], waiting[n - LAG], preferred_element_type=F32) + lift
         waiting[n - LAG] = None
         raw = e[24:32]
         density = jnp.maximum(raw, 0.0) + jnp.log1p(jnp.exp(-jnp.abs(raw)))
@@ -220,42 +230,70 @@
     return (*colours, total)
 
 
+def first_kernel(where, feats, edges, w1, w2, coverage, shift, out, x):
+    d = where[0]
+    load_plane(feats, edges, d & 1, ((d >> 1) & 3) ^ FIRST, x)
+    march(x, w1, w2, coverage, shift, out)
+
+
+def merge_cores(d, order, zpos, state, inner, outer):
+    slot = zpos >> 1
+    middle = (zpos == 1) | (zpos == 2)
+    other = tuple(jnp.where(middle, inner[slot, o], outer[slot, o]) for o in range(4))
+    return over((state, other), (order[d] & 1, order[d ^ 1] & 1))
+
+
+def first_merge_kernel(where, order, raw, inner, outer, out):
+    d = where[0]
+    state = tuple(raw[o] for o in range(4))
+    merged = merge_cores(d, order, ((d >> 1) & 3) ^ FIRST, state, inner, outer)
+    for o in range(4):
+        out[o] = merged[o]
+
+
 def keep_kernel(
-    where, order, feats, edges, w1, w2, coverage, shift, inner, outer, out, x, *, step
+    where, order, feats, edges, w1, w2, coverage, shift, inner, outer, after, out, x, *, step
 ):
     d = where[0]
     zpos = ((d >> 1) & 3) ^ step
     load_plane(feats, edges, d & 1, zpos, x)
     march(x, w1, w2, coverage, shift, out)
     state = tuple(out[o] for o in range(4))
-    slot = zpos >> 1
-    middle = (zpos == 1) | (zpos == 2)
-    other = tuple(jnp.where(middle, inner[slot, o], outer[slot, o]) for o in range(4))
-    merged = over((state, other), (order[d] & 1, order[d ^ 1] & 1))
+    merged = merge_cores(d, order, zpos, state, inner, outer)
     for o in range(4):
         out[o] = merged[o]
 
 
-def merge_z_kernel(where, order, part0, part1, part2, part3, out0, out1, out2, out3):
+def merge_z_kernel(where, order, part0, part1, part2, part3, out):
     d = where[0]
     parts = [tuple(p[o] for o in range(4)) for p in (part0, part1, part2, part3)]
     places = [(order[d ^ (k << 1)] >> 1) & 3 for k in range(4)]
     merged = over(parts, places)
-    xpos = d >> 3
-    for k, out in enumerate((out0, out1, out2, out3)):
-        shift = (8 - (xpos ^ k)) % 8
-        for o in range(4):
-            turned = pltpu.roll(merged[o], shift, 0)
-            out[o] = jnp.concatenate([turned[0:1], turned[4:5]], 0)
-
-
-def merge_x_kernel(where, order, part0, part1, part2, part3, out):
+    odd = (d & 1) == 1
+    for o in range(4):
+        rows = [merged[o][k : k + 1] for k in range(8)]
+        for t in range(4):
+            before, after = (t - 1) % 4, (t + 1) % 4
+            out[t, o] = jnp.concatenate(
+                [
+                    rows[t],
+                    rows[4 + t],
+                    jnp.where(odd, rows[before], rows[after]),
+                    jnp.where(odd, rows[4 + before], rows[4 + after]),
+                ],
+                0,
+            )
+
+
+def merge_x_kernel(where, order, parts, centre, extra):
     d = where[0]
-    parts = [tuple(p[o] for o in range(4)) for p in (part0, part1, part2, part3)]
-    places = [order[d ^ (k << 3)] >> 3 for k in range(4)]
-    merged = over(parts, places)
+    group = [tuple(parts[k, o] for o in range(4)) for k in range(4)]
+    places = [order[(d & 7) | (k << 3)] >> 3 for k in range(4)]
+    merged = over(group, places)
+    boundary = ((d & 7) == 0) | ((d & 7) == 7)
     for o in range(3):
-        out[o] = merged[o]
+        centre[o] = merged[o][0:2]
+        extra[o] = jnp.where(boundary, merged[o][2:4], merged[o][0:2])
 
 
 def filter_kernel(where, weight, bias, beside, centre, apart, out):
@@ -289,7 +327,7 @@
 SMEM = pl.BlockSpec(memory_space=pltpu.SMEM)
 
 
-def call(kernel, name, outs, specs, *args, scratch=()):
+def call(kernel, name, outs, specs, *args, scratch=(), micros=1.0):
     return pl.pallas_call(
         kernel,
         out_shape=outs,
@@ -298,6 +336,9 @@
         scratch_shapes=scratch,
         compiler_params=pltpu.CompilerParams(vmem_limit_bytes=24 * 2**20),
         name=name,
+        cost_estimate=pl.CostEstimate(
+            flops=int(micros * 1e9), bytes_accessed=0, transcendentals=0
+        ),
     )(*args)
 
 
@@ -305,8 +346,24 @@
     return jax.ShapeDtypeStruct(dims, dtype)
 
 
+def across_pairs(strips, depths):
+    pairs = []
+    for y in range(strips):
+        for d in range(depths):
+            x, low, target = d >> 3, d & 7, None
+            if low == 7:
+                target = (y, 8 * x) if x > 0 else (y + 1, 0)
+            elif low == 0:
+                target = (y, 8 * x + 7) if x < depths // 8 - 1 else (y - 1, d + 7)
+            else:
+                target = (y, d + 1 if d % 2 else d - 1)
+            if 0 <= target[0] < strips:
+                pairs.append((y * depths + d, target[0] * depths + target[1]))
+    return pairs
+
+
 def table_of(*arrays):
-    flat = [v.astype(F32).reshape(-1, v.shape[-1]) for v in arrays]
+    flat = [v.reshape(-1, v.shape[-1]).astype(F32) for v in arrays]
     rows = sum(v.shape[0] for v in flat)
     total, at = 0.0, 0
     for v in flat:
@@ -355,6 +412,7 @@
         where,
         feats,
         *net,
+        micros=6.7,
     )
     inner = lax.ppermute(sent, "depth", cores)
     edges = call(
@@ -378,51 +436,83 @@
         edges,
         *net,
         scratch=[plane],
+        micros=6.8,
     )
     outer = lax.ppermute(sent, "depth", cores)
+    raw = call(
+        first_kernel,
+        "march_first",
+        shape((4, 8, half)),
+        [SMEM] + [VMEM] * 6,
+        where,
+        feats,
+        edges,
+        *net,
+        scratch=[plane],
+        micros=4.0,
+    )
     parts = [None] * 4
-    for step in (1, 2, 3, 0):
-        piece = call(
-            functools.partial(keep_kernel, step=step),
-            f"march_keep{step}",
-            shape((4, 8, half)),
-            [SMEM, SMEM] + [VMEM] * 8,
-            where,
-            slab_order,
-            feats,
-            edges,
-            *net,
-            inner,
-            outer,
-            scratch=[plane],
-        )
+    for step in ORDER:
+        if step == FIRST:
+            piece = call(
+                first_merge_kernel,
+                "merge_first",
+                shape((4, 8, half)),
+                [SMEM, SMEM] + [VMEM] * 3,
+                where,
+                slab_order,
+                raw,
+                inner,
+                outer,
+            )
+        else:
+            piece = call(
+                functools.partial(keep_kernel, step=step),
+                f"march_keep{step}",
+                shape((4, 8, half)),
+                [SMEM, SMEM] + [VMEM] * 8 + [pl.BlockSpec(memory_space=pl.ANY)],
+                where,
+                slab_order,
+                feats,
+                edges,
+                *net,
+                inner,
+                outer,
+                earlier,
+                scratch=[plane],
+                micros=4.0,
+            )
+        earlier = piece
         if step:
             piece = lax.ppermute(piece, "depth", [(i, i ^ (step << 1)) for i in range(depths)])
         parts[step] = piece
-    quads = call(
+    rows_out = call(
         merge_z_kernel,
         "merge_z",
-        tuple(shape((4, 2, half)) for _ in range(4)),
+        shape((4, 4, 4, half)),
         [SMEM, SMEM] + [VMEM] * 4,
         where,
         slab_order,
         *parts,
     )
-    quads = [
-        lax.ppermute(quads[k], "depth", [(i, i ^ (k << 3)) for i in range(depths)]) if k else quads[0]
-        for k in range(4)
-    ]
-    picture = call(
+    rows_in = lax.all_to_all(
+        rows_out,
+        "depth",
+        0,
+        0,
+        tiled=True,
+        axis_index_groups=[[i | (k << 3) for k in range(4)] for i in range(8)],
+    )
+    picture, extra = call(
         merge_x_kernel,
         "merge_x",
-        shape((3, 2, half)),
-        [SMEM, SMEM] + [VMEM] * 4,
+        (shape((3, 2, half)), shape((3, 2, half))),
+        [SMEM, SMEM, VMEM],
         where,
         slab_order,
-        *quads,
-    )
-    pairs = [(i, i + 1) for i in range(1, strips * depths - 1, 2)]
-    apart = lax.ppermute(picture, ("strip", "depth"), pairs + [(j, i) for i, j in pairs])
+        rows_in,
+    )
+    apart = lax.ppermute(extra, ("strip", "depth"), across_pairs(strips, depths))
     beside = lax.ppermute(picture, "depth", cores)
     filtered = call(
         filter_kernel,

time: 74.5 us -> 68.1 us (0.914)
  blocking collectives: 0 us -> 10.8 us
  waiting for transfers between devices: 15.4 us -> 7.82 us
  starting transfers between devices: 19 us -> 13.6 us
  Pallas kernels: 35.7 us -> 31.5 us
    all_to_all x0 -> x1, blocking collectives: none -> 10.8 us  [shards(): lax.all_to_all(rows_out, 'depth', 0, 0, tiled=True, axis_index_groups=[[i...]
    ppermute x4 -> x1, waiting for transfers between devices: 11.9 us -> 5.12 us  [shards(): lax.ppermute(extra, ('strip', 'depth'), across_pairs(strips, depths))]
    ppermute x4 -> x1, starting transfers between devices: 6.7 us -> 1.92 us  [shards(): lax.ppermute(extra, ('strip', 'depth'), across_pairs(strips, depths))]
    pallas_call x11 -> x12, Pallas kernels: 35.7 us -> 31.5 us  [call(): pl.pallas_call(kernel, out_shape=outs, in_specs=specs, out_specs=jax.tree...]
    ppermute x1, waiting for transfers between devices: 1.16 us -> 0.01 us  [shards(): outer = lax.ppermute(sent, 'depth', cores)]
  transfers between devices with their start and end apart: 12 -> 9, of which waited for: 5 -> 2; matrix products, arithmetic and copies ran while one was open for 2% -> 2% of each run, Pallas kernels for 39% -> 42%
where the time goes in v4:
time: 68.1 us; the launch traced here: 67.8 us
  Pallas kernels  31.5 us (46%)
  starting transfers between devices  13.6 us (20%)
  blocking collectives  10.8 us (16%)
  waiting for transfers between devices  7.82 us (11%)
  local copies, waits for them, and re-layouts  2.47 us (4%)
  other arithmetic  1.4 us (2%)
    pallas_call x12, Pallas kernels, call(): pl.pallas_call(kernel, out_shape=outs, in_specs=specs, out_specs=jax.tree...  31.5 us
    all_to_all x1, blocking collectives, shards(): lax.all_to_all(rows_out, 'depth', 0, 0, tiled=True, axis_index_groups=[[i...  10.8 us
    ppermute x3, starting transfers between devices, shards(): lax.ppermute(piece, 'depth', [(i, i ^ step << 1) for i in range(depths)])  5.14 us
    ppermute x1, waiting for transfers between devices, shards(): lax.ppermute(extra, ('strip', 'depth'), across_pairs(strips, depths))  5.12 us
    ppermute x1, starting transfers between devices, shards(): lax.ppermute(volume[:, rows - 1:], 'strip', [(i, i + 1) for i in range(st...  3.48 us
    ppermute x3, waiting for transfers between devices, shards(): lax.ppermute(piece, 'depth', [(i, i ^ step << 1) for i in range(depths)])  2.68 us
    ppermute x1, starting transfers between devices, shards(): lax.ppermute(volume[:, :1], 'strip', [(i + 1, i) for i in range(strips -...  2.36 us
    ppermute x1, starting transfers between devices, shards(): lax.ppermute(extra, ('strip', 'depth'), across_pairs(strips, depths))  1.92 us
  transfers between devices with their start and end apart: 9, of which 2 were waited for; matrix products, arithmetic and copies ran while one was open for 2% of the time, Pallas kernels for 42%

profile of v4, /device:TPU:16, one launch (start us, length us, event | category | flops | bytes accessed | tf_op | source)
XLA Modules:
  0.0 67.8 jit_solution(18344628867844607442)
XLA Ops:
  0.0 1.1 %fusion = (bf16[8,1,2048]{2,1,0:T(2,128)(2,1)S(1)}, bf16[8,1,2048]{2,1,0:T(2,128)(2,1)S(1)}) fusion(bf16[8,32,2048]{2,1,0:T(8,128)(2,1)} %vol.1), kind=kLoop, calls=%fused_computation.2 | loop fusion | bytes 131072 | tf_op jit(solution)/shard_map/slice | solution.py:386
  1.1 2.4 %collective-permute-start.1 = (bf16[8,1,2048]{2,1,0:T(2,128)(2,1)S(1)}, bf16[8,1,2048]{2,1,0:T(2,128)(2,1)S(1)}, u32[]{:S(2)}, u32[]{:S(2)}) collective-permute-start(bf16[8,1,2048]{2,1,0:T(2,128)(2,1)S(1)} %get-tuple-element.19), channel_id=1, source_target_pairs={{32,0},{64,32},{96,64},{33,1},{65,33},{97,65},{34,2},{66,34},{98,6... | collective-permute-start | bytes 98312 | tf_op jit(solution)/shard_map/ppermute | solution.py:386
  3.5 3.5 %collective-permute-start = (bf16[8,1,2048]{2,1,0:T(2,128)(2,1)S(1)}, bf16[8,1,2048]{2,1,0:T(2,128)(2,1)S(1)}, u32[]{:S(2)}, u32[]{:S(2)}) collective-permute-start(bf16[8,1,2048]{2,1,0:T(2,128)(2,1)S(1)} %get-tuple-element.20), channel_id=1, source_target_pairs={{0,32},{32,64},{64,96},{1,33},{33,65},{65,97},{2,34},{34,66},{66,9... | collective-permute-start | bytes 98312 | tf_op jit(solution)/shard_map/ppermute | solution.py:385
  7.0 0.7 convert_bitcast_fusion
  7.7 0.7 %pad_add_fusion.facts = f32[11,64]{1,0:T(8,128)S(1)} fusion(f32[1,16]{1,0:T(1,128)S(1)} %convert_bitcast_fusion, f32[1,4]{1,0:T(1,128)} %bitcast.10, f32[1,64]{1,0:T(1,128)} %bitcast.11, bf16[4,64]{1,0:T(4,128)(2,1)} %bitcast.9, bf16[4,64]{1,0:T(4,128)(2,1)} %param.12), kind=kLoop, calls=%fused_computation | loop fusion | flops 4224 | bytes 4176 | tf_op jit(solution)/shard_map/add | solution.py:371
  8.4 0.0 copy-start
  8.4 1.2 %copy-done = bf16[8,32,2048]{2,1,0:T(8,128)(2,1)S(1)} copy-done((bf16[8,32,2048]{2,1,0:T(8,128)(2,1)S(1)}, bf16[8,32,2048]{2,1,0:T(8,128)(2,1)}, u32[]{:S(2)}) %copy-start) | copy-done | bytes 1048600
  9.6 3.0 %features.1 = (bf16[2,4,8,48,1024]{4,3,2,1,0:T(8,128)(2,1)S(1)}, bf16[512,48]{1,0:T(8,128)(2,1)S(1)}, bf16[32,512]{1,0:T(8,128)(2,1)S(1)}, f32[8,1024]{1,0:T(8,128)S(1)}, f32[32,128]{1,0:T(8,128)S(1)}) custom-call(bf16[8,32,2048]{2,1,0:T(8,128)(2,1)S(1)} %copy-done, f32[11,64]{1,0:T(8,128)S(1)} %pad_add_fusion.facts), custom_call_target="tpu_custom_call" | custom-call | flops 1000000000 | tf_op jit(solution)/shard_map/features/pallas_call | solution.py:331
  12.6 5.7 %march_send_inner.1.after = f32[2,4,8,1024]{3,2,1,0:T(8,128)S(1)} custom-call(s32[1]{0:T(128)} %bitcast.where, bf16[2,4,8,48,1024]{4,3,2,1,0:T(8,128)(2,1)S(1)} %get-tuple-element.12.feats, bf16[512,48]{1,0:T(8,128)(2,1)S(1)} %get-tuple-element.13.w1, bf16[32,512]{1,0:T(8,128)(2,1)S(1)} %get-tuple-element.14.w2, f32[8,1024]{1,0:T(8,128)S(1)} %get-tuple-element.15.coverage, ...), custom_call_target="tpu_custom_call" | custom-call | flops 6700000256 | tf_op jit(solution)/shard_map/march_send_inner/pallas_call | solution.py:331
  18.3 0.1 collective-permute-start.2
  18.4 0.3 edges.1
  18.7 5.8 %march_send_outer.1 = f32[2,4,8,1024]{3,2,1,0:T(8,128)S(1)} custom-call(s32[1]{0:T(128)} %bitcast.where, bf16[2,4,8,48,1024]{4,3,2,1,0:T(8,128)(2,1)S(1)} %get-tuple-element.12.feats, bf16[2,8,48,1024]{3,2,1,0:T(8,128)(2,1)S(1)} %edges.1, bf16[512,48]{1,0:T(8,128)(2,1)S(1)} %get-tuple-element.13.w1, bf16[32,512]{1,0:T(8,128)(2,1)S(1)} %get-tuple-element.14.w2, ...), custom_call_target="tpu_custom_call" | custom-call | flops 6800000000 | tf_op jit(solution)/shard_map/march_send_outer/pallas_call | solution.py:331
  24.5 0.0 copy-start.1
  24.5 0.6 collective-permute-start.3
  25.1 2.9 %march_first.1.raw = f32[4,8,1024]{2,1,0:T(8,128)S(1)} custom-call(s32[1]{0:T(128)} %bitcast.where, bf16[2,4,8,48,1024]{4,3,2,1,0:T(8,128)(2,1)S(1)} %get-tuple-element.12.feats, bf16[2,8,48,1024]{3,2,1,0:T(8,128)(2,1)S(1)} %edges.1, bf16[512,48]{1,0:T(8,128)(2,1)S(1)} %get-tuple-element.13.w1, bf16[32,512]{1,0:T(8,128)(2,1)S(1)} %get-tuple-element.14.w2, ...), custom_call_target="tpu_custom_call" | custom-call | flops 4000000000 | tf_op jit(solution)/shard_map/march_first/pallas_call | solution.py:331
  28.0 0.6 merge_first.1.after
  28.6 4.0 %collective-permute-start.5 = (f32[4,8,1024]{2,1,0:T(8,128)S(1)}, f32[4,8,1024]{2,1,0:T(8,128)S(1)}, u32[]{:S(2)}, u32[]{:S(2)}) collective-permute-start(f32[4,8,1024]{2,1,0:T(8,128)S(1)} %merge_first.1.after), channel_id=1, source_target_pairs={{0,4},{1,5},{2,6},{3,7},{4,0},{5,1},{6,2},{7,3},{8,12},{9,13},{10,... | collective-permute-start | bytes 393224 | tf_op jit(solution)/shard_map/ppermute | solution.py:487
  32.5 3.6 %march_keep1.1.after = f32[4,8,1024]{2,1,0:T(8,128)S(1)} custom-call(s32[1]{0:T(128)} %bitcast.where, s32[32]{0:T(128)S(1)} %copy-done.1, bf16[2,4,8,48,1024]{4,3,2,1,0:T(8,128)(2,1)S(1)} %get-tuple-element.12.feats, bf16[2,8,48,1024]{3,2,1,0:T(8,128)(2,1)S(1)} %edges.1, bf16[512,48]{1,0:T(8,128)(2,1)S(1)} %get-tuple-element.13.w1, ...), custom_call_target="tpu_custom_call" | custom-call | flops 4000000000 | tf_op jit(solution)/shard_map/march_keep1/pallas_call | solution.py:331
  36.2 1.1 %collective-permute-start.4 = (f32[4,8,1024]{2,1,0:T(8,128)S(1)}, f32[4,8,1024]{2,1,0:T(8,128)S(1)}, u32[]{:S(2)}, u32[]{:S(2)}) collective-permute-start(f32[4,8,1024]{2,1,0:T(8,128)S(1)} %march_keep1.1.after), channel_id=1, source_target_pairs={{0,2},{1,3},{2,0},{3,1},{4,6},{5,7},{6,4},{7,5},{8,10},{9,11},{10,... | collective-permute-start | bytes 393224 | tf_op jit(solution)/shard_map/ppermute | solution.py:487
  37.3 3.5 %march_keep3.1.after = f32[4,8,1024]{2,1,0:T(8,128)S(1)} custom-call(s32[1]{0:T(128)} %bitcast.where, s32[32]{0:T(128)S(1)} %copy-done.1, bf16[2,4,8,48,1024]{4,3,2,1,0:T(8,128)(2,1)S(1)} %get-tuple-element.12.feats, bf16[2,8,48,1024]{3,2,1,0:T(8,128)(2,1)S(1)} %edges.1, bf16[512,48]{1,0:T(8,128)(2,1)S(1)} %get-tuple-element.13.w1, ...), custom_call_target="tpu_custom_call" | custom-call | flops 4000000000 | tf_op jit(solution)/shard_map/march_keep3/pallas_call | solution.py:331
  40.7 0.1 collective-permute-start.6
  40.8 3.5 %march_keep0.1.part0 = f32[4,8,1024]{2,1,0:T(8,128)S(1)} custom-call(s32[1]{0:T(128)} %bitcast.where, s32[32]{0:T(128)S(1)} %copy-done.1, bf16[2,4,8,48,1024]{4,3,2,1,0:T(8,128)(2,1)S(1)} %get-tuple-element.12.feats, bf16[2,8,48,1024]{3,2,1,0:T(8,128)(2,1)S(1)} %edges.1, bf16[512,48]{1,0:T(8,128)(2,1)S(1)} %get-tuple-element.13.w1, ...), custom_call_target="tpu_custom_call" | custom-call | flops 4000000000 | tf_op jit(solution)/shard_map/march_keep0/pallas_call | solution.py:331
  44.3 0.0 copy-start.3
  44.3 2.7 %collective-permute-done.6.part3 = f32[4,8,1024]{2,1,0:T(8,128)S(1)} collective-permute-done((f32[4,8,1024]{2,1,0:T(8,128)S(1)}, f32[4,8,1024]{2,1,0:T(8,128)S(1)}, u32[]{:S(2)}, u32[]{:S(2)}) %collective-permute-start.6) | collective-permute-done | bytes 131104 | tf_op jit(solution)/shard_map/ppermute | solution.py:487
  47.0 0.7 %merge_z.1 = f32[4,4,4,1024]{3,2,1,0:T(4,128)S(1)} custom-call(s32[1]{0:T(128)} %bitcast.where, s32[32]{0:T(128)S(1)} %copy-done.1, f32[4,8,1024]{2,1,0:T(8,128)S(1)} %march_keep0.1.part0, f32[4,8,1024]{2,1,0:T(8,128)S(1)} %collective-permute-done.4.part1, f32[4,8,1024]{2,1,0:T(8,128)S(1)} %collective-permute-done.5.part2, ...), custom_call_target="tpu_custom_call" | custom-call | flops 1000000000 | tf_op jit(solution)/shard_map/merge_z/pallas_call | solution.py:331
  47.7 10.8 %all_to_all.5.parts = f32[4,4,4,1024]{3,2,1,0:T(4,128)S(1)} all-to-all(f32[4,4,4,1024]{3,2,1,0:T(4,128)S(1)} %merge_z.1), channel_id=1, replica_groups={{0,8,16,24},{1,9,17,25},{2,10,18,26},{3,11,19,27},{4,12,20,28},{5,13,21..., dimensions={0} | all-to-all | bytes 524288 | tf_op jit(solution)/shard_map/all_to_all | solution.py:498
  58.5 0.6 merge_x.1
  59.1 1.9 %collective-permute-start.8 = (f32[3,2,1024]{2,1,0:T(2,128)S(1)}, f32[3,2,1024]{2,1,0:T(2,128)S(1)}, u32[]{:S(2)}, u32[]{:S(2)}) collective-permute-start(f32[3,2,1024]{2,1,0:T(2,128)S(1)} %get-tuple-element.18), channel_id=1, source_target_pairs={{0,7},{1,2},{2,1},{3,4},{4,3},{5,6},{6,5},{7,32},{8,15},{9,10},{10... | collective-permute-start | bytes 73736 | tf_op jit(solution)/shard_map/ppermute | solution.py:515
  61.0 0.1 collective-permute-start.7
  61.1 0.1 reshape.30.weight
  61.2 5.1 %collective-permute-done.8.apart = f32[3,2,1024]{2,1,0:T(2,128)S(1)} collective-permute-done((f32[3,2,1024]{2,1,0:T(2,128)S(1)}, f32[3,2,1024]{2,1,0:T(2,128)S(1)}, u32[]{:S(2)}, u32[]{:S(2)}) %collective-permute-start.8) | collective-permute-done | bytes 24608 | tf_op jit(solution)/shard_map/ppermute | solution.py:515
  66.3 1.5 %filter.1 = f32[3,1,2048]{2,1,0:T(1,128)} custom-call(s32[1]{0:T(128)} %bitcast.where, f32[81]{0:T(128)S(1)} %reshape.30.weight, f32[3]{0:T(128)S(1)} %copy-done.2, f32[3,2,1024]{2,1,0:T(2,128)S(1)} %collective-permute-done.7.beside, f32[3,2,1024]{2,1,0:T(2,128)S(1)} %get-tuple-element.17.centre, f32[3,2,1024]{2,1,0:T(2,128)S(1)} %collective-permute-done.8.apart), custom_call_target="tpu_custom_call" | custom-call | flops 1000000000 | tf_op jit(solution)/shard_map/filter/pallas_call | solution.py:331
  (11 shorter events, 0.0 us)
Async XLA Ops:
  1.1 17.3 %collective-permute-start.1 = (bf16[8,1,2048]{2,1,0:T(2,128)(2,1)S(1)}, bf16[8,1,2048]{2,1,0:T(2,128)(2,1)S(1)}, u32[]{:S(2)}, u32[]{:S(2)}) collective-permute-start(bf16[8,1,2048]{2,1,0:T(2,128)(2,1)S(1)} %get-tuple-element.19), channel_id=1, source_target_pairs={{32,0},{64,32},{96,64},{33,1},{65,33},{97,65},{34,2},{66,34},{98,6... | collective-permute-start | bytes 98312 | tf_op jit(solution)/shard_map/ppermute | solution.py:386
  3.5 14.9 %collective-permute-start = (bf16[8,1,2048]{2,1,0:T(2,128)(2,1)S(1)}, bf16[8,1,2048]{2,1,0:T(2,128)(2,1)S(1)}, u32[]{:S(2)}, u32[]{:S(2)}) collective-permute-start(bf16[8,1,2048]{2,1,0:T(2,128)(2,1)S(1)} %get-tuple-element.20), channel_id=1, source_target_pairs={{0,32},{32,64},{64,96},{1,33},{33,65},{65,97},{2,34},{34,66},{66,9... | collective-permute-start | bytes 98312 | tf_op jit(solution)/shard_map/ppermute | solution.py:385
  8.4 1.2 %copy-start = (bf16[8,32,2048]{2,1,0:T(8,128)(2,1)S(1)}, bf16[8,32,2048]{2,1,0:T(8,128)(2,1)}, u32[]{:S(2)}) copy-start(bf16[8,32,2048]{2,1,0:T(8,128)(2,1)} %vol.1) | copy-start | bytes 3145732
  18.3 9.6 %collective-permute-start.2 = (f32[2,4,8,1024]{3,2,1,0:T(8,128)S(1)}, f32[2,4,8,1024]{3,2,1,0:T(8,128)S(1)}, u32[]{:S(2)}, u32[]{:S(2)}) collective-permute-start(f32[2,4,8,1024]{3,2,1,0:T(8,128)S(1)} %march_send_inner.1.after), channel_id=1, source_target_pairs={{0,1},{1,0},{2,3},{3,2},{4,5},{5,4},{6,7},{7,6},{8,9},{9,8},{10,11... | collective-permute-start | bytes 786440 | tf_op jit(solution)/shard_map/ppermute | solution.py:417
  24.5 3.5 %copy-start.1 = (s32[32]{0:T(128)S(1)}, s32[32]{0:T(128)}, u32[]{:S(2)}) copy-start(s32[32]{0:T(128)} %order.11) | copy-start | bytes 388
  24.5 3.5 %collective-permute-start.3 = (f32[2,4,8,1024]{3,2,1,0:T(8,128)S(1)}, f32[2,4,8,1024]{3,2,1,0:T(8,128)S(1)}, u32[]{:S(2)}, u32[]{:S(2)}) collective-permute-start(f32[2,4,8,1024]{3,2,1,0:T(8,128)S(1)} %march_send_outer.1), channel_id=1, source_target_pairs={{0,1},{1,0},{2,3},{3,2},{4,5},{5,4},{6,7},{7,6},{8,9},{9,8},{10,11... | collective-permute-start | bytes 786440 | tf_op jit(solution)/shard_map/ppermute | solution.py:441
  28.6 18.4 %collective-permute-start.5 = (f32[4,8,1024]{2,1,0:T(8,128)S(1)}, f32[4,8,1024]{2,1,0:T(8,128)S(1)}, u32[]{:S(2)}, u32[]{:S(2)}) collective-permute-start(f32[4,8,1024]{2,1,0:T(8,128)S(1)} %merge_first.1.after), channel_id=1, source_target_pairs={{0,4},{1,5},{2,6},{3,7},{4,0},{5,1},{6,2},{7,3},{8,12},{9,13},{10,... | collective-permute-start | bytes 393224 | tf_op jit(solution)/shard_map/ppermute | solution.py:487
  36.2 10.8 %collective-permute-start.4 = (f32[4,8,1024]{2,1,0:T(8,128)S(1)}, f32[4,8,1024]{2,1,0:T(8,128)S(1)}, u32[]{:S(2)}, u32[]{:S(2)}) collective-permute-start(f32[4,8,1024]{2,1,0:T(8,128)S(1)} %march_keep1.1.after), channel_id=1, source_target_pairs={{0,2},{1,3},{2,0},{3,1},{4,6},{5,7},{6,4},{7,5},{8,10},{9,11},{10,... | collective-permute-start | bytes 393224 | tf_op jit(solution)/shard_map/ppermute | solution.py:487
  40.7 6.3 %collective-permute-start.6 = (f32[4,8,1024]{2,1,0:T(8,128)S(1)}, f32[4,8,1024]{2,1,0:T(8,128)S(1)}, u32[]{:S(2)}, u32[]{:S(2)}) collective-permute-start(f32[4,8,1024]{2,1,0:T(8,128)S(1)} %march_keep3.1.after), channel_id=1, source_target_pairs={{0,6},{1,7},{2,4},{3,5},{4,2},{5,3},{6,0},{7,1},{8,14},{9,15},{10,... | collective-permute-start | bytes 393224 | tf_op jit(solution)/shard_map/ppermute | solution.py:487
  44.3 16.8 %copy-start.3 = (f32[3,3,3,3]{3,2,1,0:T(4,128)S(1)}, f32[3,3,3,3]{3,2,1,0:T(4,128)}, u32[]{:S(2)}) copy-start(f32[3,3,3,3]{3,2,1,0:T(4,128)} %param.16) | copy-start | bytes 976
  44.3 22.1 %copy-start.2 = (f32[3]{0:T(128)S(1)}, f32[3]{0:T(128)}, u32[]{:S(2)}) copy-start(f32[3]{0:T(128)} %bias.1) | copy-start | bytes 40
  59.1 7.3 %collective-permute-start.8 = (f32[3,2,1024]{2,1,0:T(2,128)S(1)}, f32[3,2,1024]{2,1,0:T(2,128)S(1)}, u32[]{:S(2)}, u32[]{:S(2)}) collective-permute-start(f32[3,2,1024]{2,1,0:T(2,128)S(1)} %get-tuple-element.18), channel_id=1, source_target_pairs={{0,7},{1,2},{2,1},{3,4},{4,3},{5,6},{6,5},{7,32},{8,15},{9,10},{10... | collective-permute-start | bytes 73736 | tf_op jit(solution)/shard_map/ppermute | solution.py:515
  61.0 5.3 %collective-permute-start.7 = (f32[3,2,1024]{2,1,0:T(2,128)S(1)}, f32[3,2,1024]{2,1,0:T(2,128)S(1)}, u32[]{:S(2)}, u32[]{:S(2)}) collective-permute-start(f32[3,2,1024]{2,1,0:T(2,128)S(1)} %get-tuple-element.17.centre), channel_id=1, source_target_pairs={{0,1},{1,0},{2,3},{3,2},{4,5},{5,4},{6,7},{7,6},{8,9},{9,8},{10,11... | collective-permute-start | bytes 73736 | tf_op jit(solution)/shard_map/ppermute | solution.py:516

commit v5 on v4

--- a/solution.py
+++ b/solution.py
@@ -12,8 +12,14 @@
 CHUNK = 512
 LAG = 1
 SPLIT = 2
-FIRST = 2
-ORDER = (2, 1, 3, 0)
+PLAN = (
+    ("send", (2, 1)),
+    ("send", (3,)),
+    ("keep", (2, 1, 3)),
+    ("send", (0,)),
+    ("keep", (0,)),
+)
+AWAITED = (2,)
 F32 = jnp.float32
 BF16 = jnp.bfloat16
 
@@ -52,15 +58,16 @@
 
 
 def feature_kernel(
-    vol, facts, feats, w1, w2, coverage, shift, lines, planes, *, optical
+    where, vol, facts, counts, feats, w1, w2, coverage, shift, flags, lines, planes, *, optical
 ):
     layers, rows, columns = vol.shape
     half = columns // 2
     prepare_weights(facts, w1, w2)
-    coverage[...] = coverage_of(facts[10:11], optical, half)
+    coverage[...] = coverage_of(counts[0:1].astype(F32), optical, half)
     for o in range(4):
         scale = 0.5 if o < 3 else 1.0
         shift[8 * o : 8 * o + 8] = jnp.broadcast_to(scale * facts[9:10, o : o + 1], (8, 128))
+    set_flags(flags, counts[1:2], where[0])
     blocks = half // 128
 
     def permute(z, carry):
@@ -109,7 +116,7 @@
     lax.fori_loop(0, layers, gradients, 0)
 
 
-def edge_kernel(feats, top, bot, after, edges):
+def edge_kernel(feats, top, bot, edges):
     layers = feats.shape[2]
     half = feats.shape[4]
     sub = iota((8, half), 0)
@@ -193,36 +200,43 @@
     return jnp.concatenate(cols, 1)
 
 
-def send_inner_kernel(where, feats, w1, w2, coverage, shift, out):
-    parity = 1 - (where[0] & 1)
+def send_kernel(where, feats, edges, w1, w2, coverage, shift, after, out, x, *, steps):
+    d = where[0]
+    parity = 1 - (d & 1)
+    first, *others = steps
 
     def piece(i, carry):
-        march(feats.at[parity, 1 + i], w1, w2, coverage, shift, out.at[i])
-        return carry
-
-    lax.fori_loop(0, 2, piece, 0)
-
-
-def send_outer_kernel(where, feats, edges, w1, w2, coverage, shift, out, x):
-    parity = 1 - (where[0] & 1)
-
-    def piece(i, carry):
-        load_plane(feats, edges, parity, 3 * i, x)
+        step = first
+        for n, other in enumerate(others):
+            step = jnp.where(i == n + 1, other, step)
+        load_plane(feats, edges, parity, ((d >> 1) & 3) ^ step, x)
         march(x, w1, w2, coverage, shift, out.at[i])
         return carry
 
-    lax.fori_loop(0, 2, piece, 0)
-
-
-def over(parts, places):
+    lax.fori_loop(0, len(steps), piece, 0)
+
+
+def over(parts, flags, base):
+    rows, width = parts[0][3].shape
+    front = {}
+    n = base
+    for i in range(len(parts)):
+        for j in range(i + 1, len(parts)):
+            flag = jnp.concatenate([flags[n, :rows]] * (width // 128), 1)
+            front[i, j] = flag > 0.5
+            n += 1
     colours = [None] * 3
     total = None
     for i, part in enumerate(parts):
         light = None
         for j, other in enumerate(parts):
-            if j != i:
-                factor = jnp.where(places[j] < places[i], other[3], 1.0)
-                light = factor if light is None else light * factor
+            if j == i:
+                continue
+            if j < i:
+                factor = jnp.where(front[j, i], other[3], 1.0)
+            else:
+                factor = jnp.where(front[i, j], 1.0, other[3])
+            light = factor if light is None else light * factor
         for o in range(3):
             term = light * part[o]
             colours[o] = term if colours[o] is None else colours[o] + term
@@ -230,45 +244,49 @@
     return (*colours, total)
 
 
-def first_kernel(where, feats, edges, w1, w2, coverage, shift, out, x):
+def set_flags(flags, order, d):
+    spot = iota((1, HIDDEN), 1)
+    order = order.astype(F32)
+
+    def place(index, bit, count):
+        value = jnp.sum(jnp.where(spot == index, order, 0.0), axis=1, keepdims=True)
+        return (value.astype(jnp.int32) >> bit) & (count - 1)
+
+    groups = (
+        [place(d ^ k, 0, 2) for k in range(2)],
+        [place(d ^ (k << 1), 1, 4) for k in range(4)],
+        [place((d & 7) | (k << 3), 3, 4) for k in range(4)],
+    )
+    n = 0
+    for group in groups:
+        for i in range(len(group)):
+            for j in range(i + 1, len(group)):
+                flag = jnp.where(group[i] < group[j], 1.0, 0.0)
+                flags[n] = jnp.broadcast_to(flag, (8, 128))
+                n += 1
+
+
+def keep_kernel(
+    where, flags, feats, edges, w1, w2, coverage, shift, received, *refs, step, slot
+):
+    out, x = refs[-2:]
     d = where[0]
-    load_plane(feats, edges, d & 1, ((d >> 1) & 3) ^ FIRST, x)
+    load_plane(feats, edges, d & 1, ((d >> 1) & 3) ^ step, x)
     march(x, w1, w2, coverage, shift, out)
-
-
-def merge_cores(d, order, zpos, state, inner, outer):
-    slot = zpos >> 1
-    middle = (zpos == 1) | (zpos == 2)
-    other = tuple(jnp.where(middle, inner[slot, o], outer[slot, o]) for o in range(4))
-    return over((state, other), (order[d] & 1, order[d ^ 1] & 1))
-
-
-def first_merge_kernel(where, order, raw, inner, outer, out):
-    d = where[0]
-    state = tuple(raw[o] for o in range(4))
-    merged = merge_cores(d, order, ((d >> 1) & 3) ^ FIRST, state, inner, outer)
+    if step == 0:
+        return
+    state = tuple(out[o] for o in range(4))
+    other = tuple(received[slot, o] for o in range(4))
+    merged = over((state, other), flags, 0)
     for o in range(4):
         out[o] = merged[o]
 
 
-def keep_kernel(
-    where, order, feats, edges, w1, w2, coverage, shift, inner, outer, after, out, x, *, step
-):
-    d = where[0]
-    zpos = ((d >> 1) & 3) ^ step
-    load_plane(feats, edges, d & 1, zpos, x)
-    march(x, w1, w2, coverage, shift, out)
-    state = tuple(out[o] for o in range(4))
-    merged = merge_cores(d, order, zpos, state, inner, outer)
-    for o in range(4):
-        out[o] = merged[o]
-
-
-def merge_z_kernel(where, order, part0, part1, part2, part3, out):
+def merge_z_kernel(where, flags, received, part0, part1, part2, part3, out):
     d = where[0]
     parts = [tuple(p[o] for o in range(4)) for p in (part0, part1, part2, part3)]
-    places = [(order[d ^ (k << 1)] >> 1) & 3 for k in range(4)]
-    merged = over(parts, places)
+    parts[0] = over((parts[0], tuple(received[0, o] for o in range(4))), flags, 0)
+    merged = over(parts, flags, 1)
     odd = (d & 1) == 1
     for o in range(4):
         rows = [merged[o][k : k + 1] for k in range(8)]
@@ -285,11 +303,10 @@
             )
 
 
-def merge_x_kernel(where, order, parts, centre, extra):
+def merge_x_kernel(where, flags, parts, centre, extra):
     d = where[0]
     group = [tuple(parts[k, o] for o in range(4)) for k in range(4)]
-    places = [order[(d & 7) | (k << 3)] >> 3 for k in range(4)]
-    merged = over(group, places)
+    merged = over(group, flags, 7)
     boundary = ((d & 7) == 0) | ((d & 7) == 7)
     for o in range(3):
         centre[o] = merged[o][0:2]
@@ -301,7 +318,8 @@
     even = (where[0] & 1) == 0
     lane = iota((2, half), 1)
     sub = iota((2, half), 0)
-    sums = [jnp.full((2, half), bias[o], F32) for o in range(3)]
+    spread = lambda v: jnp.concatenate([jnp.broadcast_to(v, (2, 128))] * (half // 128), 1)
+    sums = [spread(bias[:, o : o + 1]) for o in range(3)]
     for i in range(3):
         above = jnp.where(even, apart[i], beside[i])
         below = jnp.where(even, beside[i], apart[i])
@@ -317,7 +335,7 @@
             )
             for b, window in enumerate((left, row, right)):
                 for o in range(3):
-                    sums[o] = sums[o] + weight[((o * 3 + i) * 3 + a) * 3 + b] * window
+                    sums[o] = sums[o] + spread(weight[o, i, a : a + 1, b : b + 1]) * window
     for o in range(3):
         out[o, :, :half] = sums[o][0:1]
         out[o, :, half:] = sums[o][1:2]
@@ -325,6 +343,7 @@
 
 VMEM = pl.BlockSpec(memory_space=pltpu.VMEM)
 SMEM = pl.BlockSpec(memory_space=pltpu.SMEM)
+ANY = pl.BlockSpec(memory_space=pl.ANY)
 
 
 def call(kernel, name, outs, specs, *args, scratch=(), micros=1.0):
@@ -362,10 +381,10 @@
     return pairs
 
 
-def table_of(*arrays):
-    flat = [v.reshape(-1, v.shape[-1]).astype(F32) for v in arrays]
+def table_of(kind, *arrays):
+    flat = [v.reshape(-1, v.shape[-1]).astype(kind) for v in arrays]
     rows = sum(v.shape[0] for v in flat)
-    total, at = 0.0, 0
+    total, at = jnp.zeros((rows, HIDDEN), kind), 0
     for v in flat:
         n, width = v.shape
         total = total + jnp.pad(v, ((at, rows - at - n), (0, HIDDEN - width)))
@@ -381,10 +400,11 @@
     optical = 2.0 / (layers * depths)
     d = lax.axis_index("depth")
     where = d.astype(jnp.int32).reshape(1)
-    facts = table_of(w_in, b_in, w_out.T, b_out, occupancy)
+    facts = table_of(F32, w_in, b_in, w_out.T, b_out)
+    counts = table_of(jnp.int32, occupancy, slab_order)
     top = lax.ppermute(volume[:, rows - 1 :], "strip", [(i, i + 1) for i in range(strips - 1)])
     bot = lax.ppermute(volume[:, :1], "strip", [(i + 1, i) for i in range(strips - 1)])
-    feats, w1, w2, coverage, shift = call(
+    feats, w1, w2, coverage, shift, flags = call(
         functools.partial(feature_kernel, optical=optical),
         "features",
         (
@@ -393,10 +413,13 @@
             shape((32, HIDDEN * 8), BF16),
             shape((8, half)),
             shape((32, 128)),
+            shape((13, 8, 128)),
         ),
-        [VMEM] * 2,
+        [SMEM] + [VMEM] * 3,
+        where,
         volume,
         facts,
+        counts,
         scratch=[
             pltpu.VMEM((rows * columns // 128, 128), F32),
             pltpu.VMEM((layers, 8, 8, half), F32),
@@ -404,95 +427,74 @@
     )
     net = (w1, w2, coverage, shift)
     cores = [(i, i ^ 1) for i in range(depths)]
-    sent = call(
-        send_inner_kernel,
-        "march_send_inner",
-        shape((2, 4, 8, half)),
-        [SMEM] + [VMEM] * 5,
-        where,
-        feats,
-        *net,
-        micros=6.7,
-    )
-    inner = lax.ppermute(sent, "depth", cores)
     edges = call(
         edge_kernel,
         "edges",
         shape((2, layers, KDIM, half), BF16),
-        [VMEM] * 3 + [pl.BlockSpec(memory_space=pl.ANY)],
+        [VMEM] * 3,
         feats,
         top,
         bot,
-        sent,
     )
     plane = pltpu.VMEM((layers, KDIM, half), BF16)
-    sent = call(
-        send_outer_kernel,
-        "march_send_outer",
-        shape((2, 4, 8, half)),
-        [SMEM] + [VMEM] * 6,
-        where,
-        feats,
-        edges,
-        *net,
-        scratch=[plane],
-        micros=6.8,
-    )
-    outer = lax.ppermute(sent, "depth", cores)
-    raw = call(
-        first_kernel,
-        "march_first",
-        shape((4, 8, half)),
-        [SMEM] + [VMEM] * 6,
-        where,
-        feats,
-        edges,
-        *net,
-        scratch=[plane],
-        micros=4.0,
-    )
-    parts = [None] * 4
-    for step in ORDER:
-        if step == FIRST:
-            piece = call(
-                first_merge_kernel,
-                "merge_first",
-                shape((4, 8, half)),
-                [SMEM, SMEM] + [VMEM] * 3,
-                where,
-                slab_order,
-                raw,
-                inner,
-                outer,
-            )
-        else:
-            piece = call(
-                functools.partial(keep_kernel, step=step),
-                f"march_keep{step}",
-                shape((4, 8, half)),
-                [SMEM, SMEM] + [VMEM] * 8 + [pl.BlockSpec(memory_space=pl.ANY)],
-                where,
-                slab_order,
-                feats,
-                edges,
-                *net,
-                inner,
-                outer,
-                earlier,
-                scratch=[plane],
-                micros=4.0,
-            )
-        earlier = piece
-        if step:
-            piece = lax.ppermute(piece, "depth", [(i, i ^ (step << 1)) for i in range(depths)])
-        parts[step] = piece
+    latest = edges
+
+    def send(steps):
+        return call(
+            functools.partial(send_kernel, steps=steps),
+            "march_send" + "".join(map(str, steps)),
+            shape((len(steps), 4, 8, half)),
+            [SMEM] + [VMEM] * 6 + [ANY],
+            where,
+            feats,
+            edges,
+            *net,
+            latest,
+            scratch=[plane],
+            micros=3.0 * len(steps),
+        )
+
+    def keep(step, received, slot, *landed):
+        return call(
+            functools.partial(keep_kernel, step=step, slot=slot),
+            f"march_keep{step}",
+            shape((4, 8, half)),
+            [SMEM] + [VMEM] * 7 + [VMEM if step else ANY, ANY] + [ANY] * len(landed),
+            where,
+            flags,
+            feats,
+            edges,
+            *net,
+            received,
+            latest,
+            *landed,
+            scratch=[plane],
+            micros=3.0,
+        )
+
+    received, parts = {}, [None] * 4
+    for kind, steps in PLAN:
+        if kind == "send":
+            latest = send(steps)
+            arriving = lax.ppermute(latest, "depth", cores)
+            for slot, step in enumerate(steps):
+                received[step] = (arriving, slot)
+            continue
+        for step in steps:
+            landed = [parts[n] for n in AWAITED] if step == 0 else []
+            latest = keep(step, *received[step if step else 3], *landed)
+            parts[step] = latest
+            if step:
+                swap = [(i, i ^ (step << 1)) for i in range(depths)]
+                parts[step] = lax.ppermute(latest, "depth", swap)
     rows_out = call(
         merge_z_kernel,
         "merge_z",
         shape((4, 4, 4, half)),
-        [SMEM, SMEM] + [VMEM] * 4,
+        [SMEM] + [VMEM] * 6,
         where,
-        slab_order,
+        flags,
+        received[0][0],
         *parts,
     )
     rows_in = lax.all_to_all(
@@ -507,9 +509,9 @@
         merge_x_kernel,
         "merge_x",
         (shape((3, 2, half)), shape((3, 2, half))),
-        [SMEM, SMEM, VMEM],
+        [SMEM, VMEM, VMEM],
         where,
-        slab_order,
+        flags,
         rows_in,
     )
     apart = lax.ppermute(extra, ("strip", "depth"), across_pairs(strips, depths))
@@ -518,10 +520,10 @@
         filter_kernel,
         "filter",
         shape((3, 1, columns)),
-        [SMEM] * 3 + [VMEM] * 3,
+        [SMEM] + [VMEM] * 5,
         where,
-        conv_weight.reshape(-1),
-        conv_bias,
+        conv_weight,
+        conv_bias.reshape(1, 3),
         beside,
         picture,
         apart,

time: 68.1 us -> 64.5 us (0.947)
  Pallas kernels: 31.5 us -> 28.4 us
  waiting for transfers between devices: 7.82 us -> 5.47 us
  starting transfers between devices: 13.6 us -> 15.6 us
    pallas_call x12, Pallas kernels: 31.5 us -> 28.4 us  [call(): pl.pallas_call(kernel, out_shape=outs, in_specs=specs, out_specs=jax.tree...]
    ppermute x1, starting transfers between devices: 1.92 us -> 3.85 us  [shards(): lax.ppermute(extra, ('strip', 'depth'), across_pairs(strips, depths))]
    ppermute x1, waiting for transfers between devices: 5.12 us -> 3.39 us  [shards(): lax.ppermute(extra, ('strip', 'depth'), across_pairs(strips, depths))]
    add x1 -> x2, other arithmetic: 0.74 us -> 1.42 us  [table_of(): total = total + jnp.pad(v, ((at, rows - at - n), (0, HIDDEN - width)))]
    ppermute x5 -> x6, waiting for transfers between devices: 2.69 us -> 2.07 us  [the longest x3 2.06 us: shards(): parts[step] = lax.ppermute(latest, 'depth', swap)]
    ppermute x5 -> x6, starting transfers between devices: 5.79 us -> 5.79 us  [the longest x3 5.13 us: shards(): parts[step] = lax.ppermute(latest, 'depth', swap)]
  transfers between devices with their start and end apart: 9 -> 10, of which waited for: 2 -> 2; matrix products, arithmetic and copies ran while one was open for 2% -> 2% of each run, Pallas kernels for 42% -> 33%
where the time goes in v5:
time: 64.5 us; the launch traced here: 64.2 us
  Pallas kernels  28.4 us (44%)
  starting transfers between devices  15.6 us (24%)
  blocking collectives  10.8 us (17%)
  waiting for transfers between devices  5.47 us (8%)
  local copies, waits for them, and re-layouts  2.37 us (4%)
  other arithmetic  1.42 us (2%)
    pallas_call x12, Pallas kernels, call(): pl.pallas_call(kernel, out_shape=outs, in_specs=specs, out_specs=jax.tree...  28.4 us
    all_to_all x1, blocking collectives, shards(): lax.all_to_all(rows_out, 'depth', 0, 0, tiled=True, axis_index_groups=[[i...  10.8 us
    ppermute x3, starting transfers between devices, shards(): parts[step] = lax.ppermute(latest, 'depth', swap)  5.13 us
    ppermute x1, starting transfers between devices, shards(): lax.ppermute(extra, ('strip', 'depth'), across_pairs(strips, depths))  3.85 us
    ppermute x1, waiting for transfers between devices, shards(): lax.ppermute(extra, ('strip', 'depth'), across_pairs(strips, depths))  3.39 us
    ppermute x1, starting transfers between devices, shards(): lax.ppermute(volume[:, rows - 1:], 'strip', [(i, i + 1) for i in range(st...  3.19 us
    ppermute x1, starting transfers between devices, shards(): lax.ppermute(volume[:, :1], 'strip', [(i + 1, i) for i in range(strips -...  2.65 us
    ppermute x3, waiting for transfers between devices, shards(): parts[step] = lax.ppermute(latest, 'depth', swap)  2.06 us
  transfers between devices with their start and end apart: 10, of which 2 were waited for; matrix products, arithmetic and copies ran while one was open for 2% of the time, Pallas kernels for 33%

profile of v5, /device:TPU:16, one launch (start us, length us, event | category | flops | bytes accessed | tf_op | source)
XLA Modules:
  0.0 64.2 jit_solution(2429165378880126887)
XLA Ops:
  0.0 1.1 %fusion = (bf16[8,1,2048]{2,1,0:T(2,128)(2,1)S(1)}, bf16[8,1,2048]{2,1,0:T(2,128)(2,1)S(1)}) fusion(bf16[8,32,2048]{2,1,0:T(8,128)(2,1)} %vol.1), kind=kLoop, calls=%fused_computation.2 | loop fusion | bytes 131072 | tf_op jit(solution)/shard_map/slice | solution.py:406
  1.1 3.2 %collective-permute-start = (bf16[8,1,2048]{2,1,0:T(2,128)(2,1)S(1)}, bf16[8,1,2048]{2,1,0:T(2,128)(2,1)S(1)}, u32[]{:S(2)}, u32[]{:S(2)}) collective-permute-start(bf16[8,1,2048]{2,1,0:T(2,128)(2,1)S(1)} %get-tuple-element.22), channel_id=1, source_target_pairs={{0,32},{32,64},{64,96},{1,33},{33,65},{65,97},{2,34},{34,66},{66,9... | collective-permute-start | bytes 98312 | tf_op jit(solution)/shard_map/ppermute | solution.py:405
  4.3 2.7 %collective-permute-start.1 = (bf16[8,1,2048]{2,1,0:T(2,128)(2,1)S(1)}, bf16[8,1,2048]{2,1,0:T(2,128)(2,1)S(1)}, u32[]{:S(2)}, u32[]{:S(2)}) collective-permute-start(bf16[8,1,2048]{2,1,0:T(2,128)(2,1)S(1)} %get-tuple-element.21), channel_id=1, source_target_pairs={{32,0},{64,32},{96,64},{33,1},{65,33},{97,65},{34,2},{66,34},{98,6... | collective-permute-start | bytes 98312 | tf_op jit(solution)/shard_map/ppermute | solution.py:406
  7.0 0.7 %pad_add_fusion.1.counts = s32[2,64]{1,0:T(2,128)S(1)} fusion(s32[1,32]{1,0:T(1,128)} %bitcast.14, s32[1,16]{1,0:T(1,128)} %bitcast.15), kind=kLoop, calls=%fused_computation.1 | loop fusion | flops 128 | bytes 704 | tf_op jit(solution)/shard_map/add | solution.py:390
  7.7 0.7 %pad_add_fusion.facts = f32[10,64]{1,0:T(8,128)S(1)} fusion(f32[1,4]{1,0:T(1,128)} %bitcast.12, f32[1,64]{1,0:T(1,128)} %bitcast.13, bf16[4,64]{1,0:T(4,128)(2,1)} %bitcast.11, bf16[4,64]{1,0:T(4,128)(2,1)} %param.12), kind=kLoop, calls=%fused_computation | loop fusion | flops 3200 | bytes 3856 | tf_op jit(solution)/shard_map/add | solution.py:390
  8.4 1.2 %copy-done = bf16[8,32,2048]{2,1,0:T(8,128)(2,1)S(1)} copy-done((bf16[8,32,2048]{2,1,0:T(8,128)(2,1)S(1)}, bf16[8,32,2048]{2,1,0:T(8,128)(2,1)}, u32[]{:S(2)}) %copy-start) | copy-done | bytes 1048600
  9.6 3.0 %features.1 = (bf16[2,4,8,48,1024]{4,3,2,1,0:T(8,128)(2,1)S(1)}, bf16[512,48]{1,0:T(8,128)(2,1)S(1)}, bf16[32,512]{1,0:T(8,128)(2,1)S(1)}, f32[8,1024]{1,0:T(8,1...) custom-call(s32[1]{0:T(128)} %bitcast.where, bf16[8,32,2048]{2,1,0:T(8,128)(2,1)S(1)} %copy-done, ...), custom_call_target="tpu_custom_call" | custom-call | flops 1000000000 | tf_op jit(solution)/shard_map/features/pallas_call | solution.py:350
  12.7 0.0 collective-permute-done.1.bot
  12.7 0.3 edges.1.after
  12.9 5.8 %march_send21.1.after = f32[2,4,8,1024]{3,2,1,0:T(8,128)S(1)} custom-call(s32[1]{0:T(128)} %bitcast.where, bf16[2,4,8,48,1024]{4,3,2,1,0:T(8,128)(2,1)S(1)} %get-tuple-element.14.feats, bf16[2,8,48,1024]{3,2,1,0:T(8,128)(2,1)S(1)} %edges.1.after, bf16[512,48]{1,0:T(8,128)(2,1)S(1)} %get-tuple-element.15.w1, bf16[32,512]{1,0:T(8,128)(2,1)S(1)} %get-tuple-element.16.w2, ...), custom_call_target="tpu_custom_call" | custom-call | flops 6000000000 | tf_op jit(solution)/shard_map/march_send21/pallas_call | solution.py:350
  18.8 0.1 collective-permute-start.3
  18.9 2.9 %march_send3.1.refs_0_ = f32[1,4,8,1024]{3,2,1,0:T(8,128)S(1)} custom-call(s32[1]{0:T(128)} %bitcast.where, bf16[2,4,8,48,1024]{4,3,2,1,0:T(8,128)(2,1)S(1)} %get-tuple-element.14.feats, bf16[2,8,48,1024]{3,2,1,0:T(8,128)(2,1)S(1)} %edges.1.after, bf16[512,48]{1,0:T(8,128)(2,1)S(1)} %get-tuple-element.15.w1, bf16[32,512]{1,0:T(8,128)(2,1)S(1)} %get-tuple-element.16.w2, ...), custom_call_target="tpu_custom_call" | custom-call | flops 3000000000 | tf_op jit(solution)/shard_map/march_send3/pallas_call | solution.py:350
  21.8 0.6 collective-permute-start.2
  22.4 0.0 collective-permute-done.3.received
  22.4 2.9 %march_keep2.1.refs_0_ = f32[4,8,1024]{2,1,0:T(8,128)S(1)} custom-call(s32[1]{0:T(128)} %bitcast.where, f32[13,8,128]{2,1,0:T(8,128)S(1)} %get-tuple-element.13.flags, bf16[2,4,8,48,1024]{4,3,2,1,0:T(8,128)(2,1)S(1)} %get-tuple-element.14.feats, bf16[2,8,48,1024]{3,2,1,0:T(8,128)(2,1)S(1)} %edges.1.after, bf16[512,48]{1,0:T(8,128)(2,1)S(1)} %get-tuple-element.15.w1, ...), custom_call_target="tpu_custom_call" | custom-call | flops 3000000000 | tf_op jit(solution)/shard_map/march_keep2/pallas_call | solution.py:350
  25.3 3.9 %collective-permute-start.5 = (f32[4,8,1024]{2,1,0:T(8,128)S(1)}, f32[4,8,1024]{2,1,0:T(8,128)S(1)}, u32[]{:S(2)}, u32[]{:S(2)}) collective-permute-start(f32[4,8,1024]{2,1,0:T(8,128)S(1)} %march_keep2.1.refs_0_), channel_id=1, source_target_pairs={{0,4},{1,5},{2,6},{3,7},{4,0},{5,1},{6,2},{7,3},{8,12},{9,13},{10,... | collective-permute-start | bytes 393224 | tf_op jit(solution)/shard_map/ppermute | solution.py:489
  29.3 3.1 %march_keep1.1.refs_0_ = f32[4,8,1024]{2,1,0:T(8,128)S(1)} custom-call(s32[1]{0:T(128)} %bitcast.where, f32[13,8,128]{2,1,0:T(8,128)S(1)} %get-tuple-element.13.flags, bf16[2,4,8,48,1024]{4,3,2,1,0:T(8,128)(2,1)S(1)} %get-tuple-element.14.feats, bf16[2,8,48,1024]{3,2,1,0:T(8,128)(2,1)S(1)} %edges.1.after, bf16[512,48]{1,0:T(8,128)(2,1)S(1)} %get-tuple-element.15.w1, ...), custom_call_target="tpu_custom_call" | custom-call | flops 3000000000 | tf_op jit(solution)/shard_map/march_keep1/pallas_call | solution.py:350
  32.4 3.0 %march_keep3.1.after = f32[4,8,1024]{2,1,0:T(8,128)S(1)} custom-call(s32[1]{0:T(128)} %bitcast.where, f32[13,8,128]{2,1,0:T(8,128)S(1)} %get-tuple-element.13.flags, bf16[2,4,8,48,1024]{4,3,2,1,0:T(8,128)(2,1)S(1)} %get-tuple-element.14.feats, bf16[2,8,48,1024]{3,2,1,0:T(8,128)(2,1)S(1)} %edges.1.after, bf16[512,48]{1,0:T(8,128)(2,1)S(1)} %get-tuple-element.15.w1, ...), custom_call_target="tpu_custom_call" | custom-call | flops 3000000000 | tf_op jit(solution)/shard_map/march_keep3/pallas_call | solution.py:350
  35.4 2.9 %march_send0.1.refs_0_ = f32[1,4,8,1024]{3,2,1,0:T(8,128)S(1)} custom-call(s32[1]{0:T(128)} %bitcast.where, bf16[2,4,8,48,1024]{4,3,2,1,0:T(8,128)(2,1)S(1)} %get-tuple-element.14.feats, bf16[2,8,48,1024]{3,2,1,0:T(8,128)(2,1)S(1)} %edges.1.after, bf16[512,48]{1,0:T(8,128)(2,1)S(1)} %get-tuple-element.15.w1, bf16[32,512]{1,0:T(8,128)(2,1)S(1)} %get-tuple-element.16.w2, ...), custom_call_target="tpu_custom_call" | custom-call | flops 3000000000 | tf_op jit(solution)/shard_map/march_send0/pallas_call | solution.py:350
  38.3 0.8 %collective-permute-start.7 = (f32[4,8,1024]{2,1,0:T(8,128)S(1)}, f32[4,8,1024]{2,1,0:T(8,128)S(1)}, u32[]{:S(2)}, u32[]{:S(2)}) collective-permute-start(f32[4,8,1024]{2,1,0:T(8,128)S(1)} %march_keep3.1.after), channel_id=1, source_target_pairs={{0,6},{1,7},{2,4},{3,5},{4,2},{5,3},{6,0},{7,1},{8,14},{9,15},{10,... | collective-permute-start | bytes 393224 | tf_op jit(solution)/shard_map/ppermute | solution.py:489
  39.1 0.4 collective-permute-start.6
  39.5 3.1 %march_keep0.1.part0 = f32[4,8,1024]{2,1,0:T(8,128)S(1)} custom-call(s32[1]{0:T(128)} %bitcast.where, f32[13,8,128]{2,1,0:T(8,128)S(1)} %get-tuple-element.13.flags, bf16[2,4,8,48,1024]{4,3,2,1,0:T(8,128)(2,1)S(1)} %get-tuple-element.14.feats, bf16[2,8,48,1024]{3,2,1,0:T(8,128)(2,1)S(1)} %edges.1.after, bf16[512,48]{1,0:T(8,128)(2,1)S(1)} %get-tuple-element.15.w1, ...), custom_call_target="tpu_custom_call" | custom-call | flops 3000000000 | tf_op jit(solution)/shard_map/march_keep0/pallas_call | solution.py:350
  42.6 0.0 copy-start.1
  42.6 0.0 copy-start.2
  42.7 2.1 %collective-permute-done.7.part3 = f32[4,8,1024]{2,1,0:T(8,128)S(1)} collective-permute-done((f32[4,8,1024]{2,1,0:T(8,128)S(1)}, f32[4,8,1024]{2,1,0:T(8,128)S(1)}, u32[]{:S(2)}, u32[]{:S(2)}) %collective-permute-start.7) | collective-permute-done | bytes 131104 | tf_op jit(solution)/shard_map/ppermute | solution.py:489
  44.7 0.2 merge_z.1
  44.9 10.8 %all_to_all.5.parts = f32[4,4,4,1024]{3,2,1,0:T(4,128)S(1)} all-to-all(f32[4,4,4,1024]{3,2,1,0:T(4,128)S(1)} %merge_z.1), channel_id=1, replica_groups={{0,8,16,24},{1,9,17,25},{2,10,18,26},{3,11,19,27},{4,12,20,28},{5,13,21..., dimensions={0} | all-to-all | bytes 524288 | tf_op jit(solution)/shard_map/all_to_all | solution.py:500
  55.7 0.1 merge_x.1
  55.8 0.1 collective-permute-start.8
  55.9 3.9 %collective-permute-start.9 = (f32[3,2,1024]{2,1,0:T(2,128)S(1)}, f32[3,2,1024]{2,1,0:T(2,128)S(1)}, u32[]{:S(2)}, u32[]{:S(2)}) collective-permute-start(f32[3,2,1024]{2,1,0:T(2,128)S(1)} %get-tuple-element.20), channel_id=1, source_target_pairs={{0,7},{1,2},{2,1},{3,4},{4,3},{5,6},{6,5},{7,32},{8,15},{9,10},{10... | collective-permute-start | bytes 73736 | tf_op jit(solution)/shard_map/ppermute | solution.py:517
  59.8 3.4 %collective-permute-done.9.apart = f32[3,2,1024]{2,1,0:T(2,128)S(1)} collective-permute-done((f32[3,2,1024]{2,1,0:T(2,128)S(1)}, f32[3,2,1024]{2,1,0:T(2,128)S(1)}, u32[]{:S(2)}, u32[]{:S(2)}) %collective-permute-start.9) | collective-permute-done | bytes 24608 | tf_op jit(solution)/shard_map/ppermute | solution.py:517
  63.1 1.0 %filter.1 = f32[3,1,2048]{2,1,0:T(1,128)} custom-call(s32[1]{0:T(128)} %bitcast.where, f32[3,3,3,3]{3,2,1,0:T(4,128)S(1)} %copy-done.1, f32[1,3]{1,0:T(1,128)S(1)} %bitcast.10, f32[3,2,1024]{2,1,0:T(2,128)S(1)} %collective-permute-done.8.beside, f32[3,2,1024]{2,1,0:T(2,128)S(1)} %get-tuple-element.19.centre, f32[3,2,1024]{2,1,0:T(2,128)S(1)} %collective-permute-done.9.apart), custom_call_target="tpu_custom_call" | custom-call | flops 1000000000 | tf_op jit(solution)/shard_map/filter/pallas_call | solution.py:350
  (10 shorter events, 0.0 us)
Async XLA Ops:
  1.1 11.5 %collective-permute-start = (bf16[8,1,2048]{2,1,0:T(2,128)(2,1)S(1)}, bf16[8,1,2048]{2,1,0:T(2,128)(2,1)S(1)}, u32[]{:S(2)}, u32[]{:S(2)}) collective-permute-start(bf16[8,1,2048]{2,1,0:T(2,128)(2,1)S(1)} %get-tuple-element.22), channel_id=1, source_target_pairs={{0,32},{32,64},{64,96},{1,33},{33,65},{65,97},{2,34},{34,66},{66,9... | collective-permute-start | bytes 98312 | tf_op jit(solution)/shard_map/ppermute | solution.py:405
  4.3 8.3 %collective-permute-start.1 = (bf16[8,1,2048]{2,1,0:T(2,128)(2,1)S(1)}, bf16[8,1,2048]{2,1,0:T(2,128)(2,1)S(1)}, u32[]{:S(2)}, u32[]{:S(2)}) collective-permute-start(bf16[8,1,2048]{2,1,0:T(2,128)(2,1)S(1)} %get-tuple-element.21), channel_id=1, source_target_pairs={{32,0},{64,32},{96,64},{33,1},{65,33},{97,65},{34,2},{66,34},{98,6... | collective-permute-start | bytes 98312 | tf_op jit(solution)/shard_map/ppermute | solution.py:406
  8.4 1.2 %copy-start = (bf16[8,32,2048]{2,1,0:T(8,128)(2,1)S(1)}, bf16[8,32,2048]{2,1,0:T(8,128)(2,1)}, u32[]{:S(2)}) copy-start(bf16[8,32,2048]{2,1,0:T(8,128)(2,1)} %vol.1) | copy-start | bytes 3145732
  18.8 3.6 %collective-permute-start.3 = (f32[2,4,8,1024]{3,2,1,0:T(8,128)S(1)}, f32[2,4,8,1024]{3,2,1,0:T(8,128)S(1)}, u32[]{:S(2)}, u32[]{:S(2)}) collective-permute-start(f32[2,4,8,1024]{3,2,1,0:T(8,128)S(1)} %march_send21.1.after), channel_id=1, source_target_pairs={{0,1},{1,0},{2,3},{3,2},{4,5},{5,4},{6,7},{7,6},{8,9},{9,8},{10,11... | collective-permute-start | bytes 786440 | tf_op jit(solution)/shard_map/ppermute | solution.py:479
  21.8 10.6 %collective-permute-start.2 = (f32[1,4,8,1024]{3,2,1,0:T(8,128)S(1)}, f32[1,4,8,1024]{3,2,1,0:T(8,128)S(1)}, u32[]{:S(2)}, u32[]{:S(2)}) collective-permute-start(f32[1,4,8,1024]{3,2,1,0:T(8,128)S(1)} %march_send3.1.refs_0_), channel_id=1, source_target_pairs={{0,1},{1,0},{2,3},{3,2},{4,5},{5,4},{6,7},{7,6},{8,9},{9,8},{10,11... | collective-permute-start | bytes 393224 | tf_op jit(solution)/shard_map/ppermute | solution.py:479
  25.3 14.2 %collective-permute-start.5 = (f32[4,8,1024]{2,1,0:T(8,128)S(1)}, f32[4,8,1024]{2,1,0:T(8,128)S(1)}, u32[]{:S(2)}, u32[]{:S(2)}) collective-permute-start(f32[4,8,1024]{2,1,0:T(8,128)S(1)} %march_keep2.1.refs_0_), channel_id=1, source_target_pairs={{0,4},{1,5},{2,6},{3,7},{4,0},{5,1},{6,2},{7,3},{8,12},{9,13},{10,... | collective-permute-start | bytes 393224 | tf_op jit(solution)/shard_map/ppermute | solution.py:489
  38.3 6.4 %collective-permute-start.7 = (f32[4,8,1024]{2,1,0:T(8,128)S(1)}, f32[4,8,1024]{2,1,0:T(8,128)S(1)}, u32[]{:S(2)}, u32[]{:S(2)}) collective-permute-start(f32[4,8,1024]{2,1,0:T(8,128)S(1)} %march_keep3.1.after), channel_id=1, source_target_pairs={{0,6},{1,7},{2,4},{3,5},{4,2},{5,3},{6,0},{7,1},{8,14},{9,15},{10,... | collective-permute-start | bytes 393224 | tf_op jit(solution)/shard_map/ppermute | solution.py:489
  39.1 5.7 %collective-permute-start.6 = (f32[4,8,1024]{2,1,0:T(8,128)S(1)}, f32[4,8,1024]{2,1,0:T(8,128)S(1)}, u32[]{:S(2)}, u32[]{:S(2)}) collective-permute-start(f32[4,8,1024]{2,1,0:T(8,128)S(1)} %march_keep1.1.refs_0_), channel_id=1, source_target_pairs={{0,2},{1,3},{2,0},{3,1},{4,6},{5,7},{6,4},{7,5},{8,10},{9,11},{10,... | collective-permute-start | bytes 393224 | tf_op jit(solution)/shard_map/ppermute | solution.py:489
  39.5 3.2 %collective-permute-start.4 = (f32[1,4,8,1024]{3,2,1,0:T(8,128)S(1)}, f32[1,4,8,1024]{3,2,1,0:T(8,128)S(1)}, u32[]{:S(2)}, u32[]{:S(2)}) collective-permute-start(f32[1,4,8,1024]{3,2,1,0:T(8,128)S(1)} %march_send0.1.refs_0_), channel_id=1, source_target_pairs={{0,1},{1,0},{2,3},{3,2},{4,5},{5,4},{6,7},{7,6},{8,9},{9,8},{10,11... | collective-permute-start | bytes 393224 | tf_op jit(solution)/shard_map/ppermute | solution.py:479
  42.6 20.5 %copy-start.1 = (f32[3,3,3,3]{3,2,1,0:T(4,128)S(1)}, f32[3,3,3,3]{3,2,1,0:T(4,128)}, u32[]{:S(2)}) copy-start(f32[3,3,3,3]{3,2,1,0:T(4,128)} %weight.1) | copy-start | bytes 976
  42.6 20.5 %copy-start.2 = (f32[3]{0:T(128)S(1)}, f32[3]{0:T(128)}, u32[]{:S(2)}) copy-start(f32[3]{0:T(128)} %param.17) | copy-start | bytes 40
  55.8 4.0 %collective-permute-start.8 = (f32[3,2,1024]{2,1,0:T(2,128)S(1)}, f32[3,2,1024]{2,1,0:T(2,128)S(1)}, u32[]{:S(2)}, u32[]{:S(2)}) collective-permute-start(f32[3,2,1024]{2,1,0:T(2,128)S(1)} %get-tuple-element.19.centre), channel_id=1, source_target_pairs={{0,1},{1,0},{2,3},{3,2},{4,5},{5,4},{6,7},{7,6},{8,9},{9,8},{10,11... | collective-permute-start | bytes 73736 | tf_op jit(solution)/shard_map/ppermute | solution.py:518
  55.9 7.3 %collective-permute-start.9 = (f32[3,2,1024]{2,1,0:T(2,128)S(1)}, f32[3,2,1024]{2,1,0:T(2,128)S(1)}, u32[]{:S(2)}, u32[]{:S(2)}) collective-permute-start(f32[3,2,1024]{2,1,0:T(2,128)S(1)} %get-tuple-element.20), channel_id=1, source_target_pairs={{0,7},{1,2},{2,1},{3,4},{4,3},{5,6},{6,5},{7,32},{8,15},{9,10},{10... | collective-permute-start | bytes 73736 | tf_op jit(solution)/shard_map/ppermute | solution.py:517

commit v6 on v5

--- a/solution.py
+++ b/solution.py
@@ -81,7 +81,7 @@
                 planes[z, j, :, k * 128 : (k + 1) * 128] = jnp.concatenate([left, right], 0)
         return carry
 
-    lax.fori_loop(0, layers, permute, 0)
+    lax.fori_loop(0, layers, permute, 0, unroll=4)
     lane = iota((8, half), 1)
     sub = iota((8, half), 0)
     ones = jnp.ones((KDIM - 32, half), BF16)
@@ -113,7 +113,7 @@
             feats[j % 2, j // 2, z, 32:KDIM] = ones
         return carry
 
-    lax.fori_loop(0, layers, gradients, 0)
+    lax.fori_loop(0, layers, gradients, 0, unroll=4)
 
 
 def edge_kernel(feats, top, bot, edges):

time: 64.5 us -> 64.1 us (level)
  transfers between devices with their start and end apart: 10 -> 10, of which waited for: 2 -> 2; matrix products, arithmetic and copies ran while one was open for 2% -> 2% of each run, Pallas kernels for 33% -> 32%
where the time goes in v6:
time: 64.1 us; the launch traced here: 63.8 us
  Pallas kernels  28 us (44%)
  starting transfers between devices  15.6 us (24%)
  blocking collectives  10.8 us (17%)
  waiting for transfers between devices  5.44 us (8%)
  local copies, waits for them, and re-layouts  2.37 us (4%)
  other arithmetic  1.42 us (2%)
    pallas_call x12, Pallas kernels, call(): pl.pallas_call(kernel, out_shape=outs, in_specs=specs, out_specs=jax.tree...  28 us
    all_to_all x1, blocking collectives, shards(): lax.all_to_all(rows_out, 'depth', 0, 0, tiled=True, axis_index_groups=[[i...  10.8 us
    ppermute x3, starting transfers between devices, shards(): parts[step] = lax.ppermute(latest, 'depth', swap)  5.16 us
    ppermute x1, starting transfers between devices, shards(): lax.ppermute(extra, ('strip', 'depth'), across_pairs(strips, depths))  3.85 us
    ppermute x1, waiting for transfers between devices, shards(): lax.ppermute(extra, ('strip', 'depth'), across_pairs(strips, depths))  3.39 us
    ppermute x1, starting transfers between devices, shards(): lax.ppermute(volume[:, rows - 1:], 'strip', [(i, i + 1) for i in range(st...  3.19 us
    ppermute x1, starting transfers between devices, shards(): lax.ppermute(volume[:, :1], 'strip', [(i + 1, i) for i in range(strips -...  2.65 us
    ppermute x3, waiting for transfers between devices, shards(): parts[step] = lax.ppermute(latest, 'depth', swap)  2.04 us
  transfers between devices with their start and end apart: 10, of which 2 were waited for; matrix products, arithmetic and copies ran while one was open for 2% of the time, Pallas kernels for 32%

profile of v6, /device:TPU:16, one launch (start us, length us, event | category | flops | bytes accessed | tf_op | source)
XLA Modules:
  0.0 63.8 jit_solution(3664442020375835672)
XLA Ops:
  0.0 1.1 %fusion = (bf16[8,1,2048]{2,1,0:T(2,128)(2,1)S(1)}, bf16[8,1,2048]{2,1,0:T(2,128)(2,1)S(1)}) fusion(bf16[8,32,2048]{2,1,0:T(8,128)(2,1)} %vol.1), kind=kLoop, calls=%fused_computation.2 | loop fusion | bytes 131072 | tf_op jit(solution)/shard_map/slice | solution.py:406
  1.1 3.2 %collective-permute-start = (bf16[8,1,2048]{2,1,0:T(2,128)(2,1)S(1)}, bf16[8,1,2048]{2,1,0:T(2,128)(2,1)S(1)}, u32[]{:S(2)}, u32[]{:S(2)}) collective-permute-start(bf16[8,1,2048]{2,1,0:T(2,128)(2,1)S(1)} %get-tuple-element.22), channel_id=1, source_target_pairs={{0,32},{32,64},{64,96},{1,33},{33,65},{65,97},{2,34},{34,66},{66,9... | collective-permute-start | bytes 98312 | tf_op jit(solution)/shard_map/ppermute | solution.py:405
  4.3 2.7 %collective-permute-start.1 = (bf16[8,1,2048]{2,1,0:T(2,128)(2,1)S(1)}, bf16[8,1,2048]{2,1,0:T(2,128)(2,1)S(1)}, u32[]{:S(2)}, u32[]{:S(2)}) collective-permute-start(bf16[8,1,2048]{2,1,0:T(2,128)(2,1)S(1)} %get-tuple-element.21), channel_id=1, source_target_pairs={{32,0},{64,32},{96,64},{33,1},{65,33},{97,65},{34,2},{66,34},{98,6... | collective-permute-start | bytes 98312 | tf_op jit(solution)/shard_map/ppermute | solution.py:406
  7.0 0.7 %pad_add_fusion.1.counts = s32[2,64]{1,0:T(2,128)S(1)} fusion(s32[1,32]{1,0:T(1,128)} %bitcast.14, s32[1,16]{1,0:T(1,128)} %bitcast.15), kind=kLoop, calls=%fused_computation.1 | loop fusion | flops 128 | bytes 704 | tf_op jit(solution)/shard_map/add | solution.py:390
  7.7 0.7 %pad_add_fusion.facts = f32[10,64]{1,0:T(8,128)S(1)} fusion(f32[1,4]{1,0:T(1,128)} %bitcast.12, f32[1,64]{1,0:T(1,128)} %bitcast.13, bf16[4,64]{1,0:T(4,128)(2,1)} %bitcast.11, bf16[4,64]{1,0:T(4,128)(2,1)} %param.12), kind=kLoop, calls=%fused_computation | loop fusion | flops 3200 | bytes 3856 | tf_op jit(solution)/shard_map/add | solution.py:390
  8.4 1.2 %copy-done = bf16[8,32,2048]{2,1,0:T(8,128)(2,1)S(1)} copy-done((bf16[8,32,2048]{2,1,0:T(8,128)(2,1)S(1)}, bf16[8,32,2048]{2,1,0:T(8,128)(2,1)}, u32[]{:S(2)}) %copy-start) | copy-done | bytes 1048600
  9.6 2.7 %features.1 = (bf16[2,4,8,48,1024]{4,3,2,1,0:T(8,128)(2,1)S(1)}, bf16[512,48]{1,0:T(8,128)(2,1)S(1)}, bf16[32,512]{1,0:T(8,128)(2,1)S(1)}, f32[8,1024]{1,0:T(8,1...) custom-call(s32[1]{0:T(128)} %bitcast.where, bf16[8,32,2048]{2,1,0:T(8,128)(2,1)S(1)} %copy-done, ...), custom_call_target="tpu_custom_call" | custom-call | flops 1000000000 | tf_op jit(solution)/shard_map/features/pallas_call | solution.py:350
  12.3 0.0 collective-permute-done.top
  12.3 0.3 edges.1.after
  12.6 5.8 %march_send21.1.after = f32[2,4,8,1024]{3,2,1,0:T(8,128)S(1)} custom-call(s32[1]{0:T(128)} %bitcast.where, bf16[2,4,8,48,1024]{4,3,2,1,0:T(8,128)(2,1)S(1)} %get-tuple-element.14.feats, bf16[2,8,48,1024]{3,2,1,0:T(8,128)(2,1)S(1)} %edges.1.after, bf16[512,48]{1,0:T(8,128)(2,1)S(1)} %get-tuple-element.15.w1, bf16[32,512]{1,0:T(8,128)(2,1)S(1)} %get-tuple-element.16.w2, ...), custom_call_target="tpu_custom_call" | custom-call | flops 6000000000 | tf_op jit(solution)/shard_map/march_send21/pallas_call | solution.py:350
  18.4 0.1 collective-permute-start.3
  18.5 2.9 %march_send3.1.refs_0_ = f32[1,4,8,1024]{3,2,1,0:T(8,128)S(1)} custom-call(s32[1]{0:T(128)} %bitcast.where, bf16[2,4,8,48,1024]{4,3,2,1,0:T(8,128)(2,1)S(1)} %get-tuple-element.14.feats, bf16[2,8,48,1024]{3,2,1,0:T(8,128)(2,1)S(1)} %edges.1.after, bf16[512,48]{1,0:T(8,128)(2,1)S(1)} %get-tuple-element.15.w1, bf16[32,512]{1,0:T(8,128)(2,1)S(1)} %get-tuple-element.16.w2, ...), custom_call_target="tpu_custom_call" | custom-call | flops 3000000000 | tf_op jit(solution)/shard_map/march_send3/pallas_call | solution.py:350
  21.5 0.6 collective-permute-start.2
  22.0 0.0 collective-permute-done.3.received
  22.0 2.9 %march_keep2.1.refs_0_ = f32[4,8,1024]{2,1,0:T(8,128)S(1)} custom-call(s32[1]{0:T(128)} %bitcast.where, f32[13,8,128]{2,1,0:T(8,128)S(1)} %get-tuple-element.13.flags, bf16[2,4,8,48,1024]{4,3,2,1,0:T(8,128)(2,1)S(1)} %get-tuple-element.14.feats, bf16[2,8,48,1024]{3,2,1,0:T(8,128)(2,1)S(1)} %edges.1.after, bf16[512,48]{1,0:T(8,128)(2,1)S(1)} %get-tuple-element.15.w1, ...), custom_call_target="tpu_custom_call" | custom-call | flops 3000000000 | tf_op jit(solution)/shard_map/march_keep2/pallas_call | solution.py:350
  25.0 3.9 %collective-permute-start.5 = (f32[4,8,1024]{2,1,0:T(8,128)S(1)}, f32[4,8,1024]{2,1,0:T(8,128)S(1)}, u32[]{:S(2)}, u32[]{:S(2)}) collective-permute-start(f32[4,8,1024]{2,1,0:T(8,128)S(1)} %march_keep2.1.refs_0_), channel_id=1, source_target_pairs={{0,4},{1,5},{2,6},{3,7},{4,0},{5,1},{6,2},{7,3},{8,12},{9,13},{10,... | collective-permute-start | bytes 393224 | tf_op jit(solution)/shard_map/ppermute | solution.py:489
  28.9 3.1 %march_keep1.1.refs_0_ = f32[4,8,1024]{2,1,0:T(8,128)S(1)} custom-call(s32[1]{0:T(128)} %bitcast.where, f32[13,8,128]{2,1,0:T(8,128)S(1)} %get-tuple-element.13.flags, bf16[2,4,8,48,1024]{4,3,2,1,0:T(8,128)(2,1)S(1)} %get-tuple-element.14.feats, bf16[2,8,48,1024]{3,2,1,0:T(8,128)(2,1)S(1)} %edges.1.after, bf16[512,48]{1,0:T(8,128)(2,1)S(1)} %get-tuple-element.15.w1, ...), custom_call_target="tpu_custom_call" | custom-call | flops 3000000000 | tf_op jit(solution)/shard_map/march_keep1/pallas_call | solution.py:350
  32.0 3.0 %march_keep3.1.after = f32[4,8,1024]{2,1,0:T(8,128)S(1)} custom-call(s32[1]{0:T(128)} %bitcast.where, f32[13,8,128]{2,1,0:T(8,128)S(1)} %get-tuple-element.13.flags, bf16[2,4,8,48,1024]{4,3,2,1,0:T(8,128)(2,1)S(1)} %get-tuple-element.14.feats, bf16[2,8,48,1024]{3,2,1,0:T(8,128)(2,1)S(1)} %edges.1.after, bf16[512,48]{1,0:T(8,128)(2,1)S(1)} %get-tuple-element.15.w1, ...), custom_call_target="tpu_custom_call" | custom-call | flops 3000000000 | tf_op jit(solution)/shard_map/march_keep3/pallas_call | solution.py:350
  35.0 2.9 %march_send0.1.refs_0_ = f32[1,4,8,1024]{3,2,1,0:T(8,128)S(1)} custom-call(s32[1]{0:T(128)} %bitcast.where, bf16[2,4,8,48,1024]{4,3,2,1,0:T(8,128)(2,1)S(1)} %get-tuple-element.14.feats, bf16[2,8,48,1024]{3,2,1,0:T(8,128)(2,1)S(1)} %edges.1.after, bf16[512,48]{1,0:T(8,128)(2,1)S(1)} %get-tuple-element.15.w1, bf16[32,512]{1,0:T(8,128)(2,1)S(1)} %get-tuple-element.16.w2, ...), custom_call_target="tpu_custom_call" | custom-call | flops 3000000000 | tf_op jit(solution)/shard_map/march_send0/pallas_call | solution.py:350
  38.0 0.8 %collective-permute-start.7 = (f32[4,8,1024]{2,1,0:T(8,128)S(1)}, f32[4,8,1024]{2,1,0:T(8,128)S(1)}, u32[]{:S(2)}, u32[]{:S(2)}) collective-permute-start(f32[4,8,1024]{2,1,0:T(8,128)S(1)} %march_keep3.1.after), channel_id=1, source_target_pairs={{0,6},{1,7},{2,4},{3,5},{4,2},{5,3},{6,0},{7,1},{8,14},{9,15},{10,... | collective-permute-start | bytes 393224 | tf_op jit(solution)/shard_map/ppermute | solution.py:489
  38.7 0.4 collective-permute-start.6
  39.2 3.1 %march_keep0.1.part0 = f32[4,8,1024]{2,1,0:T(8,128)S(1)} custom-call(s32[1]{0:T(128)} %bitcast.where, f32[13,8,128]{2,1,0:T(8,128)S(1)} %get-tuple-element.13.flags, bf16[2,4,8,48,1024]{4,3,2,1,0:T(8,128)(2,1)S(1)} %get-tuple-element.14.feats, bf16[2,8,48,1024]{3,2,1,0:T(8,128)(2,1)S(1)} %edges.1.after, bf16[512,48]{1,0:T(8,128)(2,1)S(1)} %get-tuple-element.15.w1, ...), custom_call_target="tpu_custom_call" | custom-call | flops 3000000000 | tf_op jit(solution)/shard_map/march_keep0/pallas_call | solution.py:350
  42.3 0.0 copy-start.1
  42.3 0.0 copy-start.2
  42.4 2.0 %collective-permute-done.7.part3 = f32[4,8,1024]{2,1,0:T(8,128)S(1)} collective-permute-done((f32[4,8,1024]{2,1,0:T(8,128)S(1)}, f32[4,8,1024]{2,1,0:T(8,128)S(1)}, u32[]{:S(2)}, u32[]{:S(2)}) %collective-permute-start.7) | collective-permute-done | bytes 131104 | tf_op jit(solution)/shard_map/ppermute | solution.py:489
  44.4 0.2 merge_z.1
  44.6 10.8 %all_to_all.5.parts = f32[4,4,4,1024]{3,2,1,0:T(4,128)S(1)} all-to-all(f32[4,4,4,1024]{3,2,1,0:T(4,128)S(1)} %merge_z.1), channel_id=1, replica_groups={{0,8,16,24},{1,9,17,25},{2,10,18,26},{3,11,19,27},{4,12,20,28},{5,13,21..., dimensions={0} | all-to-all | bytes 524288 | tf_op jit(solution)/shard_map/all_to_all | solution.py:500
  55.4 0.1 merge_x.1
  55.5 0.1 collective-permute-start.8
  55.6 3.9 %collective-permute-start.9 = (f32[3,2,1024]{2,1,0:T(2,128)S(1)}, f32[3,2,1024]{2,1,0:T(2,128)S(1)}, u32[]{:S(2)}, u32[]{:S(2)}) collective-permute-start(f32[3,2,1024]{2,1,0:T(2,128)S(1)} %get-tuple-element.20), channel_id=1, source_target_pairs={{0,7},{1,2},{2,1},{3,4},{4,3},{5,6},{6,5},{7,32},{8,15},{9,10},{10... | collective-permute-start | bytes 73736 | tf_op jit(solution)/shard_map/ppermute | solution.py:517
  59.4 3.4 %collective-permute-done.9.apart = f32[3,2,1024]{2,1,0:T(2,128)S(1)} collective-permute-done((f32[3,2,1024]{2,1,0:T(2,128)S(1)}, f32[3,2,1024]{2,1,0:T(2,128)S(1)}, u32[]{:S(2)}, u32[]{:S(2)}) %collective-permute-start.9) | collective-permute-done | bytes 24608 | tf_op jit(solution)/shard_map/ppermute | solution.py:517
  62.8 1.0 %filter.1 = f32[3,1,2048]{2,1,0:T(1,128)} custom-call(s32[1]{0:T(128)} %bitcast.where, f32[3,3,3,3]{3,2,1,0:T(4,128)S(1)} %copy-done.1, f32[1,3]{1,0:T(1,128)S(1)} %bitcast.10, f32[3,2,1024]{2,1,0:T(2,128)S(1)} %collective-permute-done.8.beside, f32[3,2,1024]{2,1,0:T(2,128)S(1)} %get-tuple-element.19.centre, f32[3,2,1024]{2,1,0:T(2,128)S(1)} %collective-permute-done.9.apart), custom_call_target="tpu_custom_call" | custom-call | flops 1000000000 | tf_op jit(solution)/shard_map/filter/pallas_call | solution.py:350
  (10 shorter events, 0.0 us)
Async XLA Ops:
  1.1 11.2 %collective-permute-start = (bf16[8,1,2048]{2,1,0:T(2,128)(2,1)S(1)}, bf16[8,1,2048]{2,1,0:T(2,128)(2,1)S(1)}, u32[]{:S(2)}, u32[]{:S(2)}) collective-permute-start(bf16[8,1,2048]{2,1,0:T(2,128)(2,1)S(1)} %get-tuple-element.22), channel_id=1, source_target_pairs={{0,32},{32,64},{64,96},{1,33},{33,65},{65,97},{2,34},{34,66},{66,9... | collective-permute-start | bytes 98312 | tf_op jit(solution)/shard_map/ppermute | solution.py:405
  4.3 8.0 %collective-permute-start.1 = (bf16[8,1,2048]{2,1,0:T(2,128)(2,1)S(1)}, bf16[8,1,2048]{2,1,0:T(2,128)(2,1)S(1)}, u32[]{:S(2)}, u32[]{:S(2)}) collective-permute-start(bf16[8,1,2048]{2,1,0:T(2,128)(2,1)S(1)} %get-tuple-element.21), channel_id=1, source_target_pairs={{32,0},{64,32},{96,64},{33,1},{65,33},{97,65},{34,2},{66,34},{98,6... | collective-permute-start | bytes 98312 | tf_op jit(solution)/shard_map/ppermute | solution.py:406
  8.4 1.2 %copy-start = (bf16[8,32,2048]{2,1,0:T(8,128)(2,1)S(1)}, bf16[8,32,2048]{2,1,0:T(8,128)(2,1)}, u32[]{:S(2)}) copy-start(bf16[8,32,2048]{2,1,0:T(8,128)(2,1)} %vol.1) | copy-start | bytes 3145732
  18.4 3.6 %collective-permute-start.3 = (f32[2,4,8,1024]{3,2,1,0:T(8,128)S(1)}, f32[2,4,8,1024]{3,2,1,0:T(8,128)S(1)}, u32[]{:S(2)}, u32[]{:S(2)}) collective-permute-start(f32[2,4,8,1024]{3,2,1,0:T(8,128)S(1)} %march_send21.1.after), channel_id=1, source_target_pairs={{0,1},{1,0},{2,3},{3,2},{4,5},{5,4},{6,7},{7,6},{8,9},{9,8},{10,11... | collective-permute-start | bytes 786440 | tf_op jit(solution)/shard_map/ppermute | solution.py:479
  21.5 10.6 %collective-permute-start.2 = (f32[1,4,8,1024]{3,2,1,0:T(8,128)S(1)}, f32[1,4,8,1024]{3,2,1,0:T(8,128)S(1)}, u32[]{:S(2)}, u32[]{:S(2)}) collective-permute-start(f32[1,4,8,1024]{3,2,1,0:T(8,128)S(1)} %march_send3.1.refs_0_), channel_id=1, source_target_pairs={{0,1},{1,0},{2,3},{3,2},{4,5},{5,4},{6,7},{7,6},{8,9},{9,8},{10,11... | collective-permute-start | bytes 393224 | tf_op jit(solution)/shard_map/ppermute | solution.py:479
  25.0 14.2 %collective-permute-start.5 = (f32[4,8,1024]{2,1,0:T(8,128)S(1)}, f32[4,8,1024]{2,1,0:T(8,128)S(1)}, u32[]{:S(2)}, u32[]{:S(2)}) collective-permute-start(f32[4,8,1024]{2,1,0:T(8,128)S(1)} %march_keep2.1.refs_0_), channel_id=1, source_target_pairs={{0,4},{1,5},{2,6},{3,7},{4,0},{5,1},{6,2},{7,3},{8,12},{9,13},{10,... | collective-permute-start | bytes 393224 | tf_op jit(solution)/shard_map/ppermute | solution.py:489
  38.0 6.4 %collective-permute-start.7 = (f32[4,8,1024]{2,1,0:T(8,128)S(1)}, f32[4,8,1024]{2,1,0:T(8,128)S(1)}, u32[]{:S(2)}, u32[]{:S(2)}) collective-permute-start(f32[4,8,1024]{2,1,0:T(8,128)S(1)} %march_keep3.1.after), channel_id=1, source_target_pairs={{0,6},{1,7},{2,4},{3,5},{4,2},{5,3},{6,0},{7,1},{8,14},{9,15},{10,... | collective-permute-start | bytes 393224 | tf_op jit(solution)/shard_map/ppermute | solution.py:489
  38.7 5.6 %collective-permute-start.6 = (f32[4,8,1024]{2,1,0:T(8,128)S(1)}, f32[4,8,1024]{2,1,0:T(8,128)S(1)}, u32[]{:S(2)}, u32[]{:S(2)}) collective-permute-start(f32[4,8,1024]{2,1,0:T(8,128)S(1)} %march_keep1.1.refs_0_), channel_id=1, source_target_pairs={{0,2},{1,3},{2,0},{3,1},{4,6},{5,7},{6,4},{7,5},{8,10},{9,11},{10,... | collective-permute-start | bytes 393224 | tf_op jit(solution)/shard_map/ppermute | solution.py:489
  39.2 3.2 %collective-permute-start.4 = (f32[1,4,8,1024]{3,2,1,0:T(8,128)S(1)}, f32[1,4,8,1024]{3,2,1,0:T(8,128)S(1)}, u32[]{:S(2)}, u32[]{:S(2)}) collective-permute-start(f32[1,4,8,1024]{3,2,1,0:T(8,128)S(1)} %march_send0.1.refs_0_), channel_id=1, source_target_pairs={{0,1},{1,0},{2,3},{3,2},{4,5},{5,4},{6,7},{7,6},{8,9},{9,8},{10,11... | collective-permute-start | bytes 393224 | tf_op jit(solution)/shard_map/ppermute | solution.py:479
  42.3 20.5 %copy-start.1 = (f32[3,3,3,3]{3,2,1,0:T(4,128)S(1)}, f32[3,3,3,3]{3,2,1,0:T(4,128)}, u32[]{:S(2)}) copy-start(f32[3,3,3,3]{3,2,1,0:T(4,128)} %weight.1) | copy-start | bytes 976
  42.3 20.5 %copy-start.2 = (f32[3]{0:T(128)S(1)}, f32[3]{0:T(128)}, u32[]{:S(2)}) copy-start(f32[3]{0:T(128)} %param.17) | copy-start | bytes 40
  55.5 4.0 %collective-permute-start.8 = (f32[3,2,1024]{2,1,0:T(2,128)S(1)}, f32[3,2,1024]{2,1,0:T(2,128)S(1)}, u32[]{:S(2)}, u32[]{:S(2)}) collective-permute-start(f32[3,2,1024]{2,1,0:T(2,128)S(1)} %get-tuple-element.19.centre), channel_id=1, source_target_pairs={{0,1},{1,0},{2,3},{3,2},{4,5},{5,4},{6,7},{7,6},{8,9},{9,8},{10,11... | collective-permute-start | bytes 73736 | tf_op jit(solution)/shard_map/ppermute | solution.py:518
  55.6 7.3 %collective-permute-start.9 = (f32[3,2,1024]{2,1,0:T(2,128)S(1)}, f32[3,2,1024]{2,1,0:T(2,128)S(1)}, u32[]{:S(2)}, u32[]{:S(2)}) collective-permute-start(f32[3,2,1024]{2,1,0:T(2,128)S(1)} %get-tuple-element.20), channel_id=1, source_target_pairs={{0,7},{1,2},{2,1},{3,4},{4,3},{5,6},{6,5},{7,32},{8,15},{9,10},{10... | collective-permute-start | bytes 73736 | tf_op jit(solution)/shard_map/ppermute | solution.py:517

commit v7 on v6

--- a/solution.py
+++ b/solution.py
@@ -116,7 +116,7 @@
     lax.fori_loop(0, layers, gradients, 0, unroll=4)
 
 
-def edge_kernel(feats, top, bot, edges):
+def edge_kernel(feats, top, bot, out):
     layers = feats.shape[2]
     half = feats.shape[4]
     sub = iota((8, half), 0)
@@ -129,24 +129,11 @@
             outer = jnp.where(sub < 4, line[:, :half], line[:, half:])
             slope = 0.5 * (inner - outer) if parity == 0 else 0.5 * (outer - inner)
             fixed = jnp.where(sub % 4 == low, slope, both[0:8])
-            edges[parity, z, 0:16] = feats[parity, zpos, z, 0:16]
-            edges[parity, z, 16:32] = jnp.concatenate([fixed, both[8:16]], 0).astype(BF16)
-            edges[parity, z, 32:KDIM] = feats[parity, zpos, z, 32:KDIM]
+            fixed = jnp.concatenate([fixed, both[8:16]], 0).astype(BF16)
+            out[parity, zpos, z, 16:32] = fixed
         return carry
 
     lax.fori_loop(0, layers, fix, 0)
-
-
-def load_plane(feats, edges, parity, zpos, x):
-    at_edge = zpos == 3 * parity
-
-    @pl.when(at_edge)
-    def _():
-        x[...] = edges[parity]
-
-    @pl.when(jnp.logical_not(at_edge))
-    def _():
-        x[...] = feats[parity, zpos]
 
 
 def march(plane, w1, w2, coverage, shift, out):
@@ -200,7 +187,7 @@
     return jnp.concatenate(cols, 1)
 
 
-def send_kernel(where, feats, edges, w1, w2, coverage, shift, after, out, x, *, steps):
+def send_kernel(where, feats, w1, w2, coverage, shift, after, out, *, steps):
     d = where[0]
     parity = 1 - (d & 1)
     first, *others = steps
@@ -209,8 +196,7 @@
         step = first
         for n, other in enumerate(others):
             step = jnp.where(i == n + 1, other, step)
-        load_plane(feats, edges, parity, ((d >> 1) & 3) ^ step, x)
-        march(x, w1, w2, coverage, shift, out.at[i])
+        march(feats.at[parity, ((d >> 1) & 3) ^ step], w1, w2, coverage, shift, out.at[i])
         return carry
 
     lax.fori_loop(0, len(steps), piece, 0)
@@ -267,12 +253,11 @@
 
 
 def keep_kernel(
-    where, flags, feats, edges, w1, w2, coverage, shift, received, *refs, step, slot
+    where, flags, feats, w1, w2, coverage, shift, received, *refs, step, slot
 ):
-    out, x = refs[-2:]
+    out = refs[-1]
     d = where[0]
-    load_plane(feats, edges, d & 1, ((d >> 1) & 3) ^ step, x)
-    march(x, w1, w2, coverage, shift, out)
+    march(feats.at[d & 1, ((d >> 1) & 3) ^ step], w1, w2, coverage, shift, out)
     if step == 0:
         return
     state = tuple(out[o] for o in range(4))
@@ -346,13 +331,14 @@
 ANY = pl.BlockSpec(memory_space=pl.ANY)
 
 
-def call(kernel, name, outs, specs, *args, scratch=(), micros=1.0):
+def call(kernel, name, outs, specs, *args, scratch=(), micros=1.0, aliases={}):
     return pl.pallas_call(
         kernel,
         out_shape=outs,
         in_specs=specs,
         out_specs=jax.tree.map(lambda _: VMEM, outs),
         scratch_shapes=scratch,
+        input_output_aliases=aliases,
         compiler_params=pltpu.CompilerParams(vmem_limit_bytes=24 * 2**20),
         name=name,
         cost_estimate=pl.CostEstimate(
@@ -427,30 +413,28 @@
     )
     net = (w1, w2, coverage, shift)
     cores = [(i, i ^ 1) for i in range(depths)]
-    edges = call(
+    feats = call(
         edge_kernel,
         "edges",
-        shape((2, layers, KDIM, half), BF16),
+        shape(feats.shape, BF16),
         [VMEM] * 3,
         feats,
         top,
         bot,
-    )
-    plane = pltpu.VMEM((layers, KDIM, half), BF16)
-    latest = edges
+        aliases={0: 0},
+    )
+    latest = shift
 
     def send(steps):
         return call(
             functools.partial(send_kernel, steps=steps),
             "march_send" + "".join(map(str, steps)),
             shape((len(steps), 4, 8, half)),
-            [SMEM] + [VMEM] * 6 + [ANY],
+            [SMEM] + [VMEM] * 5 + [ANY],
             where,
             feats,
-            edges,
             *net,
             latest,
-            scratch=[plane],
             micros=3.0 * len(steps),
         )
 
@@ -459,16 +443,14 @@
             functools.partial(keep_kernel, step=step, slot=slot),
             f"march_keep{step}",
             shape((4, 8, half)),
-            [SMEM] + [VMEM] * 7 + [VMEM if step else ANY, ANY] + [ANY] * len(landed),
+            [SMEM] + [VMEM] * 6 + [VMEM if step else ANY, ANY] + [ANY] * len(landed),
             where,
             flags,
             feats,
-            edges,
             *net,
             received,
             latest,
             *landed,
-            scratch=[plane],
             micros=3.0,
         )
 

time: 64.1 us -> 63.6 us (level)
  waiting for transfers between devices: 5.44 us -> 7.56 us
  starting transfers between devices: 15.6 us -> 13.9 us
  Pallas kernels: 28 us -> 27.1 us
    ppermute x1, starting transfers between devices: 3.85 us -> 1.92 us  [shards(): lax.ppermute(extra, ('strip', 'depth'), across_pairs(strips, depths))]
    ppermute x1, waiting for transfers between devices: 3.39 us -> 5.2 us  [shards(): lax.ppermute(extra, ('strip', 'depth'), across_pairs(strips, depths))]
    pallas_call x12, Pallas kernels: 28 us -> 27.1 us  [call(): pl.pallas_call(kernel, out_shape=outs, in_specs=specs, out_specs=jax.tree...]
  transfers between devices with their start and end apart: 10 -> 10, of which waited for: 2 -> 2; matrix products, arithmetic and copies ran while one was open for 2% -> 2% of each run, Pallas kernels for 32% -> 31%
where the time goes in v7:
time: 63.6 us; the launch traced here: 63.3 us
  Pallas kernels  27.1 us (43%)
  starting transfers between devices  13.9 us (22%)
  blocking collectives  10.8 us (17%)
  waiting for transfers between devices  7.56 us (12%)
  local copies, waits for them, and re-layouts  2.37 us (4%)
  other arithmetic  1.42 us (2%)
    pallas_call x12, Pallas kernels, call(): pl.pallas_call(kernel, out_shape=outs, in_specs=specs, out_specs=jax.tree...  27.1 us
    all_to_all x1, blocking collectives, shards(): lax.all_to_all(rows_out, 'depth', 0, 0, tiled=True, axis_index_groups=[[i...  10.8 us
    ppermute x3, starting transfers between devices, shards(): parts[step] = lax.ppermute(latest, 'depth', swap)  5.34 us
    ppermute x1, waiting for transfers between devices, shards(): lax.ppermute(extra, ('strip', 'depth'), across_pairs(strips, depths))  5.2 us
    ppermute x1, starting transfers between devices, shards(): lax.ppermute(volume[:, rows - 1:], 'strip', [(i, i + 1) for i in range(st...  3.48 us
    ppermute x1, starting transfers between devices, shards(): lax.ppermute(volume[:, :1], 'strip', [(i + 1, i) for i in range(strips -...  2.36 us
    ppermute x3, waiting for transfers between devices, shards(): parts[step] = lax.ppermute(latest, 'depth', swap)  2.34 us
    ppermute x1, starting transfers between devices, shards(): lax.ppermute(extra, ('strip', 'depth'), across_pairs(strips, depths))  1.92 us
  transfers between devices with their start and end apart: 10, of which 2 were waited for; matrix products, arithmetic and copies ran while one was open for 2% of the time, Pallas kernels for 31%

profile of v7, /device:TPU:16, one launch (start us, length us, event | category | flops | bytes accessed | tf_op | source)
XLA Modules:
  0.0 63.3 jit_solution(13106065534349618918)
XLA Ops:
  0.0 1.1 %fusion = (bf16[8,1,2048]{2,1,0:T(2,128)(2,1)S(1)}, bf16[8,1,2048]{2,1,0:T(2,128)(2,1)S(1)}) fusion(bf16[8,32,2048]{2,1,0:T(8,128)(2,1)} %vol.1), kind=kLoop, calls=%fused_computation.2 | loop fusion | bytes 131072 | tf_op jit(solution)/shard_map/slice | solution.py:392
  1.1 2.4 %collective-permute-start.1 = (bf16[8,1,2048]{2,1,0:T(2,128)(2,1)S(1)}, bf16[8,1,2048]{2,1,0:T(2,128)(2,1)S(1)}, u32[]{:S(2)}, u32[]{:S(2)}) collective-permute-start(bf16[8,1,2048]{2,1,0:T(2,128)(2,1)S(1)} %get-tuple-element.21), channel_id=1, source_target_pairs={{32,0},{64,32},{96,64},{33,1},{65,33},{97,65},{34,2},{66,34},{98,6... | collective-permute-start | bytes 98312 | tf_op jit(solution)/shard_map/ppermute | solution.py:392
  3.5 3.5 %collective-permute-start = (bf16[8,1,2048]{2,1,0:T(2,128)(2,1)S(1)}, bf16[8,1,2048]{2,1,0:T(2,128)(2,1)S(1)}, u32[]{:S(2)}, u32[]{:S(2)}) collective-permute-start(bf16[8,1,2048]{2,1,0:T(2,128)(2,1)S(1)} %get-tuple-element.22), channel_id=1, source_target_pairs={{0,32},{32,64},{64,96},{1,33},{33,65},{65,97},{2,34},{34,66},{66,9... | collective-permute-start | bytes 98312 | tf_op jit(solution)/shard_map/ppermute | solution.py:391
  7.0 0.7 %pad_add_fusion.1.counts = s32[2,64]{1,0:T(2,128)S(1)} fusion(s32[1,32]{1,0:T(1,128)} %bitcast.14, s32[1,16]{1,0:T(1,128)} %bitcast.15), kind=kLoop, calls=%fused_computation.1 | loop fusion | flops 128 | bytes 704 | tf_op jit(solution)/shard_map/add | solution.py:376
  7.7 0.7 %pad_add_fusion.facts = f32[10,64]{1,0:T(8,128)S(1)} fusion(f32[1,4]{1,0:T(1,128)} %bitcast.12, f32[1,64]{1,0:T(1,128)} %bitcast.13, bf16[4,64]{1,0:T(4,128)(2,1)} %bitcast.11, bf16[4,64]{1,0:T(4,128)(2,1)} %param.12), kind=kLoop, calls=%fused_computation | loop fusion | flops 3200 | bytes 3856 | tf_op jit(solution)/shard_map/add | solution.py:376
  8.4 1.2 %copy-done = bf16[8,32,2048]{2,1,0:T(8,128)(2,1)S(1)} copy-done((bf16[8,32,2048]{2,1,0:T(8,128)(2,1)S(1)}, bf16[8,32,2048]{2,1,0:T(8,128)(2,1)}, u32[]{:S(2)}) %copy-start) | copy-done | bytes 1048600
  9.6 2.7 %features.1 = (bf16[2,4,8,48,1024]{4,3,2,1,0:T(8,128)(2,1)S(1)}, bf16[512,48]{1,0:T(8,128)(2,1)S(1)}, bf16[32,512]{1,0:T(8,128)(2,1)S(1)}, f32[8,1024]{1,0:T(8,1...) custom-call(s32[1]{0:T(128)} %bitcast.where, bf16[8,32,2048]{2,1,0:T(8,128)(2,1)S(1)} %copy-done, ...), custom_call_target="tpu_custom_call" | custom-call | flops 1000000000 | tf_op jit(solution)/shard_map/features/pallas_call | solution.py:335
  12.3 0.0 collective-permute-done.1.bot
  12.3 0.2 edges.1.feats
  12.6 5.7 %march_send21.1.after = f32[2,4,8,1024]{3,2,1,0:T(8,128)S(1)} custom-call(s32[1]{0:T(128)} %bitcast.where, bf16[2,4,8,48,1024]{4,3,2,1,0:T(8,128)(2,1)S(1)} %edges.1.feats, bf16[512,48]{1,0:T(8,128)(2,1)S(1)} %get-tuple-element.15.w1, bf16[32,512]{1,0:T(8,128)(2,1)S(1)} %get-tuple-element.16.w2, f32[8,1024]{1,0:T(8,128)S(1)} %get-tuple-element.17.coverage, ...), custom_call_target="tpu_custom_call" | custom-call | flops 6000000000 | tf_op jit(solution)/shard_map/march_send21/pallas_call | solution.py:335
  18.3 0.1 collective-permute-start.3
  18.4 2.9 %march_send3.1.refs_0_ = f32[1,4,8,1024]{3,2,1,0:T(8,128)S(1)} custom-call(s32[1]{0:T(128)} %bitcast.where, bf16[2,4,8,48,1024]{4,3,2,1,0:T(8,128)(2,1)S(1)} %edges.1.feats, bf16[512,48]{1,0:T(8,128)(2,1)S(1)} %get-tuple-element.15.w1, bf16[32,512]{1,0:T(8,128)(2,1)S(1)} %get-tuple-element.16.w2, f32[8,1024]{1,0:T(8,128)S(1)} %get-tuple-element.17.coverage, ...), custom_call_target="tpu_custom_call" | custom-call | flops 3000000000 | tf_op jit(solution)/shard_map/march_send3/pallas_call | solution.py:335
  21.2 0.6 collective-permute-start.2
  21.8 2.9 %march_keep2.1.refs_0_ = f32[4,8,1024]{2,1,0:T(8,128)S(1)} custom-call(s32[1]{0:T(128)} %bitcast.where, f32[13,8,128]{2,1,0:T(8,128)S(1)} %get-tuple-element.13.flags, bf16[2,4,8,48,1024]{4,3,2,1,0:T(8,128)(2,1)S(1)} %edges.1.feats, bf16[512,48]{1,0:T(8,128)(2,1)S(1)} %get-tuple-element.15.w1, bf16[32,512]{1,0:T(8,128)(2,1)S(1)} %get-tuple-element.16.w2, ...), custom_call_target="tpu_custom_call" | custom-call | flops 3000000000 | tf_op jit(solution)/shard_map/march_keep2/pallas_call | solution.py:335
  24.7 4.1 %collective-permute-start.5 = (f32[4,8,1024]{2,1,0:T(8,128)S(1)}, f32[4,8,1024]{2,1,0:T(8,128)S(1)}, u32[]{:S(2)}, u32[]{:S(2)}) collective-permute-start(f32[4,8,1024]{2,1,0:T(8,128)S(1)} %march_keep2.1.refs_0_), channel_id=1, source_target_pairs={{0,4},{1,5},{2,6},{3,7},{4,0},{5,1},{6,2},{7,3},{8,12},{9,13},{10,... | collective-permute-start | bytes 393224 | tf_op jit(solution)/shard_map/ppermute | solution.py:471
  28.8 2.9 %march_keep1.1.refs_0_ = f32[4,8,1024]{2,1,0:T(8,128)S(1)} custom-call(s32[1]{0:T(128)} %bitcast.where, f32[13,8,128]{2,1,0:T(8,128)S(1)} %get-tuple-element.13.flags, bf16[2,4,8,48,1024]{4,3,2,1,0:T(8,128)(2,1)S(1)} %edges.1.feats, bf16[512,48]{1,0:T(8,128)(2,1)S(1)} %get-tuple-element.15.w1, bf16[32,512]{1,0:T(8,128)(2,1)S(1)} %get-tuple-element.16.w2, ...), custom_call_target="tpu_custom_call" | custom-call | flops 3000000000 | tf_op jit(solution)/shard_map/march_keep1/pallas_call | solution.py:335
  31.7 2.9 %march_keep3.1.after = f32[4,8,1024]{2,1,0:T(8,128)S(1)} custom-call(s32[1]{0:T(128)} %bitcast.where, f32[13,8,128]{2,1,0:T(8,128)S(1)} %get-tuple-element.13.flags, bf16[2,4,8,48,1024]{4,3,2,1,0:T(8,128)(2,1)S(1)} %edges.1.feats, bf16[512,48]{1,0:T(8,128)(2,1)S(1)} %get-tuple-element.15.w1, bf16[32,512]{1,0:T(8,128)(2,1)S(1)} %get-tuple-element.16.w2, ...), custom_call_target="tpu_custom_call" | custom-call | flops 3000000000 | tf_op jit(solution)/shard_map/march_keep3/pallas_call | solution.py:335
  34.6 2.9 %march_send0.1.refs_0_ = f32[1,4,8,1024]{3,2,1,0:T(8,128)S(1)} custom-call(s32[1]{0:T(128)} %bitcast.where, bf16[2,4,8,48,1024]{4,3,2,1,0:T(8,128)(2,1)S(1)} %edges.1.feats, bf16[512,48]{1,0:T(8,128)(2,1)S(1)} %get-tuple-element.15.w1, bf16[32,512]{1,0:T(8,128)(2,1)S(1)} %get-tuple-element.16.w2, f32[8,1024]{1,0:T(8,128)S(1)} %get-tuple-element.17.coverage, ...), custom_call_target="tpu_custom_call" | custom-call | flops 3000000000 | tf_op jit(solution)/shard_map/march_send0/pallas_call | solution.py:335
  37.5 0.8 %collective-permute-start.7 = (f32[4,8,1024]{2,1,0:T(8,128)S(1)}, f32[4,8,1024]{2,1,0:T(8,128)S(1)}, u32[]{:S(2)}, u32[]{:S(2)}) collective-permute-start(f32[4,8,1024]{2,1,0:T(8,128)S(1)} %march_keep3.1.after), channel_id=1, source_target_pairs={{0,6},{1,7},{2,4},{3,5},{4,2},{5,3},{6,0},{7,1},{8,14},{9,15},{10,... | collective-permute-start | bytes 393224 | tf_op jit(solution)/shard_map/ppermute | solution.py:471
  38.2 0.4 collective-permute-start.6
  38.7 0.0 collective-permute-start.4
  38.7 2.8 %march_keep0.1.part0 = f32[4,8,1024]{2,1,0:T(8,128)S(1)} custom-call(s32[1]{0:T(128)} %bitcast.where, f32[13,8,128]{2,1,0:T(8,128)S(1)} %get-tuple-element.13.flags, bf16[2,4,8,48,1024]{4,3,2,1,0:T(8,128)(2,1)S(1)} %edges.1.feats, bf16[512,48]{1,0:T(8,128)(2,1)S(1)} %get-tuple-element.15.w1, bf16[32,512]{1,0:T(8,128)(2,1)S(1)} %get-tuple-element.16.w2, ...), custom_call_target="tpu_custom_call" | custom-call | flops 3000000000 | tf_op jit(solution)/shard_map/march_keep0/pallas_call | solution.py:335
  41.5 0.0 copy-start.1
  41.5 0.0 copy-start.2
  41.6 2.3 %collective-permute-done.7.part3 = f32[4,8,1024]{2,1,0:T(8,128)S(1)} collective-permute-done((f32[4,8,1024]{2,1,0:T(8,128)S(1)}, f32[4,8,1024]{2,1,0:T(8,128)S(1)}, u32[]{:S(2)}, u32[]{:S(2)}) %collective-permute-start.7) | collective-permute-done | bytes 131104 | tf_op jit(solution)/shard_map/ppermute | solution.py:471
  43.9 0.2 merge_z.1
  44.1 10.8 %all_to_all.5.parts = f32[4,4,4,1024]{3,2,1,0:T(4,128)S(1)} all-to-all(f32[4,4,4,1024]{3,2,1,0:T(4,128)S(1)} %merge_z.1), channel_id=1, replica_groups={{0,8,16,24},{1,9,17,25},{2,10,18,26},{3,11,19,27},{4,12,20,28},{5,13,21..., dimensions={0} | all-to-all | bytes 524288 | tf_op jit(solution)/shard_map/all_to_all | solution.py:482
  54.9 0.1 merge_x.1
  55.0 1.9 %collective-permute-start.9 = (f32[3,2,1024]{2,1,0:T(2,128)S(1)}, f32[3,2,1024]{2,1,0:T(2,128)S(1)}, u32[]{:S(2)}, u32[]{:S(2)}) collective-permute-start(f32[3,2,1024]{2,1,0:T(2,128)S(1)} %get-tuple-element.20), channel_id=1, source_target_pairs={{0,7},{1,2},{2,1},{3,4},{4,3},{5,6},{6,5},{7,32},{8,15},{9,10},{10... | collective-permute-start | bytes 73736 | tf_op jit(solution)/shard_map/ppermute | solution.py:499
  56.9 0.1 collective-permute-start.8
  57.0 5.2 %collective-permute-done.9.apart = f32[3,2,1024]{2,1,0:T(2,128)S(1)} collective-permute-done((f32[3,2,1024]{2,1,0:T(2,128)S(1)}, f32[3,2,1024]{2,1,0:T(2,128)S(1)}, u32[]{:S(2)}, u32[]{:S(2)}) %collective-permute-start.9) | collective-permute-done | bytes 24608 | tf_op jit(solution)/shard_map/ppermute | solution.py:499
  62.2 1.0 %filter.1 = f32[3,1,2048]{2,1,0:T(1,128)} custom-call(s32[1]{0:T(128)} %bitcast.where, f32[3,3,3,3]{3,2,1,0:T(4,128)S(1)} %copy-done.1, f32[1,3]{1,0:T(1,128)S(1)} %bitcast.10, f32[3,2,1024]{2,1,0:T(2,128)S(1)} %collective-permute-done.8.beside, f32[3,2,1024]{2,1,0:T(2,128)S(1)} %get-tuple-element.19.centre, f32[3,2,1024]{2,1,0:T(2,128)S(1)} %collective-permute-done.9.apart), custom_call_target="tpu_custom_call" | custom-call | flops 1000000000 | tf_op jit(solution)/shard_map/filter/pallas_call | solution.py:335
  (10 shorter events, 0.0 us)
Async XLA Ops:
  1.1 11.2 %collective-permute-start.1 = (bf16[8,1,2048]{2,1,0:T(2,128)(2,1)S(1)}, bf16[8,1,2048]{2,1,0:T(2,128)(2,1)S(1)}, u32[]{:S(2)}, u32[]{:S(2)}) collective-permute-start(bf16[8,1,2048]{2,1,0:T(2,128)(2,1)S(1)} %get-tuple-element.21), channel_id=1, source_target_pairs={{32,0},{64,32},{96,64},{33,1},{65,33},{97,65},{34,2},{66,34},{98,6... | collective-permute-start | bytes 98312 | tf_op jit(solution)/shard_map/ppermute | solution.py:392
  3.5 8.8 %collective-permute-start = (bf16[8,1,2048]{2,1,0:T(2,128)(2,1)S(1)}, bf16[8,1,2048]{2,1,0:T(2,128)(2,1)S(1)}, u32[]{:S(2)}, u32[]{:S(2)}) collective-permute-start(bf16[8,1,2048]{2,1,0:T(2,128)(2,1)S(1)} %get-tuple-element.22), channel_id=1, source_target_pairs={{0,32},{32,64},{64,96},{1,33},{33,65},{65,97},{2,34},{34,66},{66,9... | collective-permute-start | bytes 98312 | tf_op jit(solution)/shard_map/ppermute | solution.py:391
  8.4 1.2 %copy-start = (bf16[8,32,2048]{2,1,0:T(8,128)(2,1)S(1)}, bf16[8,32,2048]{2,1,0:T(8,128)(2,1)}, u32[]{:S(2)}) copy-start(bf16[8,32,2048]{2,1,0:T(8,128)(2,1)} %vol.1) | copy-start | bytes 3145732
  18.3 3.5 %collective-permute-start.3 = (f32[2,4,8,1024]{3,2,1,0:T(8,128)S(1)}, f32[2,4,8,1024]{3,2,1,0:T(8,128)S(1)}, u32[]{:S(2)}, u32[]{:S(2)}) collective-permute-start(f32[2,4,8,1024]{3,2,1,0:T(8,128)S(1)} %march_send21.1.after), channel_id=1, source_target_pairs={{0,1},{1,0},{2,3},{3,2},{4,5},{5,4},{6,7},{7,6},{8,9},{9,8},{10,11... | collective-permute-start | bytes 786440 | tf_op jit(solution)/shard_map/ppermute | solution.py:461
  21.2 10.5 %collective-permute-start.2 = (f32[1,4,8,1024]{3,2,1,0:T(8,128)S(1)}, f32[1,4,8,1024]{3,2,1,0:T(8,128)S(1)}, u32[]{:S(2)}, u32[]{:S(2)}) collective-permute-start(f32[1,4,8,1024]{3,2,1,0:T(8,128)S(1)} %march_send3.1.refs_0_), channel_id=1, source_target_pairs={{0,1},{1,0},{2,3},{3,2},{4,5},{5,4},{6,7},{7,6},{8,9},{9,8},{10,11... | collective-permute-start | bytes 393224 | tf_op jit(solution)/shard_map/ppermute | solution.py:461
  24.7 14.0 %collective-permute-start.5 = (f32[4,8,1024]{2,1,0:T(8,128)S(1)}, f32[4,8,1024]{2,1,0:T(8,128)S(1)}, u32[]{:S(2)}, u32[]{:S(2)}) collective-permute-start(f32[4,8,1024]{2,1,0:T(8,128)S(1)} %march_keep2.1.refs_0_), channel_id=1, source_target_pairs={{0,4},{1,5},{2,6},{3,7},{4,0},{5,1},{6,2},{7,3},{8,12},{9,13},{10,... | collective-permute-start | bytes 393224 | tf_op jit(solution)/shard_map/ppermute | solution.py:471
  37.5 6.4 %collective-permute-start.7 = (f32[4,8,1024]{2,1,0:T(8,128)S(1)}, f32[4,8,1024]{2,1,0:T(8,128)S(1)}, u32[]{:S(2)}, u32[]{:S(2)}) collective-permute-start(f32[4,8,1024]{2,1,0:T(8,128)S(1)} %march_keep3.1.after), channel_id=1, source_target_pairs={{0,6},{1,7},{2,4},{3,5},{4,2},{5,3},{6,0},{7,1},{8,14},{9,15},{10,... | collective-permute-start | bytes 393224 | tf_op jit(solution)/shard_map/ppermute | solution.py:471
  38.2 5.6 %collective-permute-start.6 = (f32[4,8,1024]{2,1,0:T(8,128)S(1)}, f32[4,8,1024]{2,1,0:T(8,128)S(1)}, u32[]{:S(2)}, u32[]{:S(2)}) collective-permute-start(f32[4,8,1024]{2,1,0:T(8,128)S(1)} %march_keep1.1.refs_0_), channel_id=1, source_target_pairs={{0,2},{1,3},{2,0},{3,1},{4,6},{5,7},{6,4},{7,5},{8,10},{9,11},{10,... | collective-permute-start | bytes 393224 | tf_op jit(solution)/shard_map/ppermute | solution.py:471
  38.7 2.9 %collective-permute-start.4 = (f32[1,4,8,1024]{3,2,1,0:T(8,128)S(1)}, f32[1,4,8,1024]{3,2,1,0:T(8,128)S(1)}, u32[]{:S(2)}, u32[]{:S(2)}) collective-permute-start(f32[1,4,8,1024]{3,2,1,0:T(8,128)S(1)} %march_send0.1.refs_0_), channel_id=1, source_target_pairs={{0,1},{1,0},{2,3},{3,2},{4,5},{5,4},{6,7},{7,6},{8,9},{9,8},{10,11... | collective-permute-start | bytes 393224 | tf_op jit(solution)/shard_map/ppermute | solution.py:461
  41.5 20.7 %copy-start.1 = (f32[3,3,3,3]{3,2,1,0:T(4,128)S(1)}, f32[3,3,3,3]{3,2,1,0:T(4,128)}, u32[]{:S(2)}) copy-start(f32[3,3,3,3]{3,2,1,0:T(4,128)} %weight.1) | copy-start | bytes 976
  41.5 20.7 %copy-start.2 = (f32[3]{0:T(128)S(1)}, f32[3]{0:T(128)}, u32[]{:S(2)}) copy-start(f32[3]{0:T(128)} %param.17) | copy-start | bytes 40
  55.0 7.3 %collective-permute-start.9 = (f32[3,2,1024]{2,1,0:T(2,128)S(1)}, f32[3,2,1024]{2,1,0:T(2,128)S(1)}, u32[]{:S(2)}, u32[]{:S(2)}) collective-permute-start(f32[3,2,1024]{2,1,0:T(2,128)S(1)} %get-tuple-element.20), channel_id=1, source_target_pairs={{0,7},{1,2},{2,1},{3,4},{4,3},{5,6},{6,5},{7,32},{8,15},{9,10},{10... | collective-permute-start | bytes 73736 | tf_op jit(solution)/shard_map/ppermute | solution.py:499
  56.9 5.3 %collective-permute-start.8 = (f32[3,2,1024]{2,1,0:T(2,128)S(1)}, f32[3,2,1024]{2,1,0:T(2,128)S(1)}, u32[]{:S(2)}, u32[]{:S(2)}) collective-permute-start(f32[3,2,1024]{2,1,0:T(2,128)S(1)} %get-tuple-element.19.centre), channel_id=1, source_target_pairs={{0,1},{1,0},{2,3},{3,2},{4,5},{5,4},{6,7},{7,6},{8,9},{9,8},{10,11... | collective-permute-start | bytes 73736 | tf_op jit(solution)/shard_map/ppermute | solution.py:500

commit v8 on v7

--- a/solution.py
+++ b/solution.py
@@ -81,7 +81,7 @@
                 planes[z, j, :, k * 128 : (k + 1) * 128] = jnp.concatenate([left, right], 0)
         return carry
 
-    lax.fori_loop(0, layers, permute, 0, unroll=4)
+    lax.fori_loop(0, layers, permute, 0, unroll=8)
     lane = iota((8, half), 1)
     sub = iota((8, half), 0)
     ones = jnp.ones((KDIM - 32, half), BF16)
@@ -113,7 +113,7 @@
             feats[j % 2, j // 2, z, 32:KDIM] = ones
         return carry
 
-    lax.fori_loop(0, layers, gradients, 0, unroll=4)
+    lax.fori_loop(0, layers, gradients, 0, unroll=8)
 
 
 def edge_kernel(feats, top, bot, out):

time: 63.6 us -> 62.5 us (0.983)
  Pallas kernels: 27.1 us -> 26 us
    pallas_call x12, Pallas kernels: 27.1 us -> 26 us  [call(): pl.pallas_call(kernel, out_shape=outs, in_specs=specs, out_specs=jax.tree...]
  transfers between devices with their start and end apart: 10 -> 10, of which waited for: 2 -> 2; matrix products, arithmetic and copies ran while one was open for 2% -> 2% of each run, Pallas kernels for 31% -> 30%
where the time goes in v8:
time: 62.5 us; the launch traced here: 62.2 us
  Pallas kernels  26 us (42%)
  starting transfers between devices  13.9 us (22%)
  blocking collectives  10.8 us (17%)
  waiting for transfers between devices  7.59 us (12%)
  local copies, waits for them, and re-layouts  2.37 us (4%)
  other arithmetic  1.42 us (2%)
    pallas_call x12, Pallas kernels, call(): pl.pallas_call(kernel, out_shape=outs, in_specs=specs, out_specs=jax.tree...  26 us
    all_to_all x1, blocking collectives, shards(): lax.all_to_all(rows_out, 'depth', 0, 0, tiled=True, axis_index_groups=[[i...  10.8 us
    ppermute x3, starting transfers between devices, shards(): parts[step] = lax.ppermute(latest, 'depth', swap)  5.32 us
    ppermute x1, waiting for transfers between devices, shards(): lax.ppermute(extra, ('strip', 'depth'), across_pairs(strips, depths))  5.19 us
    ppermute x1, starting transfers between devices, shards(): lax.ppermute(volume[:, rows - 1:], 'strip', [(i, i + 1) for i in range(st...  3.48 us
    ppermute x3, waiting for transfers between devices, shards(): parts[step] = lax.ppermute(latest, 'depth', swap)  2.38 us
    ppermute x1, starting transfers between devices, shards(): lax.ppermute(volume[:, :1], 'strip', [(i + 1, i) for i in range(strips -...  2.36 us
    ppermute x1, starting transfers between devices, shards(): lax.ppermute(extra, ('strip', 'depth'), across_pairs(strips, depths))  1.92 us
  transfers between devices with their start and end apart: 10, of which 2 were waited for; matrix products, arithmetic and copies ran while one was open for 2% of the time, Pallas kernels for 30%

profile of v8, /device:TPU:16, one launch (start us, length us, event | category | flops | bytes accessed | tf_op | source)
XLA Modules:
  0.0 62.2 jit_solution(12933189148840594070)
XLA Ops:
  0.0 1.1 %fusion = (bf16[8,1,2048]{2,1,0:T(2,128)(2,1)S(1)}, bf16[8,1,2048]{2,1,0:T(2,128)(2,1)S(1)}) fusion(bf16[8,32,2048]{2,1,0:T(8,128)(2,1)} %vol.1), kind=kLoop, calls=%fused_computation.2 | loop fusion | bytes 131072 | tf_op jit(solution)/shard_map/slice | solution.py:392
  1.1 2.4 %collective-permute-start.1 = (bf16[8,1,2048]{2,1,0:T(2,128)(2,1)S(1)}, bf16[8,1,2048]{2,1,0:T(2,128)(2,1)S(1)}, u32[]{:S(2)}, u32[]{:S(2)}) collective-permute-start(bf16[8,1,2048]{2,1,0:T(2,128)(2,1)S(1)} %get-tuple-element.21), channel_id=1, source_target_pairs={{32,0},{64,32},{96,64},{33,1},{65,33},{97,65},{34,2},{66,34},{98,6... | collective-permute-start | bytes 98312 | tf_op jit(solution)/shard_map/ppermute | solution.py:392
  3.5 3.5 %collective-permute-start = (bf16[8,1,2048]{2,1,0:T(2,128)(2,1)S(1)}, bf16[8,1,2048]{2,1,0:T(2,128)(2,1)S(1)}, u32[]{:S(2)}, u32[]{:S(2)}) collective-permute-start(bf16[8,1,2048]{2,1,0:T(2,128)(2,1)S(1)} %get-tuple-element.22), channel_id=1, source_target_pairs={{0,32},{32,64},{64,96},{1,33},{33,65},{65,97},{2,34},{34,66},{66,9... | collective-permute-start | bytes 98312 | tf_op jit(solution)/shard_map/ppermute | solution.py:391
  7.0 0.7 %pad_add_fusion.1.counts = s32[2,64]{1,0:T(2,128)S(1)} fusion(s32[1,32]{1,0:T(1,128)} %bitcast.14, s32[1,16]{1,0:T(1,128)} %bitcast.15), kind=kLoop, calls=%fused_computation.1 | loop fusion | flops 128 | bytes 704 | tf_op jit(solution)/shard_map/add | solution.py:376
  7.7 0.7 %pad_add_fusion.facts = f32[10,64]{1,0:T(8,128)S(1)} fusion(f32[1,4]{1,0:T(1,128)} %bitcast.12, f32[1,64]{1,0:T(1,128)} %bitcast.13, bf16[4,64]{1,0:T(4,128)(2,1)} %bitcast.11, bf16[4,64]{1,0:T(4,128)(2,1)} %param.12), kind=kLoop, calls=%fused_computation | loop fusion | flops 3200 | bytes 3856 | tf_op jit(solution)/shard_map/add | solution.py:376
  8.4 1.2 %copy-done = bf16[8,32,2048]{2,1,0:T(8,128)(2,1)S(1)} copy-done((bf16[8,32,2048]{2,1,0:T(8,128)(2,1)S(1)}, bf16[8,32,2048]{2,1,0:T(8,128)(2,1)}, u32[]{:S(2)}) %copy-start) | copy-done | bytes 1048600
  9.6 1.6 %features.1 = (bf16[2,4,8,48,1024]{4,3,2,1,0:T(8,128)(2,1)S(1)}, bf16[512,48]{1,0:T(8,128)(2,1)S(1)}, bf16[32,512]{1,0:T(8,128)(2,1)S(1)}, f32[8,1024]{1,0:T(8,1...) custom-call(s32[1]{0:T(128)} %bitcast.where, bf16[8,32,2048]{2,1,0:T(8,128)(2,1)S(1)} %copy-done, ...), custom_call_target="tpu_custom_call" | custom-call | flops 1000000000 | tf_op jit(solution)/shard_map/features/pallas_call | solution.py:335
  11.2 0.0 collective-permute-done.1.bot
  11.2 0.2 edges.1.feats
  11.5 5.7 %march_send21.1.after = f32[2,4,8,1024]{3,2,1,0:T(8,128)S(1)} custom-call(s32[1]{0:T(128)} %bitcast.where, bf16[2,4,8,48,1024]{4,3,2,1,0:T(8,128)(2,1)S(1)} %edges.1.feats, bf16[512,48]{1,0:T(8,128)(2,1)S(1)} %get-tuple-element.15.w1, bf16[32,512]{1,0:T(8,128)(2,1)S(1)} %get-tuple-element.16.w2, f32[8,1024]{1,0:T(8,128)S(1)} %get-tuple-element.17.coverage, ...), custom_call_target="tpu_custom_call" | custom-call | flops 6000000000 | tf_op jit(solution)/shard_map/march_send21/pallas_call | solution.py:335
  17.2 0.1 collective-permute-start.3
  17.3 2.9 %march_send3.1.refs_0_ = f32[1,4,8,1024]{3,2,1,0:T(8,128)S(1)} custom-call(s32[1]{0:T(128)} %bitcast.where, bf16[2,4,8,48,1024]{4,3,2,1,0:T(8,128)(2,1)S(1)} %edges.1.feats, bf16[512,48]{1,0:T(8,128)(2,1)S(1)} %get-tuple-element.15.w1, bf16[32,512]{1,0:T(8,128)(2,1)S(1)} %get-tuple-element.16.w2, f32[8,1024]{1,0:T(8,128)S(1)} %get-tuple-element.17.coverage, ...), custom_call_target="tpu_custom_call" | custom-call | flops 3000000000 | tf_op jit(solution)/shard_map/march_send3/pallas_call | solution.py:335
  20.1 0.6 collective-permute-start.2
  20.7 2.9 %march_keep2.1.refs_0_ = f32[4,8,1024]{2,1,0:T(8,128)S(1)} custom-call(s32[1]{0:T(128)} %bitcast.where, f32[13,8,128]{2,1,0:T(8,128)S(1)} %get-tuple-element.13.flags, bf16[2,4,8,48,1024]{4,3,2,1,0:T(8,128)(2,1)S(1)} %edges.1.feats, bf16[512,48]{1,0:T(8,128)(2,1)S(1)} %get-tuple-element.15.w1, bf16[32,512]{1,0:T(8,128)(2,1)S(1)} %get-tuple-element.16.w2, ...), custom_call_target="tpu_custom_call" | custom-call | flops 3000000000 | tf_op jit(solution)/shard_map/march_keep2/pallas_call | solution.py:335
  23.6 4.1 %collective-permute-start.5 = (f32[4,8,1024]{2,1,0:T(8,128)S(1)}, f32[4,8,1024]{2,1,0:T(8,128)S(1)}, u32[]{:S(2)}, u32[]{:S(2)}) collective-permute-start(f32[4,8,1024]{2,1,0:T(8,128)S(1)} %march_keep2.1.refs_0_), channel_id=1, source_target_pairs={{0,4},{1,5},{2,6},{3,7},{4,0},{5,1},{6,2},{7,3},{8,12},{9,13},{10,... | collective-permute-start | bytes 393224 | tf_op jit(solution)/shard_map/ppermute | solution.py:471
  27.7 2.9 %march_keep1.1.refs_0_ = f32[4,8,1024]{2,1,0:T(8,128)S(1)} custom-call(s32[1]{0:T(128)} %bitcast.where, f32[13,8,128]{2,1,0:T(8,128)S(1)} %get-tuple-element.13.flags, bf16[2,4,8,48,1024]{4,3,2,1,0:T(8,128)(2,1)S(1)} %edges.1.feats, bf16[512,48]{1,0:T(8,128)(2,1)S(1)} %get-tuple-element.15.w1, bf16[32,512]{1,0:T(8,128)(2,1)S(1)} %get-tuple-element.16.w2, ...), custom_call_target="tpu_custom_call" | custom-call | flops 3000000000 | tf_op jit(solution)/shard_map/march_keep1/pallas_call | solution.py:335
  30.6 2.9 %march_keep3.1.after = f32[4,8,1024]{2,1,0:T(8,128)S(1)} custom-call(s32[1]{0:T(128)} %bitcast.where, f32[13,8,128]{2,1,0:T(8,128)S(1)} %get-tuple-element.13.flags, bf16[2,4,8,48,1024]{4,3,2,1,0:T(8,128)(2,1)S(1)} %edges.1.feats, bf16[512,48]{1,0:T(8,128)(2,1)S(1)} %get-tuple-element.15.w1, bf16[32,512]{1,0:T(8,128)(2,1)S(1)} %get-tuple-element.16.w2, ...), custom_call_target="tpu_custom_call" | custom-call | flops 3000000000 | tf_op jit(solution)/shard_map/march_keep3/pallas_call | solution.py:335
  33.5 2.9 %march_send0.1.refs_0_ = f32[1,4,8,1024]{3,2,1,0:T(8,128)S(1)} custom-call(s32[1]{0:T(128)} %bitcast.where, bf16[2,4,8,48,1024]{4,3,2,1,0:T(8,128)(2,1)S(1)} %edges.1.feats, bf16[512,48]{1,0:T(8,128)(2,1)S(1)} %get-tuple-element.15.w1, bf16[32,512]{1,0:T(8,128)(2,1)S(1)} %get-tuple-element.16.w2, f32[8,1024]{1,0:T(8,128)S(1)} %get-tuple-element.17.coverage, ...), custom_call_target="tpu_custom_call" | custom-call | flops 3000000000 | tf_op jit(solution)/shard_map/march_send0/pallas_call | solution.py:335
  36.4 0.8 %collective-permute-start.7 = (f32[4,8,1024]{2,1,0:T(8,128)S(1)}, f32[4,8,1024]{2,1,0:T(8,128)S(1)}, u32[]{:S(2)}, u32[]{:S(2)}) collective-permute-start(f32[4,8,1024]{2,1,0:T(8,128)S(1)} %march_keep3.1.after), channel_id=1, source_target_pairs={{0,6},{1,7},{2,4},{3,5},{4,2},{5,3},{6,0},{7,1},{8,14},{9,15},{10,... | collective-permute-start | bytes 393224 | tf_op jit(solution)/shard_map/ppermute | solution.py:471
  37.2 0.4 collective-permute-start.6
  37.6 0.0 collective-permute-start.4
  37.6 2.8 %march_keep0.1.part0 = f32[4,8,1024]{2,1,0:T(8,128)S(1)} custom-call(s32[1]{0:T(128)} %bitcast.where, f32[13,8,128]{2,1,0:T(8,128)S(1)} %get-tuple-element.13.flags, bf16[2,4,8,48,1024]{4,3,2,1,0:T(8,128)(2,1)S(1)} %edges.1.feats, bf16[512,48]{1,0:T(8,128)(2,1)S(1)} %get-tuple-element.15.w1, bf16[32,512]{1,0:T(8,128)(2,1)S(1)} %get-tuple-element.16.w2, ...), custom_call_target="tpu_custom_call" | custom-call | flops 3000000000 | tf_op jit(solution)/shard_map/march_keep0/pallas_call | solution.py:335
  40.4 0.0 copy-start.1
  40.4 0.0 copy-start.2
  40.4 2.4 %collective-permute-done.7.part3 = f32[4,8,1024]{2,1,0:T(8,128)S(1)} collective-permute-done((f32[4,8,1024]{2,1,0:T(8,128)S(1)}, f32[4,8,1024]{2,1,0:T(8,128)S(1)}, u32[]{:S(2)}, u32[]{:S(2)}) %collective-permute-start.7) | collective-permute-done | bytes 131104 | tf_op jit(solution)/shard_map/ppermute | solution.py:471
  42.8 0.2 merge_z.1
  43.0 10.8 %all_to_all.5.parts = f32[4,4,4,1024]{3,2,1,0:T(4,128)S(1)} all-to-all(f32[4,4,4,1024]{3,2,1,0:T(4,128)S(1)} %merge_z.1), channel_id=1, replica_groups={{0,8,16,24},{1,9,17,25},{2,10,18,26},{3,11,19,27},{4,12,20,28},{5,13,21..., dimensions={0} | all-to-all | bytes 524288 | tf_op jit(solution)/shard_map/all_to_all | solution.py:482
  53.8 0.1 merge_x.1
  53.9 1.9 %collective-permute-start.9 = (f32[3,2,1024]{2,1,0:T(2,128)S(1)}, f32[3,2,1024]{2,1,0:T(2,128)S(1)}, u32[]{:S(2)}, u32[]{:S(2)}) collective-permute-start(f32[3,2,1024]{2,1,0:T(2,128)S(1)} %get-tuple-element.20), channel_id=1, source_target_pairs={{0,7},{1,2},{2,1},{3,4},{4,3},{5,6},{6,5},{7,32},{8,15},{9,10},{10... | collective-permute-start | bytes 73736 | tf_op jit(solution)/shard_map/ppermute | solution.py:499
  55.8 0.1 collective-permute-start.8
  55.9 5.2 %collective-permute-done.9.apart = f32[3,2,1024]{2,1,0:T(2,128)S(1)} collective-permute-done((f32[3,2,1024]{2,1,0:T(2,128)S(1)}, f32[3,2,1024]{2,1,0:T(2,128)S(1)}, u32[]{:S(2)}, u32[]{:S(2)}) %collective-permute-start.9) | collective-permute-done | bytes 24608 | tf_op jit(solution)/shard_map/ppermute | solution.py:499
  61.1 1.0 %filter.1 = f32[3,1,2048]{2,1,0:T(1,128)} custom-call(s32[1]{0:T(128)} %bitcast.where, f32[3,3,3,3]{3,2,1,0:T(4,128)S(1)} %copy-done.1, f32[1,3]{1,0:T(1,128)S(1)} %bitcast.10, f32[3,2,1024]{2,1,0:T(2,128)S(1)} %collective-permute-done.8.beside, f32[3,2,1024]{2,1,0:T(2,128)S(1)} %get-tuple-element.19.centre, f32[3,2,1024]{2,1,0:T(2,128)S(1)} %collective-permute-done.9.apart), custom_call_target="tpu_custom_call" | custom-call | flops 1000000000 | tf_op jit(solution)/shard_map/filter/pallas_call | solution.py:335
  (10 shorter events, 0.0 us)
Async XLA Ops:
  1.1 10.1 %collective-permute-start.1 = (bf16[8,1,2048]{2,1,0:T(2,128)(2,1)S(1)}, bf16[8,1,2048]{2,1,0:T(2,128)(2,1)S(1)}, u32[]{:S(2)}, u32[]{:S(2)}) collective-permute-start(bf16[8,1,2048]{2,1,0:T(2,128)(2,1)S(1)} %get-tuple-element.21), channel_id=1, source_target_pairs={{32,0},{64,32},{96,64},{33,1},{65,33},{97,65},{34,2},{66,34},{98,6... | collective-permute-start | bytes 98312 | tf_op jit(solution)/shard_map/ppermute | solution.py:392
  3.5 7.7 %collective-permute-start = (bf16[8,1,2048]{2,1,0:T(2,128)(2,1)S(1)}, bf16[8,1,2048]{2,1,0:T(2,128)(2,1)S(1)}, u32[]{:S(2)}, u32[]{:S(2)}) collective-permute-start(bf16[8,1,2048]{2,1,0:T(2,128)(2,1)S(1)} %get-tuple-element.22), channel_id=1, source_target_pairs={{0,32},{32,64},{64,96},{1,33},{33,65},{65,97},{2,34},{34,66},{66,9... | collective-permute-start | bytes 98312 | tf_op jit(solution)/shard_map/ppermute | solution.py:391
  8.4 1.2 %copy-start = (bf16[8,32,2048]{2,1,0:T(8,128)(2,1)S(1)}, bf16[8,32,2048]{2,1,0:T(8,128)(2,1)}, u32[]{:S(2)}) copy-start(bf16[8,32,2048]{2,1,0:T(8,128)(2,1)} %vol.1) | copy-start | bytes 3145732
  17.2 3.5 %collective-permute-start.3 = (f32[2,4,8,1024]{3,2,1,0:T(8,128)S(1)}, f32[2,4,8,1024]{3,2,1,0:T(8,128)S(1)}, u32[]{:S(2)}, u32[]{:S(2)}) collective-permute-start(f32[2,4,8,1024]{3,2,1,0:T(8,128)S(1)} %march_send21.1.after), channel_id=1, source_target_pairs={{0,1},{1,0},{2,3},{3,2},{4,5},{5,4},{6,7},{7,6},{8,9},{9,8},{10,11... | collective-permute-start | bytes 786440 | tf_op jit(solution)/shard_map/ppermute | solution.py:461
  20.1 10.5 %collective-permute-start.2 = (f32[1,4,8,1024]{3,2,1,0:T(8,128)S(1)}, f32[1,4,8,1024]{3,2,1,0:T(8,128)S(1)}, u32[]{:S(2)}, u32[]{:S(2)}) collective-permute-start(f32[1,4,8,1024]{3,2,1,0:T(8,128)S(1)} %march_send3.1.refs_0_), channel_id=1, source_target_pairs={{0,1},{1,0},{2,3},{3,2},{4,5},{5,4},{6,7},{7,6},{8,9},{9,8},{10,11... | collective-permute-start | bytes 393224 | tf_op jit(solution)/shard_map/ppermute | solution.py:461
  23.6 14.0 %collective-permute-start.5 = (f32[4,8,1024]{2,1,0:T(8,128)S(1)}, f32[4,8,1024]{2,1,0:T(8,128)S(1)}, u32[]{:S(2)}, u32[]{:S(2)}) collective-permute-start(f32[4,8,1024]{2,1,0:T(8,128)S(1)} %march_keep2.1.refs_0_), channel_id=1, source_target_pairs={{0,4},{1,5},{2,6},{3,7},{4,0},{5,1},{6,2},{7,3},{8,12},{9,13},{10,... | collective-permute-start | bytes 393224 | tf_op jit(solution)/shard_map/ppermute | solution.py:471
  36.4 6.5 %collective-permute-start.7 = (f32[4,8,1024]{2,1,0:T(8,128)S(1)}, f32[4,8,1024]{2,1,0:T(8,128)S(1)}, u32[]{:S(2)}, u32[]{:S(2)}) collective-permute-start(f32[4,8,1024]{2,1,0:T(8,128)S(1)} %march_keep3.1.after), channel_id=1, source_target_pairs={{0,6},{1,7},{2,4},{3,5},{4,2},{5,3},{6,0},{7,1},{8,14},{9,15},{10,... | collective-permute-start | bytes 393224 | tf_op jit(solution)/shard_map/ppermute | solution.py:471
  37.2 5.7 %collective-permute-start.6 = (f32[4,8,1024]{2,1,0:T(8,128)S(1)}, f32[4,8,1024]{2,1,0:T(8,128)S(1)}, u32[]{:S(2)}, u32[]{:S(2)}) collective-permute-start(f32[4,8,1024]{2,1,0:T(8,128)S(1)} %march_keep1.1.refs_0_), channel_id=1, source_target_pairs={{0,2},{1,3},{2,0},{3,1},{4,6},{5,7},{6,4},{7,5},{8,10},{9,11},{10,... | collective-permute-start | bytes 393224 | tf_op jit(solution)/shard_map/ppermute | solution.py:471
  37.6 2.9 %collective-permute-start.4 = (f32[1,4,8,1024]{3,2,1,0:T(8,128)S(1)}, f32[1,4,8,1024]{3,2,1,0:T(8,128)S(1)}, u32[]{:S(2)}, u32[]{:S(2)}) collective-permute-start(f32[1,4,8,1024]{3,2,1,0:T(8,128)S(1)} %march_send0.1.refs_0_), channel_id=1, source_target_pairs={{0,1},{1,0},{2,3},{3,2},{4,5},{5,4},{6,7},{7,6},{8,9},{9,8},{10,11... | collective-permute-start | bytes 393224 | tf_op jit(solution)/shard_map/ppermute | solution.py:461
  40.4 20.7 %copy-start.1 = (f32[3,3,3,3]{3,2,1,0:T(4,128)S(1)}, f32[3,3,3,3]{3,2,1,0:T(4,128)}, u32[]{:S(2)}) copy-start(f32[3,3,3,3]{3,2,1,0:T(4,128)} %weight.1) | copy-start | bytes 976
  40.4 20.7 %copy-start.2 = (f32[3]{0:T(128)S(1)}, f32[3]{0:T(128)}, u32[]{:S(2)}) copy-start(f32[3]{0:T(128)} %param.17) | copy-start | bytes 40
  53.9 7.3 %collective-permute-start.9 = (f32[3,2,1024]{2,1,0:T(2,128)S(1)}, f32[3,2,1024]{2,1,0:T(2,128)S(1)}, u32[]{:S(2)}, u32[]{:S(2)}) collective-permute-start(f32[3,2,1024]{2,1,0:T(2,128)S(1)} %get-tuple-element.20), channel_id=1, source_target_pairs={{0,7},{1,2},{2,1},{3,4},{4,3},{5,6},{6,5},{7,32},{8,15},{9,10},{10... | collective-permute-start | bytes 73736 | tf_op jit(solution)/shard_map/ppermute | solution.py:499
  55.8 5.3 %collective-permute-start.8 = (f32[3,2,1024]{2,1,0:T(2,128)S(1)}, f32[3,2,1024]{2,1,0:T(2,128)S(1)}, u32[]{:S(2)}, u32[]{:S(2)}) collective-permute-start(f32[3,2,1024]{2,1,0:T(2,128)S(1)} %get-tuple-element.19.centre), channel_id=1, source_target_pairs={{0,1},{1,0},{2,3},{3,2},{4,5},{5,4},{6,7},{7,6},{8,9},{9,8},{10,11... | collective-permute-start | bytes 73736 | tf_op jit(solution)/shard_map/ppermute | solution.py:500
